TPU v7x, 32 devices: a whole 2x2x4 slice. The times are simulated.
32 devices in a mesh: rep: 4 (over y, x), shard: 8 (over z, core).
Axes of the slice: x: 2, y: 2, z: 4, core: 2. Of those that a mesh axis runs over, the one named last changes fastest.
Arguments:
- inputs: bfloat16 [4096, 1024], P(('rep', 'shard')), may hold values from -6 to 6
- cotangent: bfloat16 [4096, 1024], P(('rep', 'shard')), may hold values from -6 to 6
- mix_gain: bfloat16 [1024], P('shard'), may hold values from 0.5 to 1.5
- query_proj: bfloat16 [1024, 512], P('shard'), may hold values from -0.1875 to 0.1875
- key_proj: bfloat16 [1024, 512], P('shard'), may hold values from -0.1875 to 0.1875
- value_proj: bfloat16 [1024, 1024], P('shard'), may hold values from -0.1875 to 0.1875
- beta_proj: bfloat16 [1024, 4], P('shard'), may hold values from -0.1875 to 0.1875
- decay_proj: bfloat16 [1024, 4], P('shard'), may hold values from -0.1875 to 0.1875
- gate_proj: bfloat16 [1024, 1024], P('shard'), may hold values from -0.1875 to 0.1875
- query_conv: bfloat16 [4, 512], P(None, 'shard'), may hold values from -3 to 3
- key_conv: bfloat16 [4, 512], P(None, 'shard'), may hold values from -3 to 3
- value_conv: bfloat16 [4, 1024], P(None, 'shard'), may hold values from -3 to 3
- decay_log: float32 [4], replicated, may hold values from -1.5 to 0.5
- decay_bias: float32 [4], replicated, may hold values from -4 to -2
- head_gain: bfloat16 [256], P('shard'), may hold values from 0.5 to 1.5
- out_proj: bfloat16 [1024, 1024], P('shard'), may hold values from -0.1875 to 0.1875
- ffn_gain: bfloat16 [1024], P('shard'), may hold values from 0.5 to 1.5
- ffn_gate: bfloat16 [1024, 2816], P('shard'), may hold values from -0.1875 to 0.1875
- ffn_up: bfloat16 [1024, 2816], P('shard'), may hold values from -0.1875 to 0.1875
- ffn_down: bfloat16 [2816, 1024], P('shard'), may hold values from -0.109375 to 0.109375
Outputs:
- outputs: bfloat16 [4096, 1024], P(('rep', 'shard'))
- inputs_grad: float32 [4096, 1024], P(('rep', 'shard'))
- mix_gain_grad: float32 [1024], P('shard')
- query_proj_grad: float32 [1024, 512], P('shard')
- key_proj_grad: float32 [1024, 512], P('shard')
- value_proj_grad: float32 [1024, 1024], P('shard')
- beta_proj_grad: float32 [1024, 4], P('shard')
- decay_proj_grad: float32 [1024, 4], P('shard')
- gate_proj_grad: float32 [1024, 1024], P('shard')
- query_conv_grad: float32 [4, 512], P(None, 'shard')
- key_conv_grad: float32 [4, 512], P(None, 'shard')
- value_conv_grad: float32 [4, 1024], P(None, 'shard')
- decay_log_grad: float32 [4], replicated
- decay_bias_grad: float32 [4], replicated
- head_gain_grad: float32 [256], P('shard')
- out_proj_grad: float32 [1024, 1024], P('shard')
- ffn_gain_grad: float32 [1024], P('shard')
- ffn_gate_grad: float32 [1024, 2816], P('shard')
- ffn_up_grad: float32 [1024, 2816], P('shard')
- ffn_down_grad: float32 [2816, 1024], P('shard')
All inputs are finite; a program needn't handle non-finite values.
Results may differ from a plain program's by a relative error of at most 0.018.
Values may be sent and summed in bfloat16 or wider, within the bound.
No kernel may reach another device: no remote copies, remote signals or barrier semaphores. Data moves between devices by JAX's collectives and lax.ppermute only.
A program may use at most 192 MiB of HBM per device.

v0:
```python
import functools
import math

import jax
import jax.numpy as jnp
from jax import lax
from jax.experimental import pallas as pl
from jax.experimental.pallas import tpu as pltpu
from jax.sharding import PartitionSpec as P

EPS = 1e-06
HIGH = lax.Precision.HIGHEST
LOW = jnp.bfloat16
WIDE = jnp.float32
LANES = 128
ROWS16 = 16


def local_dot(left, right):
    return jnp.dot(left, right, preferred_element_type=WIDE)


def left_dot(left, right):
    return lax.dot_general(left, right, (((0,), (0,)), ((), ())), preferred_element_type=WIDE)


def right_dot(left, right):
    return lax.dot_general(left, right, (((1,), (1,)), ((), ())), preferred_element_type=WIDE)


def dot_nn(left, right):
    return jnp.dot(left, right, preferred_element_type=WIDE, precision=HIGH)


def dot_nt(left, right):
    return lax.dot_general(
        left, right, (((1,), (1,)), ((), ())), preferred_element_type=WIDE, precision=HIGH
    )


def dot_tn(left, right):
    return lax.dot_general(
        left, right, (((0,), (0,)), ((), ())), preferred_element_type=WIDE, precision=HIGH
    )


def sigmoid(v):
    return 1.0 / (1.0 + jnp.exp(-v))


def iotas(size):
    return (
        lax.broadcasted_iota(jnp.int32, (size, size), 0),
        lax.broadcasted_iota(jnp.int32, (size, size), 1),
    )


def later(v, steps):
    rows = lax.broadcasted_iota(jnp.int32, v.shape, 0)
    return jnp.where(rows >= steps, pltpu.roll(v, steps, 0), 0.0)


def earlier(v, steps):
    rows = lax.broadcasted_iota(jnp.int32, v.shape, 0)
    return jnp.where(rows < v.shape[0] - steps, pltpu.roll(v, v.shape[0] - steps, 0), 0.0)


def conv_silu(raw, taps):
    count = taps.shape[0]
    run = raw * taps[count - 1 : count]
    for steps in range(1, count):
        run = run + later(raw, steps) * taps[count - 1 - steps : count - steps]
    sig = sigmoid(run)
    return run, sig


def unit_features(act, keys):
    query_act, key_act, value = act[:, :keys], act[:, keys : 2 * keys], act[:, 2 * keys :]
    query_r = lax.rsqrt(jnp.sum(query_act * query_act, -1, keepdims=True) + EPS)
    key_r = lax.rsqrt(jnp.sum(key_act * key_act, -1, keepdims=True) + EPS)
    query = query_act * query_r * (1.0 / math.sqrt(keys))
    return query, key_act * key_r, value, query_act, query_r, key_act, key_r


def softplus(v):
    return jnp.maximum(v, 0.0) + jnp.log1p(jnp.exp(-jnp.abs(v)))


def decay_matrix(gates, decay, bias):
    size = gates.shape[0]
    rows, cols = iotas(size)
    beta = sigmoid(gates[:, 0:1])
    decay_in = gates[:, 1:2] + bias
    log_decay = -decay * softplus(decay_in)
    decay_row = jnp.sum(jnp.where(rows == cols, log_decay, 0.0), 0, keepdims=True)
    total_col = jnp.sum(jnp.where(cols <= rows, decay_row, 0.0), 1, keepdims=True)
    total_row = jnp.sum(jnp.where(rows <= cols, log_decay, 0.0), 0, keepdims=True)
    spread = jnp.where(rows >= cols, total_col - total_row, 0.0)
    upto = jnp.where(rows >= cols, jnp.exp(spread), 0.0)
    return beta, decay_in, log_decay, upto


def unit_lower_inverse(systems):
    size = systems[0].shape[0]
    rows, cols = iotas(size)
    block = 8
    near = [jnp.where(rows // block == cols // block, a, 0.0) for a in systems]
    eye = jnp.where(rows == cols, 1.0, 0.0)
    power = [dot_nn(a, a) for a in near]
    inverse = [eye - a for a in near]
    inverse = [x + dot_nn(x, p) for x, p in zip(inverse, power)]
    power = [dot_nn(p, p) for p in power]
    inverse = [x + dot_nn(x, p) for x, p in zip(inverse, power)]
    while block < size:
        cross = (rows // (2 * block) == cols // (2 * block)) & (rows // block != cols // block)
        middle = [dot_nn(jnp.where(cross, a, 0.0), x) for a, x in zip(systems, inverse)]
        inverse = [x - dot_nn(x, m) for x, m in zip(inverse, middle)]
        block *= 2
    return inverse


def pack_kernel(
    team,
    places,
    query,
    key,
    value,
    gate,
    proj,
    beta,
    decay,
    mix_gain,
    ffn_gain,
    query_conv,
    key_conv,
    value_conv,
    head_gain,
    pack_out,
    proj_out,
):
    part, shard = places[0], places[1]
    chunk = query.shape[0]
    keys, values = query.shape[1] // team, value.shape[1] // team
    outs = proj.shape[1] // team
    width = pack_out.shape[1]
    count = query_conv.shape[0]
    head_each = head_gain.shape[1]

    def columns(matrix, size):
        return matrix[:, pl.ds(pl.multiple_of(part * size, size), size)]

    pack_out[:chunk, :keys] = columns(query, keys)
    pack_out[:chunk, keys : 2 * keys] = columns(key, keys)
    pack_out[:chunk, 2 * keys : 2 * keys + values] = columns(value, values)
    pack_out[:chunk, 2 * keys + values :] = columns(gate, values)
    proj_out[...] = columns(proj, outs)
    rows, cols = iotas(chunk)

    def column_row(matrix):
        lane = lax.broadcasted_iota(jnp.int32, matrix.shape, 1)
        column = jnp.sum(jnp.where(lane == part, matrix[...].astype(WIDE), 0.0), 1, keepdims=True)
        return jnp.sum(jnp.where(rows == cols, column, 0.0), 0, keepdims=True)

    gains = [mix_gain[...].astype(WIDE), ffn_gain[...].astype(WIDE)]
    gains += [column_row(beta), column_row(decay)]
    gains.append(jnp.zeros((1, width - 4 * chunk), WIDE))
    pieces = []
    for taps, size in ((query_conv, keys), (key_conv, keys), (value_conv, values)):
        wide = taps[...].astype(WIDE)
        pieces.append(jnp.concatenate([wide] * (size // wide.shape[1]), 1))
    pieces = jnp.concatenate(pieces, 1)
    lane = lax.broadcasted_iota(jnp.int32, pieces.shape, 1)
    inside = jnp.where(lane < 2 * keys, lane % keys // query_conv.shape[1], 0)
    inside = jnp.where(lane < 2 * keys, inside, (lane - 2 * keys) // value_conv.shape[1])
    owners = keys // query_conv.shape[1]
    pieces = jnp.where(inside + part * owners == shard, pieces, 0.0)
    taps_rows = jnp.concatenate(
        [pieces, jnp.zeros((count, width - pieces.shape[1]), WIDE)], 1
    )
    head = jnp.concatenate([head_gain[...].astype(WIDE)] * (values // head_each), 1)
    lane = lax.broadcasted_iota(jnp.int32, head.shape, 1)
    head = jnp.where(lane // head_each == shard, head, 0.0)
    head = jnp.concatenate([head, jnp.zeros((1, width - values), WIDE)], 1)
    small = jnp.concatenate(
        [
            jnp.concatenate(gains, 1),
            taps_rows,
            head,
            jnp.zeros((ROWS16 - count - 2, width), WIDE),
        ],
        0,
    )
    pack_out[chunk:] = small.astype(LOW)


def slot_shard(places, slot, chips, same_core):
    chip, core = lax.div(places[1], 2), lax.rem(places[1], 2)
    return 2 * lax.rem(chip + chips - slot, chips) + (core if same_core else 1 - core)


def mixer_forward_kernel(
    seqs,
    keys,
    count,
    scalars,
    places,
    tokens,
    mine,
    theirs,
    first_out,
    raw_out,
    gate_out,
    gates_out,
    inverse_out,
    update_out,
    heads_out,
    mixed_out,
    weights,
    mix_row,
    ffn_row,
    gate_rows,
    taps,
    head_gain,
    gate_wide,
):
    size = tokens.shape[0] // seqs
    chips, block = mine.shape[0], mine.shape[1]
    chunk = block - ROWS16
    values = heads_out.shape[1]
    conv_width = 2 * keys + values
    gate_wide[...] = jnp.zeros(gate_wide.shape, WIDE)
    total = None
    for same_core, slots in ((True, mine), (False, theirs)):
        for slot in range(chips):
            shard = slot_shard(places, slot, chips, same_core)
            line = pl.ds(pl.multiple_of(shard * chunk, chunk), chunk)
            weights[line, :] = slots[slot, :chunk]
            small = slots[slot, chunk:].astype(WIDE)
            mix_row[:, line] = small[0:1, :chunk]
            ffn_row[:, line] = small[0:1, chunk : 2 * chunk]
            pair = small[0:1, 2 * chunk : 3 * chunk], small[0:1, 3 * chunk : 4 * chunk]
            for row in range(4):
                gate_wide[row : row + 1, line] = pair[row % 2]
            total = small if total is None else total + small
    gate_rows[...] = gate_wide[...].astype(LOW)
    taps[...] = total[1 : count + 1, :conv_width]
    head_gain[...] = total[count + 1 : count + 2, :values]
    wide = tokens[...].astype(WIDE)
    first = (
        wide * lax.rsqrt(jnp.mean(wide * wide, -1, keepdims=True) + EPS) * mix_row[...]
    ).astype(LOW)
    first_out[...] = first
    raw_out[...] = local_dot(first, weights[:, :conv_width])
    gate_out[...] = local_dot(first, weights[:, conv_width:])
    gates_out[...] = right_dot(first, gate_rows[...])
    rows, cols = iotas(size)
    parts = []
    for seq in range(seqs):
        span = slice(seq * size, (seq + 1) * size)
        run, sig = conv_silu(raw_out[span], taps[...])
        query, key, value = unit_features(run * sig, keys)[:3]
        beta, _, _, upto = decay_matrix(gates_out[span], scalars[0], scalars[1])
        system = jnp.where(rows > cols, beta * dot_nt(key, key) * upto, 0.0)
        scores = dot_nt(query, key) * upto
        parts.append((system, scores, beta * value))
    inverses = unit_lower_inverse([p[0] for p in parts])
    for seq in range(seqs):
        span = slice(seq * size, (seq + 1) * size)
        inverse_out[span] = inverses[seq]
        update = dot_nn(inverses[seq], parts[seq][2])
        heads = dot_nn(parts[seq][1], update)
        update_out[span] = update
        heads_out[span] = heads
        gate = gate_out[span]
        normed = heads * lax.rsqrt(jnp.mean(heads * heads, -1, keepdims=True) + EPS)
        mixed_out[span] = (normed * head_gain[...] * (gate * sigmoid(gate))).astype(LOW)


def member(part, steps):
    return jnp.bitwise_xor(part, steps)


def feed_forward_kernel(
    team,
    scalars,
    tokens,
    cotangents,
    *refs,
):
    mixed_slots, out_slots = refs[:team], refs[team : 2 * team]
    (
        gain,
        up_weights,
        down_weights,
        mixed_out,
        hidden_out,
        second_out,
        active_out,
        back_out,
        second_grad_out,
        gain_grad_out,
        result_out,
        out_full,
        hidden,
    ) = refs[2 * team :]
    part = scalars[0]
    size = tokens.shape[0] // team
    values = mixed_slots[0].shape[1]
    outs = out_slots[0].shape[2]
    for steps in range(team):
        place = pl.multiple_of(member(part, steps) * values, values)
        for slot in range(team):
            there = slot ^ steps
            mixed_out[slot * size : (slot + 1) * size, pl.ds(place, values)] = mixed_slots[
                steps
            ][there * size : (there + 1) * size]
    blocks = out_slots[0].shape[0]
    chunk = out_slots[0].shape[1]
    for steps in range(team):
        place = pl.multiple_of(member(part, steps) * outs, outs)
        for slot in range(blocks):
            chips = blocks // 2
            shard = slot_shard(scalars, slot % chips, chips, slot < chips)
            line = pl.ds(pl.multiple_of(shard * chunk, chunk), chunk)
            out_full[line, pl.ds(place, outs)] = out_slots[steps][slot]
    wide = tokens[...].astype(WIDE) + local_dot(mixed_out[...], out_full[...])
    hidden_out[...] = wide[:size]
    normed = wide * lax.rsqrt(jnp.mean(wide * wide, -1, keepdims=True) + EPS)
    second = (normed * gain[...]).astype(LOW)
    second_out[...] = second
    hidden[...] = normed
    part_width = active_out.shape[1]
    both = local_dot(second, up_weights[...])
    gate, up = both[:, :part_width], both[:, part_width:]
    gate_sig = sigmoid(gate)
    gate_act = gate * gate_sig
    active = (gate_act * up).astype(LOW)
    active_out[...] = active
    result_out[...] = local_dot(active, down_weights[...]).astype(LOW)
    active_grad = right_dot(cotangents[...], down_weights[...])
    gate_back = (active_grad * up * gate_sig * (1.0 + gate * (1.0 - gate_sig))).astype(LOW)
    up_back = (active_grad * gate_act).astype(LOW)
    back = jnp.concatenate([gate_back, up_back], 1)
    back_out[...] = back
    second_grad = right_dot(back, up_weights[...])
    second_grad_out[...] = second_grad.astype(LOW)
    gain_grad_out[...] = jnp.sum(second_grad * hidden[...], 0, keepdims=True)


def feed_forward_pack_kernel(team, shards, places, gate, up, down, pack):
    chunk = gate.shape[0]
    each = down.shape[0] // team
    padded = -(-each // ROWS16) * ROWS16
    ups = 2 * shards * each // LANES
    pad = jnp.zeros((padded - each, LANES), WIDE)

    for choice in range(team):

        @pl.when(places[0] == choice)
        def _():
            starts = [(s * team + choice) * each for s in range(shards)]
            wide = jnp.concatenate(
                [matrix[:, i : i + each].astype(WIDE) for matrix in (gate, up) for i in starts],
                1,
            )
            for index in range(ups):
                pack[index * chunk : (index + 1) * chunk] = wide[
                    :, index * LANES : (index + 1) * LANES
                ].astype(LOW)
            rows = down[...].astype(WIDE)[choice * each : (choice + 1) * each]
            for index in range(rows.shape[1] // LANES):
                start = ups * chunk + index * padded
                block = rows[:, index * LANES : (index + 1) * LANES]
                pack[start : start + padded] = jnp.concatenate([block, pad], 0).astype(LOW)


def feed_forward_unpack_kernel(shards, packs, up_out, down_out):
    chunk = up_out.shape[0] // shards
    each = down_out.shape[0] // shards
    padded = -(-each // ROWS16) * ROWS16
    ups = up_out.shape[1] // LANES
    for shard in range(shards):
        for index in range(ups):
            up_out[shard * chunk : (shard + 1) * chunk, index * LANES : (index + 1) * LANES] = (
                packs[shard, index * chunk : (index + 1) * chunk]
            )
    for pair in range(shards // 2):
        for index in range(down_out.shape[1] // LANES):
            start = ups * chunk + index * padded
            block = jnp.concatenate(
                [
                    packs[shard, start : start + padded].astype(WIDE)[:each]
                    for shard in (2 * pair, 2 * pair + 1)
                ],
                0,
            )
            down_out[
                2 * pair * each : 2 * (pair + 1) * each, index * LANES : (index + 1) * LANES
            ] = block.astype(LOW)


def feed_forward_weights_kernel(shards, second, back, active, cotangents, pack):
    up_grad = left_dot(second[...], back[...])
    down_grad = left_dot(active[...], cotangents[...])
    chunk = up_grad.shape[0] // shards
    each = down_grad.shape[0] // shards
    padded = -(-each // ROWS16) * ROWS16
    pad = jnp.zeros((padded - each, LANES), WIDE)
    ups = up_grad.shape[1] // LANES
    for shard in range(shards):
        for index in range(ups):
            pack[shard, index * chunk : (index + 1) * chunk] = up_grad[
                shard * chunk : (shard + 1) * chunk, index * LANES : (index + 1) * LANES
            ].astype(LOW)
        for index in range(down_grad.shape[1] // LANES):
            start = ups * chunk + index * padded
            block = down_grad[
                shard * each : (shard + 1) * each, index * LANES : (index + 1) * LANES
            ]
            pack[shard, start : start + padded] = jnp.concatenate([block, pad], 0).astype(LOW)


def feed_forward_finish_kernel(team, shards, places, *refs):
    slots = refs[:team]
    gate_out, up_out, down_out, ordered = refs[team:]
    chunk = gate_out.shape[0]
    each = down_out.shape[0] // team
    padded = -(-each // ROWS16) * ROWS16
    half = shards * each
    ups = 2 * half // LANES
    for steps in range(team):
        ordered[member(places[0], steps)] = slots[steps][...].astype(LOW)
    wide = [
        jnp.concatenate(
            [ordered[h, i * chunk : (i + 1) * chunk].astype(WIDE) for i in range(ups)], 1
        )
        for h in range(team)
    ]
    for base, out in ((0, gate_out), (half, up_out)):
        out[...] = jnp.concatenate(
            [
                wide[h][:, base + s * each : base + (s + 1) * each]
                for s in range(shards)
                for h in range(team)
            ],
            1,
        )
    for h in range(team):
        for index in range(down_out.shape[1] // LANES):
            start = ups * chunk + index * padded
            down_out[h * each : (h + 1) * each, index * LANES : (index + 1) * LANES] = ordered[
                h, start : start + padded
            ].astype(WIDE)[:each]


def mixer_backward_kernel(
    seqs,
    keys,
    shards,
    scalars,
    places,
    *refs,
):
    branch_slots = refs[:seqs]
    (
        out_full,
        gate_raw,
        heads,
        head_gain,
        first,
        mixed,
        raw,
        gates,
        inverse,
        update,
        taps,
        weights,
        gate_rows,
        tokens,
        ffn_gain_grad,
        mine,
        theirs,
        first_grad_out,
        raw_grad_out,
        gates_grad_out,
        branch_grad,
        heads_grad,
    ) = refs[seqs:]
    values = heads.shape[1]
    outs = out_full.shape[1] // seqs
    for slot in range(seqs):
        rows_each = branch_slots[slot].shape[0]
        branch_grad[slot * rows_each : (slot + 1) * rows_each] = branch_slots[slot][...]
    row = pl.multiple_of(places[0] * values, values)
    mixed_grad = right_dot(branch_grad[...], out_full[pl.ds(row, values)])
    out = heads[...]
    gate = gate_raw[...]
    gain = head_gain[...]
    scale = lax.rsqrt(jnp.mean(out * out, -1, keepdims=True) + EPS)
    normed = out * scale
    gate_sig = sigmoid(gate)
    gate_act = gate * gate_sig
    gate_grad = (
        mixed_grad * normed * gain * gate_sig * (1.0 + gate * (1.0 - gate_sig))
    ).astype(LOW)
    head_gain_grad = jnp.sum(mixed_grad * normed * gate_act, 0, keepdims=True)
    normed_grad = mixed_grad * gain * gate_act
    heads_grad[...] = scale * (
        normed_grad - normed * jnp.mean(normed_grad * normed, -1, keepdims=True)
    )
    place = pl.multiple_of(places[0] * outs, outs)
    gate_wgrad = left_dot(first[...], gate_grad)
    out_wgrad = left_dot(mixed[...], branch_grad[:, pl.ds(place, outs)])
    size = raw.shape[0] // seqs
    conv_width = taps.shape[1]
    count = taps.shape[0]
    part, shard = places[0], places[1]
    rows, cols = iotas(size)
    taps_grad = [jnp.zeros((1, conv_width), WIDE) for _ in range(count)]
    log_total = jnp.zeros((1, 1), WIDE)
    bias_total = jnp.zeros((1, 1), WIDE)
    for seq in range(seqs):
        span = slice(seq * size, (seq + 1) * size)
        out_grad = heads_grad[span]
        raw_in = raw[span]
        run, sig = conv_silu(raw_in, taps[...])
        query, key, value, query_act, query_r, key_act, key_r = unit_features(run * sig, keys)
        beta, decay_in, log_decay, upto = decay_matrix(gates[span], scalars[0], scalars[1])
        key_key = dot_nt(key, key) * upto
        scores = dot_nt(query, key) * upto
        solved = update[span]
        scores_grad = jnp.where(rows >= cols, dot_nt(out_grad, solved), 0.0)
        solved_grad = dot_tn(scores, out_grad)
        target_grad = dot_tn(inverse[span], solved_grad)
        system_grad = jnp.where(rows > cols, -dot_nt(target_grad, solved), 0.0)
        value_grad = beta * target_grad
        system_part = system_grad * key_key
        beta_grad = jnp.sum(target_grad * value, 1, keepdims=True) + jnp.sum(
            system_part, 1, keepdims=True
        )
        key_key_grad = system_grad * (beta * upto)
        scores_part = scores_grad * upto
        spread_grad = system_part * beta + scores_grad * scores
        query_grad = dot_nn(scores_part, key)
        key_grad = (
            dot_tn(scores_part, query) + dot_nn(key_key_grad, key) + dot_tn(key_key_grad, key)
        )
        total_row = jnp.sum(
            jnp.where(rows == cols, jnp.sum(spread_grad, 1, keepdims=True), 0.0),
            0,
            keepdims=True,
        ) - jnp.sum(spread_grad, 0, keepdims=True)
        decay_grad = jnp.sum(jnp.where(cols >= rows, total_row, 0.0), 1, keepdims=True)
        decay_raw_grad = -scalars[0] * decay_grad * sigmoid(decay_in)
        beta_raw_grad = beta_grad * beta * (1.0 - beta)
        log_total = log_total + jnp.sum(decay_grad * log_decay, 0, keepdims=True)
        bias_total = bias_total + jnp.sum(decay_raw_grad, 0, keepdims=True)
        beta_high = beta_raw_grad.astype(LOW).astype(WIDE)
        decay_high = decay_raw_grad.astype(LOW).astype(WIDE)
        lane = lax.broadcasted_iota(jnp.int32, (size, ROWS16), 1)
        gates_grad_out[span] = jnp.where(
            lane == 0,
            beta_high,
            jnp.where(
                lane == 1,
                decay_high,
                jnp.where(
                    lane == 2,
                    beta_raw_grad - beta_high,
                    jnp.where(lane == 3, decay_raw_grad - decay_high, 0.0),
                ),
            ),
        ).astype(LOW)
        query_grad = query_grad * (1.0 / math.sqrt(keys))
        query_unit = query_act * query_r
        query_act_grad = query_r * (
            query_grad - query_unit * jnp.sum(query_unit * query_grad, -1, keepdims=True)
        )
        key_act_grad = key_r * (key_grad - key * jnp.sum(key * key_grad, -1, keepdims=True))
        act_grad = jnp.concatenate([query_act_grad, key_act_grad, value_grad], 1)
        run_grad = act_grad * sig * (1.0 + run * (1.0 - sig))
        raw_grad = run_grad * taps[count - 1 : count]
        taps_grad[count - 1] = taps_grad[count - 1] + jnp.sum(
            run_grad * raw_in, 0, keepdims=True
        )
        for steps in range(1, count):
            tap = count - 1 - steps
            moved = earlier(run_grad, steps)
            raw_grad = raw_grad + moved * taps[tap : tap + 1]
            taps_grad[tap] = taps_grad[tap] + jnp.sum(moved * raw_in, 0, keepdims=True)
        raw_grad_out[span] = raw_grad.astype(LOW)
    width = tokens.shape[1]
    chunk = width // shards
    core = lax.rem(shard, 2)
    raw_low = raw_grad_out[...]
    head_wgrad = left_dot(first[...], raw_low)
    gates_rows = left_dot(gates_grad_out[...], first[...])
    first_grad = (
        right_dot(raw_low, weights[:, :conv_width])
        + right_dot(gate_grad, weights[:, conv_width:])
        + local_dot(gates_grad_out[...], gate_rows[...])
    )
    first_grad_out[...] = first_grad.astype(LOW)
    wide = tokens[...].astype(WIDE)
    normed = wide * lax.rsqrt(jnp.mean(wide * wide, -1, keepdims=True) + EPS)
    gain_grad = jnp.sum(first_grad * normed, 0, keepdims=True)
    beta_row = gates_rows[0:1] + gates_rows[2:3]
    decay_row = gates_rows[1:2] + gates_rows[3:4]
    head_shards = shards // seqs
    key_each = keys // head_shards
    value_each = (conv_width - 2 * keys) // head_shards
    head_each = head_gain_grad.shape[1] // shards
    all_taps = jnp.concatenate(taps_grad, 0)
    lane = lax.broadcasted_iota(jnp.int32, (1, conv_width), 1)
    decay_terms = jnp.zeros((1, conv_width), WIDE)
    for which, total in enumerate((log_total, bias_total)):
        for piece in range(3):
            high = total.astype(LOW).astype(WIDE)
            place = head_each + (which * 3 + piece) * shards + shard
            decay_terms = jnp.where(lane == place, high, decay_terms)
            total = total - high
    blocks = []
    for s in range(shards):
        line = slice(s * chunk, (s + 1) * chunk)
        i = s % head_shards
        gains = jnp.concatenate(
            [beta_row[:, line], decay_row[:, line], gain_grad[:, line], ffn_gain_grad[:, line]], 1
        )
        tap_rows = jnp.concatenate(
            [
                all_taps[:, i * key_each : (i + 1) * key_each],
                all_taps[:, keys + i * key_each : keys + (i + 1) * key_each],
                all_taps[:, 2 * keys + i * value_each : 2 * keys + (i + 1) * value_each],
            ],
            1,
        )
        tap_rows = jnp.where(part == s // head_shards, tap_rows, 0.0)
        tap_rows = jnp.concatenate(
            [tap_rows, jnp.zeros((count, conv_width - tap_rows.shape[1]), WIDE)], 1
        )
        head_row = jnp.concatenate(
            [
                head_gain_grad[:, s * head_each : (s + 1) * head_each],
                jnp.zeros((1, conv_width - head_each), WIDE),
            ],
            1,
        )
        small = jnp.concatenate(
            [
                gains,
                tap_rows,
                head_row + decay_terms,
                jnp.zeros((ROWS16 - count - 2, conv_width), WIDE),
            ],
            0,
        )
        empty = jnp.zeros((ROWS16, values + outs), WIDE)
        blocks.append(
            (
                head_wgrad[line],
                gate_wgrad[line],
                out_wgrad[line],
                jnp.concatenate([small, empty], 1),
            )
        )
    top, all_lanes = slice(0, chunk), slice(0, conv_width + values + outs)
    spots = (
        (top, slice(0, conv_width)),
        (top, slice(conv_width, conv_width + values)),
        (top, slice(conv_width + values, conv_width + values + outs)),
        (slice(chunk, chunk + ROWS16), all_lanes),
    )
    for pair in range(shards // 2):
        for even, odd, (line, lanes) in zip(blocks[2 * pair], blocks[2 * pair + 1], spots):
            mine[pair, line, lanes] = jnp.where(core == 0, even, odd).astype(LOW)
            theirs[pair, line, lanes] = jnp.where(core == 0, odd, even).astype(LOW)


def finish_kernel(
    team,
    keys,
    shards,
    count,
    scalars,
    *refs,
):
    slots = refs[:team]
    (
        query_out,
        key_out,
        value_out,
        gate_out,
        proj_out,
        beta_out,
        decay_out,
        mix_out,
        ffn_out,
        query_conv_out,
        key_conv_out,
        value_conv_out,
        head_out,
        log_out,
        bias_out,
        pair,
    ) = refs[team:]
    part = scalars[0]
    chunk = query_out.shape[0]
    values = value_out.shape[1] // team
    conv_width = 2 * keys + values
    key_each = query_conv_out.shape[1]
    conv_each = 2 * key_each + value_conv_out.shape[1]
    head_each = head_out.shape[1]
    total = None
    lane = lax.broadcasted_iota(jnp.int32, (1, LANES), 1)
    log_row = jnp.zeros((1, LANES), WIDE)
    bias_row = jnp.zeros((1, LANES), WIDE)
    pair[...] = jnp.zeros(pair.shape, WIDE)
    for steps in range(team):
        head = member(part, steps)
        key_place = pl.ds(pl.multiple_of(head * keys, keys), keys)
        value_place = pl.ds(pl.multiple_of(head * values, values), values)
        block = slots[steps]
        query_out[:, key_place] = block[:chunk, :keys].astype(WIDE)
        key_out[:, key_place] = block[:chunk, keys : 2 * keys].astype(WIDE)
        value_out[:, value_place] = block[:chunk, 2 * keys : conv_width].astype(WIDE)
        gate_out[:, value_place] = block[:chunk, conv_width : conv_width + values].astype(WIDE)
        proj_out[:, value_place] = block[:chunk, conv_width + values :].astype(WIDE)
        small = block[chunk:, :conv_width].astype(WIDE)
        total = small if total is None else total + small
        pair[pl.ds(head, 1), :] = small[0:1, :chunk]
        pair[pl.ds(head + team, 1), :] = small[0:1, chunk : 2 * chunk]
        terms = small[count + 1 : count + 2]
        wide_lane = lax.broadcasted_iota(jnp.int32, (1, conv_width), 1)
        ends = [head_each + 3 * shards * k for k in range(3)]
        log_sum = jnp.sum(
            jnp.where((wide_lane >= ends[0]) & (wide_lane < ends[1]), terms, 0.0),
            1,
            keepdims=True,
        )
        bias_sum = jnp.sum(
            jnp.where((wide_lane >= ends[1]) & (wide_lane < ends[2]), terms, 0.0),
            1,
            keepdims=True,
        )
        log_row = jnp.where(lane == head, log_sum, log_row)
        bias_row = jnp.where(lane == head, bias_sum, bias_row)
    flipped = pair[...].T
    beta_out[...] = flipped[:, :team]
    decay_out[...] = flipped[:, team : 2 * team]
    mix_out[...] = total[0:1, 2 * chunk : 3 * chunk]
    ffn_out[...] = total[0:1, 3 * chunk : 4 * chunk]
    query_conv_out[...] = total[1 : count + 1, :key_each]
    key_conv_out[...] = total[1 : count + 1, key_each : 2 * key_each]
    value_conv_out[...] = total[1 : count + 1, 2 * key_each : conv_each]
    head_out[...] = total[count + 1 : count + 2, :head_each]
    log_out[...] = log_row[:, :team]
    bias_out[...] = bias_row[:, :team]


def array(shape, dtype):
    return jax.ShapeDtypeStruct(shape, dtype)


def run_kernel(kernel, name, scalars, operands, outs, flops, scratch=()):
    spec = pl.BlockSpec(memory_space=pltpu.VMEM)
    moved = sum(math.prod(v.shape) * v.dtype.itemsize for v in (*operands, *outs))
    return pl.pallas_call(
        kernel,
        out_shape=tuple(outs),
        in_specs=[pl.BlockSpec(memory_space=pltpu.SMEM)] * len(scalars) + [spec] * len(operands),
        out_specs=[spec] * len(outs),
        scratch_shapes=list(scratch),
        compiler_params=pltpu.CompilerParams(vmem_limit_bytes=48 * 1024 * 1024),
        cost_estimate=pl.CostEstimate(flops=flops, bytes_accessed=moved, transcendentals=0),
        name=name,
    )(*scalars, *operands)


def team_pairs(devices, steps):
    return [(j, j ^ steps) for j in range(devices)]


def team_gather(block, devices, team):
    return [block] + [
        lax.ppermute(block, "rep", team_pairs(devices, steps)) for steps in range(1, team)
    ]


def team_double(block, devices, team, axis, order):
    size = block.shape[axis]
    held = {0: block}
    for bit in order:
        both = jnp.concatenate([held[e] for e in held], axis) if len(held) > 1 else block
        moved = lax.ppermute(both, "rep", team_pairs(devices, bit))
        fresh = {
            e ^ bit: lax.slice_in_dim(moved, i * size, (i + 1) * size, axis=axis)
            for i, e in enumerate(held)
        }
        held = held | fresh
    return [held[e] for e in range(team)]


def team_send(slots, devices, team):
    return [slots[0]] + [
        lax.ppermute(slots[steps], "rep", team_pairs(devices, steps)) for steps in range(1, team)
    ]


def wide_sum(blocks):
    total = blocks[0].astype(WIDE)
    for block in blocks[1:]:
        total = total + block.astype(WIDE)
    return total


def line_ring(shards, steps):
    return [(j, (j + 2 * steps) % shards) for j in range(shards)]


def pair_ring(shards):
    return [(j, j ^ 1) for j in range(shards)]


def line_gather(block, shards):
    return [block] + [
        lax.ppermute(block, "shard", line_ring(shards, steps))
        for steps in range(1, shards // 2)
    ]


def core_swap(block, shards):
    return lax.ppermute(block, "shard", pair_ring(shards))


def pair_sum(mine, theirs, shards):
    moved = lax.ppermute(theirs, "shard", pair_ring(shards))
    return (mine.astype(WIDE) + moved.astype(WIDE)).astype(LOW)


def line_send(summed, shard, shards):
    chips = shards // 2
    chip = shard // 2
    terms = [lax.dynamic_index_in_dim(summed, chip, 0, keepdims=False)]
    for steps in range(1, chips):
        block = lax.dynamic_index_in_dim(summed, (chip + steps) % chips, 0, keepdims=False)
        terms.append(lax.ppermute(block, "shard", line_ring(shards, steps)))
    return terms


def norm_scale(v):
    return lax.rsqrt(jnp.mean(v * v, -1, keepdims=True) + EPS)


def replica_slots(block, part, devices, team):
    if devices == team:
        return team_gather(block, devices, team)
    blocks = lax.all_gather(block, "rep").astype(WIDE)
    blocks = jnp.sum(blocks.reshape((devices // team, team) + block.shape), 0)
    return [
        lax.dynamic_index_in_dim(blocks, part ^ e, 0, keepdims=False)
        for e in range(team)
    ]


def after(values, first):
    return lax.optimization_barrier((values, first))[0]


def body(
    inputs,
    cotangent,
    mix_gain,
    query_proj,
    key_proj,
    value_proj,
    beta_proj,
    decay_proj,
    gate_proj,
    query_conv,
    key_conv,
    value_conv,
    decay_log,
    decay_bias,
    head_gain,
    out_proj,
    ffn_gain,
    ffn_gate,
    ffn_up,
    ffn_down,
):
    devices = lax.axis_size("rep")
    shards = lax.axis_size("shard")
    team = beta_proj.shape[1]
    part = lax.axis_index("rep") % team
    shard = lax.axis_index("shard")
    places = jnp.stack([part, shard]).astype(jnp.int32)
    tokens_each, width = inputs.shape
    count = team * tokens_each
    chunk = mix_gain.shape[0]
    keys = query_proj.shape[1] // team
    values = value_proj.shape[1] // team
    outs = out_proj.shape[1] // team
    conv_width = 2 * keys + values
    hidden_each = ffn_down.shape[0] // team
    hidden_part = hidden_each * shards
    taps_count = query_conv.shape[0]
    key_each, value_each = query_conv.shape[1], value_conv.shape[1]
    head_each = head_gain.shape[0]

    padded = -(-hidden_each // ROWS16) * ROWS16
    ffn_rows = 2 * hidden_part * chunk // LANES + padded * (width // LANES)

    mixer_pack, proj_part = run_kernel(
        functools.partial(pack_kernel, team),
        "pack",
        (places,),
        (
            query_proj,
            key_proj,
            value_proj,
            gate_proj,
            out_proj,
            beta_proj,
            decay_proj,
            mix_gain[None],
            ffn_gain[None],
            query_conv,
            key_conv,
            value_conv,
            head_gain[None],
        ),
        (
            array((chunk + ROWS16, conv_width + values), LOW),
            array((chunk, outs), LOW),
        ),
        10**8,
    )
    proj_slots = line_gather(proj_part, shards)
    mixer_slots = line_gather(mixer_pack, shards)
    ffn_pack = run_kernel(
        functools.partial(feed_forward_pack_kernel, team, shards),
        "feed_forward_pack",
        (places,),
        (ffn_gate, ffn_up, ffn_down),
        (array((ffn_rows, LANES), LOW),),
        10**8,
    )[0]
    ffn_packs = lax.all_gather(ffn_pack, "shard", axis=0)
    proj_mine = jnp.stack(proj_slots)
    proj_all = jnp.concatenate([proj_mine, core_swap(proj_mine, shards)], 0)
    token_slots = team_double(after(inputs, proj_mine), devices, team, 0, (1, 2))
    proj_slots = team_double(proj_all, devices, team, 0, (2, 1))
    pack_mine = jnp.stack(mixer_slots)
    pack_theirs = core_swap(pack_mine, shards)
    cotangent_slots = team_double(after(cotangent, pack_mine), devices, team, 0, (1, 2))
    tokens = jnp.concatenate(token_slots, 0)
    cotangents = jnp.concatenate(cotangent_slots, 0)
    scalars = jnp.stack(
        [
            jnp.exp(lax.dynamic_index_in_dim(decay_log, part, 0, keepdims=False)),
            lax.dynamic_index_in_dim(decay_bias, part, 0, keepdims=False),
        ]
    )

    (
        first,
        raw,
        gate_raw,
        gates,
        inverse,
        update,
        heads,
        mixed_part,
        head_weights,
        mix_row,
        ffn_row,
        gate_rows,
        taps,
        head_row,
    ) = run_kernel(
        functools.partial(mixer_forward_kernel, team, keys, taps_count),
        "mixer_forward",
        (scalars, places),
        (tokens, pack_mine, pack_theirs),
        (
            array((count, width), LOW),
            array((count, conv_width), WIDE),
            array((count, values), WIDE),
            array((count, ROWS16), WIDE),
            array((count, tokens_each), WIDE),
            array((count, values), WIDE),
            array((count, values), WIDE),
            array((count, values), LOW),
            array((width, conv_width + values), LOW),
            array((1, width), WIDE),
            array((1, width), WIDE),
            array((ROWS16, width), LOW),
            array((taps_count, conv_width), WIDE),
            array((1, values), WIDE),
        ),
        8 * 10**9,
        (pltpu.VMEM((ROWS16, width), WIDE),),
    )
    mixed_slots = team_gather(mixed_part, devices, team)
    up_weights, down_weights = run_kernel(
        functools.partial(feed_forward_unpack_kernel, shards),
        "feed_forward_unpack",
        (),
        (ffn_packs,),
        (
            array((width, 2 * hidden_part), LOW),
            array((hidden_part, width), LOW),
        ),
        10**8,
    )

    (
        mixed,
        hidden_own,
        second,
        active,
        both_back,
        second_part,
        ffn_gain_part,
        result_part,
        out_full,
    ) = run_kernel(
        functools.partial(feed_forward_kernel, team),
        "feed_forward",
        (places,),
        (tokens, cotangents, *mixed_slots, *proj_slots, ffn_row, up_weights, down_weights),
        (
            array((count, width), LOW),
            array((tokens_each, width), WIDE),
            array((count, width), LOW),
            array((count, hidden_part), LOW),
            array((count, 2 * hidden_part), LOW),
            array((count, width), LOW),
            array((1, width), WIDE),
            array((count, width), LOW),
            array((width, width), LOW),
        ),
        10 * 10**9,
        (pltpu.VMEM((count, width), WIDE),),
    )

    def slots_of(v):
        return [v[e * tokens_each : (e + 1) * tokens_each] for e in range(team)]

    second_slots = team_send(slots_of(second_part), devices, team)
    ffn_grads = run_kernel(
        functools.partial(feed_forward_weights_kernel, shards),
        "feed_forward_weights",
        (),
        (second, both_back, active, cotangents),
        (array((shards, ffn_rows, LANES), LOW),),
        6 * 10**9,
    )[0]
    second_slots = after(second_slots, ffn_grads)
    ffn_shard = lax.psum_scatter(ffn_grads, "shard", scatter_dimension=0)
    second_grad = wide_sum(second_slots)
    scale_own = norm_scale(hidden_own)
    weighted = second_grad * ffn_row
    hidden_grad = cotangent.astype(WIDE) + scale_own * (
        weighted
        - hidden_own
        * (scale_own * scale_own * jnp.mean(hidden_own * weighted, -1, keepdims=True))
    )
    branch_slots = team_gather(hidden_grad.astype(LOW), devices, team)
    result_part = after(result_part, branch_slots)
    result_slots = team_send(slots_of(result_part), devices, team)

    head_mine, head_theirs, first_part = run_kernel(
        functools.partial(mixer_backward_kernel, team, keys, shards),
        "mixer_backward",
        (scalars, places),
        (
            *branch_slots,
            out_full,
            gate_raw,
            heads,
            head_row,
            first,
            mixed,
            raw,
            gates,
            inverse,
            update,
            taps,
            head_weights,
            gate_rows,
            tokens,
            ffn_gain_part,
        ),
        (
            array((shards // 2, chunk + ROWS16, conv_width + values + outs), LOW),
            array((shards // 2, chunk + ROWS16, conv_width + values + outs), LOW),
            array((count, width), LOW),
        ),
        10 * 10**9,
        (
            pltpu.VMEM((count, conv_width), LOW),
            pltpu.VMEM((count, ROWS16), LOW),
            pltpu.VMEM((count, width), LOW),
            pltpu.VMEM((count, values), WIDE),
        ),
    )
    head_summed = pair_sum(head_mine, head_theirs, shards)
    head_terms = line_send(head_summed, shard, shards)
    first_grad = wide_sum(team_send(slots_of(first_part), devices, team))
    seq_in = inputs.astype(WIDE)
    seq_scale = norm_scale(seq_in)
    weighted = first_grad * mix_row
    inputs_grad = hidden_grad + seq_scale * (
        weighted
        - seq_in * (seq_scale * seq_scale * jnp.mean(seq_in * weighted, -1, keepdims=True))
    )
    result = hidden_own + wide_sum(result_slots)

    head_totals = replica_slots(wide_sum(head_terms).astype(LOW), part, devices, team)
    ffn_totals = replica_slots(ffn_shard, part, devices, team)
    gate_grads, up_grads, down_grads = run_kernel(
        functools.partial(feed_forward_finish_kernel, team, shards),
        "feed_forward_finish",
        (places,),
        ffn_totals,
        (
            array(ffn_gate.shape, WIDE),
            array(ffn_up.shape, WIDE),
            array(ffn_down.shape, WIDE),
        ),
        10**8,
        (pltpu.VMEM((team, ffn_rows, LANES), LOW),),
    )
    (
        query_total,
        key_total,
        value_total,
        gate_total,
        out_total,
        beta_total,
        decay_total,
        mix_total,
        ffn_total,
        query_conv_total,
        key_conv_total,
        value_conv_total,
        head_total,
        log_total,
        bias_total,
    ) = run_kernel(
        functools.partial(finish_kernel, team, keys, shards, taps_count),
        "finish",
        (places,),
        head_totals,
        (
            array((chunk, team * keys), WIDE),
            array((chunk, team * keys), WIDE),
            array((chunk, team * values), WIDE),
            array((chunk, team * values), WIDE),
            array((chunk, team * outs), WIDE),
            array((chunk, team), WIDE),
            array((chunk, team), WIDE),
            array((1, chunk), WIDE),
            array((1, chunk), WIDE),
            array((taps_count, key_each), WIDE),
            array((taps_count, key_each), WIDE),
            array((taps_count, value_each), WIDE),
            array((1, head_each), WIDE),
            array((1, team), WIDE),
            array((1, team), WIDE),
        ),
        10**8,
        (pltpu.VMEM((max(8, 2 * team), chunk), WIDE),),
    )
    return (
        result.astype(LOW),
        inputs_grad,
        mix_total[0],
        query_total,
        key_total,
        value_total,
        beta_total,
        decay_total,
        gate_total,
        query_conv_total,
        key_conv_total,
        value_conv_total,
        log_total[0],
        bias_total[0],
        head_total[0],
        out_total,
        ffn_total[0],
        gate_grads,
        up_grads,
        down_grads,
    )


def solution(mesh):
    rows = P("shard", None)
    return jax.shard_map(
        body,
        mesh=mesh,
        in_specs=(
            P(("rep", "shard"), None),
            P(("rep", "shard"), None),
            P("shard"),
            rows,
            rows,
            rows,
            rows,
            rows,
            rows,
            P(None, "shard"),
            P(None, "shard"),
            P(None, "shard"),
            P(),
            P(),
            P("shard"),
            rows,
            P("shard"),
            rows,
            rows,
            rows,
        ),
        out_specs=(
            P(("rep", "shard"), None),
            P(("rep", "shard"), None),
            P("shard"),
            rows,
            rows,
            rows,
            rows,
            rows,
            rows,
            P(None, "shard"),
            P(None, "shard"),
            P(None, "shard"),
            P(),
            P(),
            P("shard"),
            rows,
            P("shard"),
            rows,
            rows,
            rows,
        ),
        check_vma=False,
    )
```

profile of v0, /device:TPU:0, one launch (start us, length us, event | category | flops | bytes accessed | tf_op | source)
XLA Modules:
  0.0 287.1 jit_solution(5648000243745677536)
XLA Ops:
  13.6 3.1 %collective-permute-start = (bf16[128,256]{1,0:T(8,128)(2,1)S(1)}, bf16[128,256]{1,0:T(8,128)(2,1)S(1)}, u32[]{:S(2)}, u32[]{:S(2)}) collective-permute-start(bf16[128,256]{1,0:T(8,128)(2,1)S(1)} %get-tuple-element.75), channel_id=1, source_target_pairs={{0,2},{1,3},{2,4},{3,5},{4,6},{5,7},{6,0},{7,1},{8,10},{9,11},{10,... | collective-permute-start | bytes 196616 | tf_op jit(solution)/shard_map/ppermute | solution.py:826
  24.2 3.0 %collective-permute-start.7 = (bf16[144,768]{1,0:T(8,128)(2,1)S(1)}, bf16[144,768]{1,0:T(8,128)(2,1)S(1)}, u32[]{:S(2)}, u32[]{:S(2)}) collective-permute-start(bf16[144,768]{1,0:T(8,128)(2,1)S(1)} %get-tuple-element.77), channel_id=1, source_target_pairs={{0,6},{1,7},{2,0},{3,1},{4,2},{5,3},{6,4},{7,5},{8,14},{9,15},{10,... | collective-permute-start | bytes 663560 | tf_op jit(solution)/shard_map/ppermute | solution.py:826
  29.0 4.8 %collective-permute-done.5 = bf16[144,768]{1,0:T(8,128)(2,1)S(1)} collective-permute-done((bf16[144,768]{1,0:T(8,128)(2,1)S(1)}, bf16[144,768]{1,0:T(8,128)(2,1)S(1)}, u32[]{:S(2)}, u32[]{:S(2)}) %collective-permute-start.5) | collective-permute-done | bytes 221216 | tf_op jit(solution)/shard_map/ppermute | solution.py:826
  33.8 18.7 %collective-permute-done.6 = bf16[144,768]{1,0:T(8,128)(2,1)S(1)} collective-permute-done((bf16[144,768]{1,0:T(8,128)(2,1)S(1)}, bf16[144,768]{1,0:T(8,128)(2,1)S(1)}, u32[]{:S(2)}, u32[]{:S(2)}) %collective-permute-start.6) | collective-permute-done | bytes 221216 | tf_op jit(solution)/shard_map/ppermute | solution.py:826
  57.1 3.4 %collective-permute-done.8 = bf16[128,1024]{1,0:T(8,128)(2,1)S(1)} collective-permute-done((bf16[128,1024]{1,0:T(8,128)(2,1)S(1)}, bf16[128,1024]{1,0:T(8,128)(2,1)S(1)}, u32[]{:S(2)}, u32[]{:S(2)}) %collective-permute-start.8) | collective-permute-done | bytes 262176 | tf_op jit(solution)/shard_map/ppermute | solution.py:794
  61.3 8.4 %collective-permute-done.15.refs_6_ = bf16[8,128,256]{2,1,0:T(8,128)(2,1)S(1)} collective-permute-done((bf16[8,128,256]{2,1,0:T(8,128)(2,1)S(1)}, bf16[8,128,256]{2,1,0:T(8,128)(2,1)S(1)}, u32[]{:S(2)}, u32[]{:S(2)}) %collective-permute-start.15) | collective-permute-done | bytes 524320 | tf_op jit(solution)/shard_map/ppermute | solution.py:794
  69.9 11.1 %collective-permute-done.4 = bf16[256,1024]{1,0:T(8,128)(2,1)S(1)} collective-permute-done((bf16[256,1024]{1,0:T(8,128)(2,1)S(1)}, bf16[256,1024]{1,0:T(8,128)(2,1)S(1)}, u32[]{:S(2)}, u32[]{:S(2)}) %collective-permute-start.4) | collective-permute-done | bytes 524320 | tf_op jit(solution)/shard_map/ppermute | solution.py:794
  81.0 7.7 %collective-permute-done.9 = bf16[256,1024]{1,0:T(8,128)(2,1)S(1)} collective-permute-done((bf16[256,1024]{1,0:T(8,128)(2,1)S(1)}, bf16[256,1024]{1,0:T(8,128)(2,1)S(1)}, u32[]{:S(2)}, u32[]{:S(2)}) %collective-permute-start.9) | collective-permute-done | bytes 524320 | tf_op jit(solution)/shard_map/ppermute | solution.py:794
  88.8 9.4 %mixer_forward.1 = (bf16[512,1024]{1,0:T(8,128)(2,1)S(1)}, f32[512,512]{1,0:T(8,128)}, f32[512,256]{1,0:T(8,128)S(1)}, f32[512,16]{1,0:T(8,128)S(1)}, f32[512,12...) custom-call(f32[2]{0:T(128)S(1)} %pad_maximum_fusion.4.scalars, ...), custom_call_target="tpu_custom_call" | custom-call | flops 8000000000 | bytes 8668160 | tf_op jit(solution)/shard_map/mixer_forward/pallas_call | solution.py:767
  106.6 3.2 %feed_forward_unpack.1 = (bf16[1024,1408]{1,0:T(8,128)(2,1)S(1)}, bf16[704,1024]{1,0:T(8,128)(2,1)S(1)}) custom-call(bf16[8,2176,128]{2,1,0:T(8,128)(2,1)} %bitcast.52), custom_call_target="tpu_custom_call" | custom-call | flops 100000000 | bytes 8781824 | tf_op jit(solution)/shard_map/feed_forward_unpack/pallas_call | solution.py:767
  112.5 4.1 %collective-permute-done.12.refs_2_ = bf16[512,256]{1,0:T(8,128)(2,1)S(1)} collective-permute-done((bf16[512,256]{1,0:T(8,128)(2,1)S(1)}, bf16[512,256]{1,0:T(8,128)(2,1)S(1)}, u32[]{:S(2)}, u32[]{:S(2)}) %collective-permute-start.12) | collective-permute-done | bytes 262176 | tf_op jit(solution)/shard_map/ppermute | solution.py:785
  118.2 11.8 %feed_forward.1 = (bf16[512,1024]{1,0:T(8,128)(2,1)S(1)}, f32[128,1024]{1,0:T(8,128)S(1)}, bf16[512,1024]{1,0:T(8,128)(2,1)}, bf16[512,704]{1,0:T(8,128)(2,1)S(1...) custom-call(s32[2]{0:T(128)S(1)} %pad_add_fusion.places.scalars, ...), custom_call_target="tpu_custom_call" | custom-call | flops 10000000000 | bytes 18554880 | tf_op jit(solution)/shard_map/feed_forward/pallas_call | solution.py:767
  133.6 4.7 %feed_forward_weights.1 = bf16[8,2176,128]{2,1,0:T(8,128)(2,1)} custom-call(bf16[512,1024]{1,0:T(8,128)(2,1)S(1)} %copy-done.26, bf16[512,1408]{1,0:T(8,128)(2,1)S(1)} %copy-done.25, bf16[512,704]{1,0:T(8,128)(2,1)S(1)} %get-tuple-element.88.active, bf16[512,1024]{1,0:T(8,128)(2,1)S(1)} %copy-done.12), custom_call_target="tpu_custom_call" | custom-call | flops 6000000000 | bytes 8716288 | tf_op jit(solution)/shard_map/feed_forward_weights/pallas_call | solution.py:767
  143.1 5.8 %collective-permute-done.17 = bf16[128,1024]{1,0:T(8,128)(2,1)S(1)} collective-permute-done((bf16[128,1024]{1,0:T(8,128)(2,1)S(1)}, bf16[128,1024]{1,0:T(8,128)(2,1)S(1)}, u32[]{:S(2)}, u32[]{:S(2)}) %collective-permute-start.17) | collective-permute-done | bytes 262176 | tf_op jit(solution)/shard_map/ppermute | solution.py:805
  148.9 3.0 %collective-permute-done.18 = bf16[128,1024]{1,0:T(8,128)(2,1)S(1)} collective-permute-done((bf16[128,1024]{1,0:T(8,128)(2,1)S(1)}, bf16[128,1024]{1,0:T(8,128)(2,1)S(1)}, u32[]{:S(2)}, u32[]{:S(2)}) %collective-permute-start.18) | collective-permute-done | bytes 262176 | tf_op jit(solution)/shard_map/ppermute | solution.py:805
  156.8 3.5 %collective-permute-done.20.refs_1_ = bf16[128,1024]{1,0:T(8,128)(2,1)S(1)} collective-permute-done((bf16[128,1024]{1,0:T(8,128)(2,1)S(1)}, bf16[128,1024]{1,0:T(8,128)(2,1)S(1)}, u32[]{:S(2)}, u32[]{:S(2)}) %collective-permute-start.20) | collective-permute-done | bytes 262176 | tf_op jit(solution)/shard_map/ppermute | solution.py:785
  160.3 5.3 %collective-permute-done.21.refs_2_ = bf16[128,1024]{1,0:T(8,128)(2,1)S(1)} collective-permute-done((bf16[128,1024]{1,0:T(8,128)(2,1)S(1)}, bf16[128,1024]{1,0:T(8,128)(2,1)S(1)}, u32[]{:S(2)}, u32[]{:S(2)}) %collective-permute-start.21) | collective-permute-done | bytes 262176 | tf_op jit(solution)/shard_map/ppermute | solution.py:785
  165.6 15.0 %mixer_backward.1 = (bf16[4,144,1024]{2,1,0:T(8,128)(2,1)}, bf16[4,144,1024]{2,1,0:T(8,128)(2,1)}, bf16[512,1024]{1,0:T(8,128)(2,1)S(1)}) custom-call(f32[2]{0:T(128)S(1)} %pad_maximum_fusion.4.scalars, s32[2]{0:T(128)S(1)} %pad_add_fusion.places.scalars, bf16[128,1024]{1,0:T(8,128)(2,1)S(1)} %get-tuple-element.154.refs_0_, ...), custom_call_target="tpu_custom_call" | custom-call | flops 10000000000 | bytes 14234624 | tf_op jit(solution)/shard_map/mixer_backward/pallas_call | solution.py:767
  180.6 3.2 %collective-permute-done.29 = bf16[4,144,1024]{2,1,0:T(8,128)(2,1)} collective-permute-done((bf16[4,144,1024]{2,1,0:T(8,128)(2,1)}, bf16[4,144,1024]{2,1,0:T(8,128)(2,1)}, u32[]{:S(2)}, u32[]{:S(2)}) %collective-permute-start.29) | collective-permute-done | bytes 1179680 | tf_op jit(solution)/shard_map/ppermute | solution.py:836
  186.8 16.3 %collective-permute-start.30 = (bf16[144,1024]{1,0:T(8,128)(2,1)}, bf16[144,1024]{1,0:T(8,128)(2,1)}, u32[]{:S(2)}, u32[]{:S(2)}) collective-permute-start(bf16[144,1024]{1,0:T(8,128)(2,1)} %get-tuple-element.156), channel_id=1, source_target_pairs={{0,2},{1,3},{2,4},{3,5},{4,6},{5,7},{6,0},{7,1},{8,10},{9,11},{10,... | collective-permute-start | bytes 884744 | tf_op jit(solution)/shard_map/ppermute | solution.py:846
  213.4 8.3 %collective-permute-done.31 = bf16[144,1024]{1,0:T(8,128)(2,1)S(1)} collective-permute-done((bf16[144,1024]{1,0:T(8,128)(2,1)}, bf16[144,1024]{1,0:T(8,128)(2,1)S(1)}, u32[]{:S(2)}, u32[]{:S(2)}) %collective-permute-start.31) | collective-permute-done | bytes 294944 | tf_op jit(solution)/shard_map/ppermute | solution.py:846
  232.4 4.5 %collective-permute-done.27 = bf16[128,1024]{1,0:T(8,128)(2,1)} collective-permute-done((bf16[128,1024]{1,0:T(8,128)(2,1)}, bf16[128,1024]{1,0:T(8,128)(2,1)}, u32[]{:S(2)}, u32[]{:S(2)}) %collective-permute-start.27) | collective-permute-done | bytes 262176 | tf_op jit(solution)/shard_map/ppermute | solution.py:805
  248.4 24.7 %collective-permute-done.34.refs_2_ = bf16[144,1024]{1,0:T(8,128)(2,1)S(1)} collective-permute-done((bf16[144,1024]{1,0:T(8,128)(2,1)S(1)}, bf16[144,1024]{1,0:T(8,128)(2,1)S(1)}, u32[]{:S(2)}, u32[]{:S(2)}) %collective-permute-start.34) | collective-permute-done | bytes 294944 | tf_op jit(solution)/shard_map/ppermute | solution.py:785
  276.6 3.8 %feed_forward_finish.1 = (f32[128,2816]{1,0:T(8,128)}, f32[128,2816]{1,0:T(8,128)}, f32[352,1024]{1,0:T(8,128)}) custom-call(s32[2]{0:T(128)S(1)} %pad_add_fusion.places.scalars, bf16[2176,128]{1,0:T(8,128)(2,1)S(1)} %bitcast.42, bf16[2176,128]{1,0:T(8,128)(2,1)S(1)} %collective-permute-done.36.refs_1_, ...), custom_call_target="tpu_custom_call" | custom-call | flops 100000000 | bytes 6553600 | tf_op jit(solution)/shard_map/feed_forward_finish/pallas_call | solution.py:767
  (205 shorter events, 85.3 us)
Async XLA Ops:
  7.2 99.4 %all-gather.3.cloned.1.call-start = ((), (), s32[]{:S(2)}) async-start(), calls=%async_computation.2 | async-start | bytes 5013504 | tf_op jit(solution)/shard_map/all_gather | solution.py:948
  12.4 217.1 %reduce-scatter.2.cloned.1.call-start = ((), (), s32[]{:S(2)}) async-start(), calls=%async_computation.1 | async-start | bytes 5013504 | tf_op jit(solution)/shard_map/reduce_scatter | solution.py:1060
  21.3 31.2 %collective-permute-start.6 = (bf16[144,768]{1,0:T(8,128)(2,1)S(1)}, bf16[144,768]{1,0:T(8,128)(2,1)S(1)}, u32[]{:S(2)}, u32[]{:S(2)}) collective-permute-start(bf16[144,768]{1,0:T(8,128)(2,1)S(1)} %get-tuple-element.77), channel_id=1, source_target_pairs={{0,4},{1,5},{2,6},{3,7},{4,0},{5,1},{6,2},{7,3},{8,12},{9,13},{10,... | collective-permute-start | bytes 663560 | tf_op jit(solution)/shard_map/ppermute | solution.py:826
  24.2 28.3 %collective-permute-start.7 = (bf16[144,768]{1,0:T(8,128)(2,1)S(1)}, bf16[144,768]{1,0:T(8,128)(2,1)S(1)}, u32[]{:S(2)}, u32[]{:S(2)}) collective-permute-start(bf16[144,768]{1,0:T(8,128)(2,1)S(1)} %get-tuple-element.77), channel_id=1, source_target_pairs={{0,6},{1,7},{2,0},{3,1},{4,2},{5,3},{6,4},{7,5},{8,14},{9,15},{10,... | collective-permute-start | bytes 663560 | tf_op jit(solution)/shard_map/ppermute | solution.py:826
  27.3 27.5 %collective-permute-start.14 = (bf16[4,128,256]{2,1,0:T(8,128)(2,1)S(1)}, bf16[4,128,256]{2,1,0:T(8,128)(2,1)S(1)}, u32[]{:S(2)}, u32[]{:S(2)}) collective-permute-start(bf16[4,128,256]{2,1,0:T(8,128)(2,1)S(1)} %pad_maximum_fusion.3), channel_id=1, source_target_pairs={{0,1},{1,0},{2,3},{3,2},{4,5},{5,4},{6,7},{7,6},{8,9},{9,8},{10,11... | collective-permute-start | bytes 786440 | tf_op jit(solution)/shard_map/ppermute | solution.py:832
  27.4 29.1 %collective-permute-start.3 = (bf16[128,1024]{1,0:T(8,128)(2,1)S(1)}, bf16[128,1024]{1,0:T(8,128)(2,1)S(1)}, u32[]{:S(2)}, u32[]{:S(2)}) collective-permute-start(bf16[128,1024]{1,0:T(8,128)(2,1)S(1)} %copy-done.40), channel_id=1, source_target_pairs={{0,8},{8,0},{16,24},{24,16},{1,9},{9,1},{17,25},{25,17},{2,10},{10... | collective-permute-start | bytes 786440 | tf_op jit(solution)/shard_map/ppermute | solution.py:794
  54.8 14.9 %collective-permute-start.15 = (bf16[8,128,256]{2,1,0:T(8,128)(2,1)S(1)}, bf16[8,128,256]{2,1,0:T(8,128)(2,1)S(1)}, u32[]{:S(2)}, u32[]{:S(2)}) collective-permute-start(bf16[8,128,256]{2,1,0:T(8,128)(2,1)S(1)} %get-tuple-element.172.refs_4_), channel_id=1, source_target_pairs={{0,16},{8,24},{16,0},{24,8},{1,17},{9,25},{17,1},{25,9},{2,18},{10... | collective-permute-start | bytes 1572872 | tf_op jit(solution)/shard_map/ppermute | solution.py:794
  56.4 32.4 %collective-permute-start.10 = (bf16[4,144,768]{2,1,0:T(8,128)(2,1)S(1)}, bf16[4,144,768]{2,1,0:T(8,128)(2,1)S(1)}, u32[]{:S(2)}, u32[]{:S(2)}) collective-permute-start(bf16[4,144,768]{2,1,0:T(8,128)(2,1)S(1)} %pad_maximum_fusion.mine), channel_id=1, source_target_pairs={{0,1},{1,0},{2,3},{3,2},{4,5},{5,4},{6,7},{7,6},{8,9},{9,8},{10,11... | collective-permute-start | bytes 2654216 | tf_op jit(solution)/shard_map/ppermute | solution.py:832
  56.5 24.4 %collective-permute-start.4 = (bf16[256,1024]{1,0:T(8,128)(2,1)S(1)}, bf16[256,1024]{1,0:T(8,128)(2,1)S(1)}, u32[]{:S(2)}, u32[]{:S(2)}) collective-permute-start(bf16[256,1024]{1,0:T(8,128)(2,1)S(1)} %pad_maximum_fusion.1), channel_id=1, source_target_pairs={{0,16},{8,24},{16,0},{24,8},{1,17},{9,25},{17,1},{25,9},{2,18},{10... | collective-permute-start | bytes 1572872 | tf_op jit(solution)/shard_map/ppermute | solution.py:794
  60.5 28.2 %collective-permute-start.9 = (bf16[256,1024]{1,0:T(8,128)(2,1)S(1)}, bf16[256,1024]{1,0:T(8,128)(2,1)S(1)}, u32[]{:S(2)}, u32[]{:S(2)}) collective-permute-start(bf16[256,1024]{1,0:T(8,128)(2,1)S(1)} %pad_maximum_fusion.2), channel_id=1, source_target_pairs={{0,16},{8,24},{16,0},{24,8},{1,17},{9,25},{17,1},{25,9},{2,18},{10... | collective-permute-start | bytes 1572872 | tf_op jit(solution)/shard_map/ppermute | solution.py:794
  69.8 36.7 %collective-permute-start.16 = (bf16[16,128,256]{2,1,0:T(8,128)(2,1)S(1)}, bf16[16,128,256]{2,1,0:T(8,128)(2,1)S(1)}, u32[]{:S(2)}, u32[]{:S(2)}) collective-permute-start(bf16[16,128,256]{2,1,0:T(8,128)(2,1)S(1)} %constant_dynamic-update-slice_fusion.11), channel_id=1, source_target_pairs={{0,8},{8,0},{16,24},{24,16},{1,9},{9,1},{17,25},{25,17},{2,10},{10... | collective-permute-start | bytes 3145736 | tf_op jit(solution)/shard_map/ppermute | solution.py:794
  186.8 24.0 %collective-permute-start.30 = (bf16[144,1024]{1,0:T(8,128)(2,1)}, bf16[144,1024]{1,0:T(8,128)(2,1)}, u32[]{:S(2)}, u32[]{:S(2)}) collective-permute-start(bf16[144,1024]{1,0:T(8,128)(2,1)} %get-tuple-element.156), channel_id=1, source_target_pairs={{0,2},{1,3},{2,4},{3,5},{4,6},{5,7},{6,0},{7,1},{8,10},{9,11},{10,... | collective-permute-start | bytes 884744 | tf_op jit(solution)/shard_map/ppermute | solution.py:846
  203.1 18.6 %collective-permute-start.31 = (bf16[144,1024]{1,0:T(8,128)(2,1)}, bf16[144,1024]{1,0:T(8,128)(2,1)S(1)}, u32[]{:S(2)}, u32[]{:S(2)}) collective-permute-start(bf16[144,1024]{1,0:T(8,128)(2,1)} %get-tuple-element.158), channel_id=1, source_target_pairs={{0,4},{1,5},{2,6},{3,7},{4,0},{5,1},{6,2},{7,3},{8,12},{9,13},{10,... | collective-permute-start | bytes 884744 | tf_op jit(solution)/shard_map/ppermute | solution.py:846
  203.1 19.8 %collective-permute-start.32 = (bf16[144,1024]{1,0:T(8,128)(2,1)S(1)}, bf16[144,1024]{1,0:T(8,128)(2,1)S(1)}, u32[]{:S(2)}, u32[]{:S(2)}) collective-permute-start(bf16[144,1024]{1,0:T(8,128)(2,1)S(1)} %get-tuple-element.157), channel_id=1, source_target_pairs={{0,6},{1,7},{2,0},{3,1},{4,2},{5,3},{6,4},{7,5},{8,14},{9,15},{10,... | collective-permute-start | bytes 884744 | tf_op jit(solution)/shard_map/ppermute | solution.py:846
  206.6 18.9 %collective-permute-start.23 = (bf16[128,1024]{1,0:T(8,128)(2,1)S(1)}, bf16[128,1024]{1,0:T(8,128)(2,1)S(1)}, u32[]{:S(2)}, u32[]{:S(2)}) collective-permute-start(bf16[128,1024]{1,0:T(8,128)(2,1)S(1)} %get-tuple-element.162), channel_id=1, source_target_pairs={{0,8},{8,0},{16,24},{24,16},{1,9},{9,1},{17,25},{25,17},{2,10},{10... | collective-permute-start | bytes 786440 | tf_op jit(solution)/shard_map/ppermute | solution.py:805
  207.3 19.2 %collective-permute-start.24 = (bf16[128,1024]{1,0:T(8,128)(2,1)S(1)}, bf16[128,1024]{1,0:T(8,128)(2,1)S(1)}, u32[]{:S(2)}, u32[]{:S(2)}) collective-permute-start(bf16[128,1024]{1,0:T(8,128)(2,1)S(1)} %get-tuple-element.164), channel_id=1, source_target_pairs={{0,16},{8,24},{16,0},{24,8},{1,17},{9,25},{17,1},{25,9},{2,18},{10... | collective-permute-start | bytes 786440 | tf_op jit(solution)/shard_map/ppermute | solution.py:805
  210.8 16.9 %collective-permute-start.25 = (bf16[128,1024]{1,0:T(8,128)(2,1)S(1)}, bf16[128,1024]{1,0:T(8,128)(2,1)S(1)}, u32[]{:S(2)}, u32[]{:S(2)}) collective-permute-start(bf16[128,1024]{1,0:T(8,128)(2,1)S(1)} %get-tuple-element.163), channel_id=1, source_target_pairs={{0,24},{8,16},{16,8},{24,0},{1,25},{9,17},{17,9},{25,1},{2,26},{10... | collective-permute-start | bytes 786440 | tf_op jit(solution)/shard_map/ppermute | solution.py:805
  222.9 14.0 %collective-permute-start.27 = (bf16[128,1024]{1,0:T(8,128)(2,1)}, bf16[128,1024]{1,0:T(8,128)(2,1)}, u32[]{:S(2)}, u32[]{:S(2)}) collective-permute-start(bf16[128,1024]{1,0:T(8,128)(2,1)} %get-tuple-element.161), channel_id=1, source_target_pairs={{0,16},{8,24},{16,0},{24,8},{1,17},{9,25},{17,1},{25,9},{2,18},{10... | collective-permute-start | bytes 786440 | tf_op jit(solution)/shard_map/ppermute | solution.py:805
  226.5 16.7 %collective-permute-start.33 = (bf16[144,1024]{1,0:T(8,128)(2,1)S(1)}, bf16[144,1024]{1,0:T(8,128)(2,1)S(1)}, u32[]{:S(2)}, u32[]{:S(2)}) collective-permute-start(bf16[144,1024]{1,0:T(8,128)(2,1)S(1)} %fusion.2.refs_0_), channel_id=1, source_target_pairs={{0,8},{8,0},{16,24},{24,16},{1,9},{9,1},{17,25},{25,17},{2,10},{10... | collective-permute-start | bytes 884744 | tf_op jit(solution)/shard_map/ppermute | solution.py:785
  229.5 47.0 %collective-permute-start.36 = (bf16[2176,128]{1,0:T(8,128)(2,1)}, bf16[2176,128]{1,0:T(8,128)(2,1)S(1)}, u32[]{:S(2)}, u32[]{:S(2)}) collective-permute-start(bf16[2176,128]{1,0:T(8,128)(2,1)} %bitcast.39), channel_id=1, source_target_pairs={{0,8},{8,0},{16,24},{24,16},{1,9},{9,1},{17,25},{25,17},{2,10},{10... | collective-permute-start | bytes 1671176 | tf_op jit(solution)/shard_map/ppermute | solution.py:785
  231.3 45.2 %collective-permute-start.37 = (bf16[2176,128]{1,0:T(8,128)(2,1)}, bf16[2176,128]{1,0:T(8,128)(2,1)S(1)}, u32[]{:S(2)}, u32[]{:S(2)}) collective-permute-start(bf16[2176,128]{1,0:T(8,128)(2,1)} %bitcast.40), channel_id=1, source_target_pairs={{0,16},{8,24},{16,0},{24,8},{1,17},{9,25},{17,1},{25,9},{2,18},{10... | collective-permute-start | bytes 1671176 | tf_op jit(solution)/shard_map/ppermute | solution.py:785
  236.9 39.6 %collective-permute-start.38 = (bf16[2176,128]{1,0:T(8,128)(2,1)}, bf16[2176,128]{1,0:T(8,128)(2,1)}, u32[]{:S(2)}, u32[]{:S(2)}) collective-permute-start(bf16[2176,128]{1,0:T(8,128)(2,1)} %bitcast.41), channel_id=1, source_target_pairs={{0,24},{8,16},{16,8},{24,0},{1,25},{9,17},{17,9},{25,1},{2,26},{10... | collective-permute-start | bytes 1671176 | tf_op jit(solution)/shard_map/ppermute | solution.py:785
  239.1 34.1 %collective-permute-start.34 = (bf16[144,1024]{1,0:T(8,128)(2,1)S(1)}, bf16[144,1024]{1,0:T(8,128)(2,1)S(1)}, u32[]{:S(2)}, u32[]{:S(2)}) collective-permute-start(bf16[144,1024]{1,0:T(8,128)(2,1)S(1)} %fusion.2.refs_0_), channel_id=1, source_target_pairs={{0,16},{8,24},{16,0},{24,8},{1,17},{9,25},{17,1},{25,9},{2,18},{10... | collective-permute-start | bytes 884744 | tf_op jit(solution)/shard_map/ppermute | solution.py:785
  243.9 29.3 %collective-permute-start.35 = (bf16[144,1024]{1,0:T(8,128)(2,1)S(1)}, bf16[144,1024]{1,0:T(8,128)(2,1)S(1)}, u32[]{:S(2)}, u32[]{:S(2)}) collective-permute-start(bf16[144,1024]{1,0:T(8,128)(2,1)S(1)} %fusion.2.refs_0_), channel_id=1, source_target_pairs={{0,24},{8,16},{16,8},{24,0},{1,25},{9,17},{17,9},{25,1},{2,26},{10... | collective-permute-start | bytes 884744 | tf_op jit(solution)/shard_map/ppermute | solution.py:785
  (66 other events, 471.5 us)
Sparse Core Ops, SparseCore 0:
  12.6 68.7 all-gather.2
  138.4 70.2 reduce-scatter.1
where the time goes:
time: 292 us; the launch traced here: 287 us
  waiting for transfers between devices  122 us (42%)
  starting transfers between devices  62.5 us (21%)
  Pallas kernels  52.1 us (18%)
  local copies, waits for them, and re-layouts  24.2 us (8%)
  between operations  15.3 us (5%)
  other arithmetic  11.4 us (4%)
    pallas_call x9, Pallas kernels, run_kernel(): pl.pallas_call(kernel, out_shape=tuple(outs), in_specs=[pl.BlockSpec(memo...  52.1 us
    ppermute x12, waiting for transfers between devices, team_gather(): lax.ppermute(block, 'rep', team_pairs(devices, steps))  39.9 us
    ppermute x6, waiting for transfers between devices, team_double(): moved = lax.ppermute(both, 'rep', team_pairs(devices, bit))  30.6 us
    ppermute x6, waiting for transfers between devices, line_gather(): lax.ppermute(block, 'shard', line_ring(shards, steps))  23.5 us
    unnamed x111, local copies, waits for them, and re-layouts  19.8 us
    ppermute x3, starting transfers between devices, line_send(): terms.append(lax.ppermute(block, 'shard', line_ring(shards, steps)))  18.7 us
    ppermute x12, starting transfers between devices, team_gather(): lax.ppermute(block, 'rep', team_pairs(devices, steps))  14.7 us
    ppermute x9, waiting for transfers between devices, team_send(): lax.ppermute(slots[steps], 'rep', team_pairs(devices, steps))  14.2 us
  transfers between devices with their start and end apart: 41, of which 18 were waited for; matrix products, arithmetic and copies ran while one was open for 6% of the time, Pallas kernels for 11%

commit v1 on v0

--- a/solution.py
+++ b/solution.py
@@ -136,7 +136,7 @@
     value_conv,
     head_gain,
     pack_out,
-    proj_out,
+    sems,
 ):
     part, shard = places[0], places[1]
     chunk = query.shape[0]
@@ -145,24 +145,24 @@
     width = pack_out.shape[1]
     count = query_conv.shape[0]
     head_each = head_gain.shape[1]
-
-    def columns(matrix, size):
-        return matrix[:, pl.ds(pl.multiple_of(part * size, size), size)]
-
-    pack_out[:chunk, :keys] = columns(query, keys)
-    pack_out[:chunk, keys : 2 * keys] = columns(key, keys)
-    pack_out[:chunk, 2 * keys : 2 * keys + values] = columns(value, values)
-    pack_out[:chunk, 2 * keys + values :] = columns(gate, values)
-    proj_out[...] = columns(proj, outs)
-    rows, cols = iotas(chunk)
-
-    def column_row(matrix):
-        lane = lax.broadcasted_iota(jnp.int32, matrix.shape, 1)
-        column = jnp.sum(jnp.where(lane == part, matrix[...].astype(WIDE), 0.0), 1, keepdims=True)
-        return jnp.sum(jnp.where(rows == cols, column, 0.0), 0, keepdims=True)
+    copies = []
+    start = 0
+    for index, (matrix, size) in enumerate(
+        ((query, keys), (key, keys), (value, values), (gate, values), (proj, outs))
+    ):
+        source = matrix.at[:, pl.ds(pl.multiple_of(part * size, size), size)]
+        target = pack_out.at[:chunk, start : start + size]
+        start += size
+        copies.append(pltpu.make_async_copy(source, target, sems.at[index]))
+    for copy in copies:
+        copy.start()
+
+    def head_row(matrix):
+        line = lax.broadcasted_iota(jnp.int32, matrix.shape, 0)
+        return jnp.sum(jnp.where(line == part, matrix[...].astype(WIDE), 0.0), 0, keepdims=True)
 
     gains = [mix_gain[...].astype(WIDE), ffn_gain[...].astype(WIDE)]
-    gains += [column_row(beta), column_row(decay)]
+    gains += [head_row(beta), head_row(decay)]
     gains.append(jnp.zeros((1, width - 4 * chunk), WIDE))
     pieces = []
     for taps, size in ((query_conv, keys), (key_conv, keys), (value_conv, values)):
@@ -191,11 +191,12 @@
         0,
     )
     pack_out[chunk:] = small.astype(LOW)
-
-
-def slot_shard(places, slot, chips, same_core):
-    chip, core = lax.div(places[1], 2), lax.rem(places[1], 2)
-    return 2 * lax.rem(chip + chips - slot, chips) + (core if same_core else 1 - core)
+    for copy in copies:
+        copy.wait()
+
+
+def slot_shard(places, slot, same_core):
+    return jnp.bitwise_xor(places[1], 2 * slot + (0 if same_core else 1))
 
 
 def mixer_forward_kernel(
@@ -232,9 +233,9 @@
     total = None
     for same_core, slots in ((True, mine), (False, theirs)):
         for slot in range(chips):
-            shard = slot_shard(places, slot, chips, same_core)
+            shard = slot_shard(places, slot, same_core)
             line = pl.ds(pl.multiple_of(shard * chunk, chunk), chunk)
-            weights[line, :] = slots[slot, :chunk]
+            weights[line, :] = slots[slot, :chunk, : conv_width + values]
             small = slots[slot, chunk:].astype(WIDE)
             mix_row[:, line] = small[0:1, :chunk]
             ffn_row[:, line] = small[0:1, chunk : 2 * chunk]
@@ -283,26 +284,32 @@
 def feed_forward_kernel(
     team,
     scalars,
-    tokens,
-    cotangents,
     *refs,
 ):
-    mixed_slots, out_slots = refs[:team], refs[team : 2 * team]
+    far_out, far = refs[:team], refs[team : team + 3]
+    mixed_slots, gain = refs[team + 3 : 2 * team + 3], refs[2 * team + 3]
     (
-        gain,
-        up_weights,
-        down_weights,
         mixed_out,
         hidden_out,
-        second_out,
-        active_out,
-        back_out,
         second_grad_out,
         gain_grad_out,
         result_out,
         out_full,
+        grads_out,
         hidden,
-    ) = refs[2 * team :]
+        up_weights,
+        down_weights,
+        *near,
+        sems,
+    ) = refs[2 * team + 4 :]
+    fetch = [
+        pltpu.make_async_copy(source, target, sems.at[index])
+        for index, (source, target) in enumerate(zip((*far_out, *far), near))
+    ]
+    for copy in fetch:
+        copy.start()
+    out_slots = near[:team]
+    tokens, packs, cotangents = near[team:]
     part = scalars[0]
     size = tokens.shape[0] // team
     values = mixed_slots[0].shape[1]
@@ -316,43 +323,54 @@
             ][there * size : (there + 1) * size]
     blocks = out_slots[0].shape[0]
     chunk = out_slots[0].shape[1]
+    for copy in fetch[: team + 1]:
+        copy.wait()
     for steps in range(team):
         place = pl.multiple_of(member(part, steps) * outs, outs)
         for slot in range(blocks):
             chips = blocks // 2
-            shard = slot_shard(scalars, slot % chips, chips, slot < chips)
+            shard = slot_shard(scalars, slot % chips, slot < chips)
             line = pl.ds(pl.multiple_of(shard * chunk, chunk), chunk)
             out_full[line, pl.ds(place, outs)] = out_slots[steps][slot]
     wide = tokens[...].astype(WIDE) + local_dot(mixed_out[...], out_full[...])
     hidden_out[...] = wide[:size]
     normed = wide * lax.rsqrt(jnp.mean(wide * wide, -1, keepdims=True) + EPS)
     second = (normed * gain[...]).astype(LOW)
-    second_out[...] = second
     hidden[...] = normed
-    part_width = active_out.shape[1]
+    fetch[team + 1].wait()
+    feed_forward_unpack(packs.shape[0], packs, up_weights, down_weights)
+    fetch[team + 2].wait()
+    part_width = down_weights.shape[0]
     both = local_dot(second, up_weights[...])
     gate, up = both[:, :part_width], both[:, part_width:]
     gate_sig = sigmoid(gate)
     gate_act = gate * gate_sig
     active = (gate_act * up).astype(LOW)
-    active_out[...] = active
     result_out[...] = local_dot(active, down_weights[...]).astype(LOW)
     active_grad = right_dot(cotangents[...], down_weights[...])
     gate_back = (active_grad * up * gate_sig * (1.0 + gate * (1.0 - gate_sig))).astype(LOW)
     up_back = (active_grad * gate_act).astype(LOW)
     back = jnp.concatenate([gate_back, up_back], 1)
-    back_out[...] = back
     second_grad = right_dot(back, up_weights[...])
     second_grad_out[...] = second_grad.astype(LOW)
     gain_grad_out[...] = jnp.sum(second_grad * hidden[...], 0, keepdims=True)
-
-
-def feed_forward_pack_kernel(team, shards, places, gate, up, down, pack):
+    feed_forward_pack_grads(grads_out.shape[0], second, back, active, cotangents[...], grads_out)
+
+
+def feed_forward_pack_kernel(team, shards, places, gate_far, up_far, down_far, pack, gate, up, down, sems):
+    fetch = [
+        pltpu.make_async_copy(far, near, sems.at[index])
+        for index, (far, near) in enumerate(((gate_far, gate), (up_far, up), (down_far, down)))
+    ]
+    for copy in fetch:
+        copy.start()
     chunk = gate.shape[0]
     each = down.shape[0] // team
     padded = -(-each // ROWS16) * ROWS16
     ups = 2 * shards * each // LANES
     pad = jnp.zeros((padded - each, LANES), WIDE)
+    for copy in fetch:
+        copy.wait()
 
     for choice in range(team):
 
@@ -374,7 +392,7 @@
                 pack[start : start + padded] = jnp.concatenate([block, pad], 0).astype(LOW)
 
 
-def feed_forward_unpack_kernel(shards, packs, up_out, down_out):
+def feed_forward_unpack(shards, packs, up_out, down_out):
     chunk = up_out.shape[0] // shards
     each = down_out.shape[0] // shards
     padded = -(-each // ROWS16) * ROWS16
@@ -399,9 +417,9 @@
             ] = block.astype(LOW)
 
 
-def feed_forward_weights_kernel(shards, second, back, active, cotangents, pack):
-    up_grad = left_dot(second[...], back[...])
-    down_grad = left_dot(active[...], cotangents[...])
+def feed_forward_pack_grads(shards, second, back, active, cotangents, pack):
+    up_grad = left_dot(second, back)
+    down_grad = left_dot(active, cotangents)
     chunk = up_grad.shape[0] // shards
     each = down_grad.shape[0] // shards
     padded = -(-each // ROWS16) * ROWS16
@@ -421,15 +439,16 @@
 
 
 def feed_forward_finish_kernel(team, shards, places, *refs):
-    slots = refs[:team]
-    gate_out, up_out, down_out, ordered = refs[team:]
+    *slots, gate_out, up_out, down_out, ordered = refs
     chunk = gate_out.shape[0]
     each = down_out.shape[0] // team
     padded = -(-each // ROWS16) * ROWS16
     half = shards * each
     ups = 2 * half // LANES
-    for steps in range(team):
-        ordered[member(places[0], steps)] = slots[steps][...].astype(LOW)
+    size = slots[0].shape[0]
+    for index, slot in enumerate(slots):
+        start = index // team * size
+        ordered[member(places[0], index % team), start : start + size] = slot[...].astype(LOW)
     wide = [
         jnp.concatenate(
             [ordered[h, i * chunk : (i + 1) * chunk].astype(WIDE) for i in range(ups)], 1
@@ -478,8 +497,7 @@
         gate_rows,
         tokens,
         ffn_gain_grad,
-        mine,
-        theirs,
+        pack,
         first_grad_out,
         raw_grad_out,
         gates_grad_out,
@@ -591,7 +609,6 @@
         raw_grad_out[span] = raw_grad.astype(LOW)
     width = tokens.shape[1]
     chunk = width // shards
-    core = lax.rem(shard, 2)
     raw_low = raw_grad_out[...]
     head_wgrad = left_dot(first[...], raw_low)
     gates_rows = left_dot(gates_grad_out[...], first[...])
@@ -670,10 +687,9 @@
         (top, slice(conv_width + values, conv_width + values + outs)),
         (slice(chunk, chunk + ROWS16), all_lanes),
     )
-    for pair in range(shards // 2):
-        for even, odd, (line, lanes) in zip(blocks[2 * pair], blocks[2 * pair + 1], spots):
-            mine[pair, line, lanes] = jnp.where(core == 0, even, odd).astype(LOW)
-            theirs[pair, line, lanes] = jnp.where(core == 0, odd, even).astype(LOW)
+    for s in range(shards):
+        for block, (line, lanes) in zip(blocks[s], spots):
+            pack[s, line, lanes] = block.astype(LOW)
 
 
 def finish_kernel(
@@ -744,9 +760,8 @@
         )
         log_row = jnp.where(lane == head, log_sum, log_row)
         bias_row = jnp.where(lane == head, bias_sum, bias_row)
-    flipped = pair[...].T
-    beta_out[...] = flipped[:, :team]
-    decay_out[...] = flipped[:, team : 2 * team]
+    beta_out[...] = pair[:team]
+    decay_out[...] = pair[team : 2 * team]
     mix_out[...] = total[0:1, 2 * chunk : 3 * chunk]
     ffn_out[...] = total[0:1, 3 * chunk : 4 * chunk]
     query_conv_out[...] = total[1 : count + 1, :key_each]
@@ -761,16 +776,18 @@
     return jax.ShapeDtypeStruct(shape, dtype)
 
 
-def run_kernel(kernel, name, scalars, operands, outs, flops, scratch=()):
+def run_kernel(kernel, name, scalars, operands, outs, flops, scratch=(), far=0):
     spec = pl.BlockSpec(memory_space=pltpu.VMEM)
     moved = sum(math.prod(v.shape) * v.dtype.itemsize for v in (*operands, *outs))
     return pl.pallas_call(
         kernel,
         out_shape=tuple(outs),
-        in_specs=[pl.BlockSpec(memory_space=pltpu.SMEM)] * len(scalars) + [spec] * len(operands),
+        in_specs=[pl.BlockSpec(memory_space=pltpu.SMEM)] * len(scalars)
+        + [pl.BlockSpec(memory_space=pl.ANY)] * far
+        + [spec] * (len(operands) - far),
         out_specs=[spec] * len(outs),
         scratch_shapes=list(scratch),
-        compiler_params=pltpu.CompilerParams(vmem_limit_bytes=48 * 1024 * 1024),
+        compiler_params=pltpu.CompilerParams(vmem_limit_bytes=(60 if far else 48) * 1024 * 1024),
         cost_estimate=pl.CostEstimate(flops=flops, bytes_accessed=moved, transcendentals=0),
         name=name,
     )(*scalars, *operands)
@@ -786,18 +803,29 @@
     ]
 
 
-def team_double(block, devices, team, axis, order):
-    size = block.shape[axis]
-    held = {0: block}
-    for bit in order:
-        both = jnp.concatenate([held[e] for e in held], axis) if len(held) > 1 else block
-        moved = lax.ppermute(both, "rep", team_pairs(devices, bit))
-        fresh = {
-            e ^ bit: lax.slice_in_dim(moved, i * size, (i + 1) * size, axis=axis)
-            for i, e in enumerate(held)
-        }
-        held = held | fresh
-    return [held[e] for e in range(team)]
+def swap(block, name, size, mask):
+    return lax.ppermute(block, name, [(j, j ^ mask) for j in range(size)])
+
+
+def line_gather(block, shards):
+    return [block] + [
+        swap(block, "shard", shards, 2 * steps) for steps in range(1, shards // 2)
+    ]
+
+
+def team_halves(block, devices):
+    half = block.shape[0] // 2
+    found = []
+    for part, (near, far) in ((block[:half], (1, 2)), (block[half:], (2, 1))):
+        pair = swap(part, "rep", devices, near)
+        quad = swap(both_ends(part, pair), "rep", devices, far)
+        held = {0: part, near: pair, far: quad[:half], near | far: quad[half:]}
+        found.append([held[e] for e in range(4)])
+    return found[0] + found[1]
+
+
+def both_ends(block, moved):
+    return jnp.concatenate([block, moved], 0)
 
 
 def team_send(slots, devices, team):
@@ -811,40 +839,6 @@
     for block in blocks[1:]:
         total = total + block.astype(WIDE)
     return total
-
-
-def line_ring(shards, steps):
-    return [(j, (j + 2 * steps) % shards) for j in range(shards)]
-
-
-def pair_ring(shards):
-    return [(j, j ^ 1) for j in range(shards)]
-
-
-def line_gather(block, shards):
-    return [block] + [
-        lax.ppermute(block, "shard", line_ring(shards, steps))
-        for steps in range(1, shards // 2)
-    ]
-
-
-def core_swap(block, shards):
-    return lax.ppermute(block, "shard", pair_ring(shards))
-
-
-def pair_sum(mine, theirs, shards):
-    moved = lax.ppermute(theirs, "shard", pair_ring(shards))
-    return (mine.astype(WIDE) + moved.astype(WIDE)).astype(LOW)
-
-
-def line_send(summed, shard, shards):
-    chips = shards // 2
-    chip = shard // 2
-    terms = [lax.dynamic_index_in_dim(summed, chip, 0, keepdims=False)]
-    for steps in range(1, chips):
-        block = lax.dynamic_index_in_dim(summed, (chip + steps) % chips, 0, keepdims=False)
-        terms.append(lax.ppermute(block, "shard", line_ring(shards, steps)))
-    return terms
 
 
 def norm_scale(v):
@@ -910,7 +904,7 @@
     padded = -(-hidden_each // ROWS16) * ROWS16
     ffn_rows = 2 * hidden_part * chunk // LANES + padded * (width // LANES)
 
-    mixer_pack, proj_part = run_kernel(
+    mixer_pack = run_kernel(
         functools.partial(pack_kernel, team),
         "pack",
         (places,),
@@ -920,8 +914,8 @@
             value_proj,
             gate_proj,
             out_proj,
-            beta_proj,
-            decay_proj,
+            beta_proj.T,
+            decay_proj.T,
             mix_gain[None],
             ffn_gain[None],
             query_conv,
@@ -930,31 +924,48 @@
             head_gain[None],
         ),
         (
-            array((chunk + ROWS16, conv_width + values), LOW),
-            array((chunk, outs), LOW),
+            array((chunk + ROWS16, conv_width + values + outs), LOW),
         ),
         10**8,
-    )
-    proj_slots = line_gather(proj_part, shards)
-    mixer_slots = line_gather(mixer_pack, shards)
+        (pltpu.SemaphoreType.DMA((5,)),),
+        5,
+    )[0]
+    pack_slots = line_gather(mixer_pack, shards)
+    token_pair = swap(inputs, "rep", devices, 1)
+    cotangent_pair = swap(cotangent, "rep", devices, 2)
+    token_pair = both_ends(inputs, token_pair)
+    cotangent_pair = both_ends(cotangent, cotangent_pair)
+    token_quad = swap(token_pair, "rep", devices, 2)
+    cotangent_quad = swap(cotangent_pair, "rep", devices, 1)
+    pack_slots = after(pack_slots, (token_quad, cotangent_quad))
     ffn_pack = run_kernel(
         functools.partial(feed_forward_pack_kernel, team, shards),
         "feed_forward_pack",
         (places,),
-        (ffn_gate, ffn_up, ffn_down),
+        (after(ffn_gate, pack_slots), ffn_up, ffn_down),
         (array((ffn_rows, LANES), LOW),),
         10**8,
+        (
+            pltpu.VMEM(ffn_gate.shape, LOW),
+            pltpu.VMEM(ffn_up.shape, LOW),
+            pltpu.VMEM(ffn_down.shape, LOW),
+            pltpu.SemaphoreType.DMA((3,)),
+        ),
+        3,
     )[0]
     ffn_packs = lax.all_gather(ffn_pack, "shard", axis=0)
-    proj_mine = jnp.stack(proj_slots)
-    proj_all = jnp.concatenate([proj_mine, core_swap(proj_mine, shards)], 0)
-    token_slots = team_double(after(inputs, proj_mine), devices, team, 0, (1, 2))
-    proj_slots = team_double(proj_all, devices, team, 0, (2, 1))
-    pack_mine = jnp.stack(mixer_slots)
-    pack_theirs = core_swap(pack_mine, shards)
-    cotangent_slots = team_double(after(cotangent, pack_mine), devices, team, 0, (1, 2))
-    tokens = jnp.concatenate(token_slots, 0)
-    cotangents = jnp.concatenate(cotangent_slots, 0)
+    pack_mine = jnp.stack(pack_slots)
+    pack_theirs = swap(pack_mine, "shard", shards, 1)
+    tokens = both_ends(token_pair, token_quad)
+    cotangents = jnp.concatenate(
+        [
+            cotangent,
+            cotangent_quad[:tokens_each],
+            cotangent_pair[tokens_each:],
+            cotangent_quad[tokens_each:],
+        ],
+        0,
+    )
     scalars = jnp.stack(
         [
             jnp.exp(lax.dynamic_index_in_dim(decay_log, part, 0, keepdims=False)),
@@ -1002,61 +1013,53 @@
         (pltpu.VMEM((ROWS16, width), WIDE),),
     )
     mixed_slots = team_gather(mixed_part, devices, team)
-    up_weights, down_weights = run_kernel(
-        functools.partial(feed_forward_unpack_kernel, shards),
-        "feed_forward_unpack",
-        (),
-        (ffn_packs,),
-        (
-            array((width, 2 * hidden_part), LOW),
-            array((hidden_part, width), LOW),
-        ),
-        10**8,
-    )
+    proj_all = both_ends(
+        pack_mine[:, :chunk, conv_width + values :],
+        pack_theirs[:, :chunk, conv_width + values :],
+    )
+    proj_all = after(proj_all, mixed_part)
+    proj_slots = team_gather(proj_all, devices, team)
 
     (
         mixed,
         hidden_own,
-        second,
-        active,
-        both_back,
         second_part,
         ffn_gain_part,
         result_part,
         out_full,
+        ffn_grads,
     ) = run_kernel(
         functools.partial(feed_forward_kernel, team),
         "feed_forward",
         (places,),
-        (tokens, cotangents, *mixed_slots, *proj_slots, ffn_row, up_weights, down_weights),
+        (*proj_slots, tokens, ffn_packs, cotangents, *mixed_slots, ffn_row),
         (
             array((count, width), LOW),
             array((tokens_each, width), WIDE),
             array((count, width), LOW),
-            array((count, hidden_part), LOW),
-            array((count, 2 * hidden_part), LOW),
-            array((count, width), LOW),
             array((1, width), WIDE),
             array((count, width), LOW),
             array((width, width), LOW),
+            array((shards, ffn_rows, LANES), LOW),
         ),
-        10 * 10**9,
-        (pltpu.VMEM((count, width), WIDE),),
+        16 * 10**9,
+        (
+            pltpu.VMEM((count, width), WIDE),
+            pltpu.VMEM((width, 2 * hidden_part), LOW),
+            pltpu.VMEM((hidden_part, width), LOW),
+            *(pltpu.VMEM(slot.shape, LOW) for slot in proj_slots),
+            pltpu.VMEM(tokens.shape, LOW),
+            pltpu.VMEM(ffn_packs.shape, LOW),
+            pltpu.VMEM(cotangents.shape, LOW),
+            pltpu.SemaphoreType.DMA((team + 3,)),
+        ),
+        team + 3,
     )
 
     def slots_of(v):
         return [v[e * tokens_each : (e + 1) * tokens_each] for e in range(team)]
 
     second_slots = team_send(slots_of(second_part), devices, team)
-    ffn_grads = run_kernel(
-        functools.partial(feed_forward_weights_kernel, shards),
-        "feed_forward_weights",
-        (),
-        (second, both_back, active, cotangents),
-        (array((shards, ffn_rows, LANES), LOW),),
-        6 * 10**9,
-    )[0]
-    second_slots = after(second_slots, ffn_grads)
     ffn_shard = lax.psum_scatter(ffn_grads, "shard", scatter_dimension=0)
     second_grad = wide_sum(second_slots)
     scale_own = norm_scale(hidden_own)
@@ -1067,10 +1070,9 @@
         * (scale_own * scale_own * jnp.mean(hidden_own * weighted, -1, keepdims=True))
     )
     branch_slots = team_gather(hidden_grad.astype(LOW), devices, team)
-    result_part = after(result_part, branch_slots)
-    result_slots = team_send(slots_of(result_part), devices, team)
-
-    head_mine, head_theirs, first_part = run_kernel(
+
+
+    head_grads, first_part = run_kernel(
         functools.partial(mixer_backward_kernel, team, keys, shards),
         "mixer_backward",
         (scalars, places),
@@ -1093,8 +1095,7 @@
             ffn_gain_part,
         ),
         (
-            array((shards // 2, chunk + ROWS16, conv_width + values + outs), LOW),
-            array((shards // 2, chunk + ROWS16, conv_width + values + outs), LOW),
+            array((shards, chunk + ROWS16, conv_width + values + outs), LOW),
             array((count, width), LOW),
         ),
         10 * 10**9,
@@ -1105,9 +1106,17 @@
             pltpu.VMEM((count, values), WIDE),
         ),
     )
-    head_summed = pair_sum(head_mine, head_theirs, shards)
-    head_terms = line_send(head_summed, shard, shards)
-    first_grad = wide_sum(team_send(slots_of(first_part), devices, team))
+    head_shard = lax.psum_scatter(head_grads, "shard", scatter_dimension=0)
+    last_slots = [
+        jnp.concatenate(pair, 0) for pair in zip(slots_of(first_part), slots_of(result_part))
+    ]
+    last_slots = team_send(last_slots, devices, team)
+    if devices == team == 4:
+        ffn_totals = team_halves(ffn_shard, devices)
+    else:
+        ffn_totals = replica_slots(ffn_shard, part, devices, team)
+    last = wide_sum(after(last_slots, ffn_totals))
+    first_grad = last[:tokens_each]
     seq_in = inputs.astype(WIDE)
     seq_scale = norm_scale(seq_in)
     weighted = first_grad * mix_row
@@ -1115,10 +1124,9 @@
         weighted
         - seq_in * (seq_scale * seq_scale * jnp.mean(seq_in * weighted, -1, keepdims=True))
     )
-    result = hidden_own + wide_sum(result_slots)
-
-    head_totals = replica_slots(wide_sum(head_terms).astype(LOW), part, devices, team)
-    ffn_totals = replica_slots(ffn_shard, part, devices, team)
+    result = hidden_own + last[tokens_each:]
+
+    head_totals = replica_slots(after(head_shard, ffn_totals), part, devices, team)
     gate_grads, up_grads, down_grads = run_kernel(
         functools.partial(feed_forward_finish_kernel, team, shards),
         "feed_forward_finish",
@@ -1159,8 +1167,8 @@
             array((chunk, team * values), WIDE),
             array((chunk, team * values), WIDE),
             array((chunk, team * outs), WIDE),
-            array((chunk, team), WIDE),
-            array((chunk, team), WIDE),
+            array((team, chunk), WIDE),
+            array((team, chunk), WIDE),
             array((1, chunk), WIDE),
             array((1, chunk), WIDE),
             array((taps_count, key_each), WIDE),
@@ -1180,8 +1188,8 @@
         query_total,
         key_total,
         value_total,
-        beta_total,
-        decay_total,
+        beta_total.T,
+        decay_total.T,
         gate_total,
         query_conv_total,
         key_conv_total,

time: 292 us -> 250 us (0.86)
  starting transfers between devices: 62.5 us -> 37.6 us
  local copies, waits for them, and re-layouts: 24.2 us -> 9.67 us
    ppermute x18 -> x12, starting transfers between devices: 36.5 us -> 17.5 us  [swap(): return lax.ppermute(block, name, [(j, j ^ mask) for j in range(size)])]
    unnamed x111 -> x88, local copies, waits for them, and re-layouts: 19.8 us -> 4.81 us
    concatenate x2 -> x10, other arithmetic: 0.07 us -> 5.72 us  [the longest x4 2.52 us: body(): jnp.concatenate(pair, 0)]
    convert_element_type x3 -> x0, other arithmetic: 5.14 us -> none  [the longest x1 2.14 us: pair_sum(): return (mine.astype(WIDE) + moved.astype(WIDE)).astype(LOW)]
    ppermute x9 -> x6, starting transfers between devices: 11.2 us -> 7.08 us  [team_send(): lax.ppermute(slots[steps], 'rep', team_pairs(devices, steps))]
    reduce_scatter x1, waiting for transfers between devices: 0.01 us -> 3.09 us  [body(): ffn_shard = lax.psum_scatter(ffn_grads, 'shard', scatter_dimension=0)]
    ppermute x9 -> x6, waiting for transfers between devices: 14.2 us -> 11.7 us  [team_send(): lax.ppermute(slots[steps], 'rep', team_pairs(devices, steps))]
    ppermute x18 -> x12, waiting for transfers between devices: 67.4 us -> 65.6 us  [swap(): return lax.ppermute(block, name, [(j, j ^ mask) for j in range(size)])]
  transfers between devices with their start and end apart: 41 -> 33, of which waited for: 18 -> 17; matrix products, arithmetic and copies ran while one was open for 6% -> 7% of each run, Pallas kernels for 11% -> 12%
where the time goes in v1:
time: 250 us; the launch traced here: 248 us
  waiting for transfers between devices  120 us (48%)
  Pallas kernels  52.3 us (21%)
  starting transfers between devices  37.6 us (15%)
  between operations  15.1 us (6%)
  other arithmetic  12.6 us (5%)
  local copies, waits for them, and re-layouts  9.67 us (4%)
    ppermute x12, waiting for transfers between devices, swap(): return lax.ppermute(block, name, [(j, j ^ mask) for j in range(size)])  65.6 us
    pallas_call x7, Pallas kernels, run_kernel(): pl.pallas_call(kernel, out_shape=tuple(outs), in_specs=[pl.BlockSpec(memo...  52.3 us
    ppermute x12, waiting for transfers between devices, team_gather(): lax.ppermute(block, 'rep', team_pairs(devices, steps))  39.9 us
    ppermute x12, starting transfers between devices, swap(): return lax.ppermute(block, name, [(j, j ^ mask) for j in range(size)])  17.5 us
    ppermute x12, starting transfers between devices, team_gather(): lax.ppermute(block, 'rep', team_pairs(devices, steps))  12.9 us
    ppermute x6, waiting for transfers between devices, team_send(): lax.ppermute(slots[steps], 'rep', team_pairs(devices, steps))  11.7 us
    ppermute x6, starting transfers between devices, team_send(): lax.ppermute(slots[steps], 'rep', team_pairs(devices, steps))  7.08 us
  transfers between devices with their start and end apart: 33, of which 17 were waited for; matrix products, arithmetic and copies ran while one was open for 7% of the time, Pallas kernels for 12%

profile of v1, /device:TPU:0, one launch (start us, length us, event | category | flops | bytes accessed | tf_op | source)
XLA Modules:
  0.0 247.6 jit_solution(2057395076959757532)
XLA Ops:
  7.2 3.0 %collective-permute-start.5 = (bf16[128,1024]{1,0:T(8,128)(2,1)}, bf16[128,1024]{1,0:T(8,128)(2,1)S(1)}, u32[]{:S(2)}, u32[]{:S(2)}) collective-permute-start(bf16[128,1024]{1,0:T(8,128)(2,1)} %param.21), channel_id=1, source_target_pairs={{0,16},{8,24},{16,0},{24,8},{1,17},{9,25},{17,1},{25,9},{2,18},{10... | collective-permute-start | bytes 786440 | tf_op jit(solution)/shard_map/ppermute | solution.py:807
  11.8 5.0 %collective-permute-done.5 = bf16[128,1024]{1,0:T(8,128)(2,1)S(1)} collective-permute-done((bf16[128,1024]{1,0:T(8,128)(2,1)}, bf16[128,1024]{1,0:T(8,128)(2,1)S(1)}, u32[]{:S(2)}, u32[]{:S(2)}) %collective-permute-start.5) | collective-permute-done | bytes 262176 | tf_op jit(solution)/shard_map/ppermute | solution.py:807
  22.8 2.5 %pack.1 = bf16[144,1024]{1,0:T(8,128)(2,1)} custom-call(s32[2]{0:T(128)} %pad_add_fusion.places.scalars, bf16[128,512]{1,0:T(8,128)(2,1)} %query.1, bf16[128,512]{1,0:T(8,128)(2,1)} %key.1, bf16[128,1024]{1,0:T(8,128)(2,1)} %value.1, bf16[128,1024]{1,0:T(8,128)(2,1)} %gate.1, bf16[128,1024]{1,0:T(8,128)(2,1)} %proj.1, bf16[4,128]{1,0:T(4,128)(2,1)} %bitcast.37, ...), custom_call_target="tpu_custom_call" | custom-call | flops 100000000 | bytes 1348160 | tf_op jit(solution)/shard_map/pack/pallas_call | solution.py:782
  25.3 3.7 %collective-permute-start.2 = (bf16[144,1024]{1,0:T(8,128)(2,1)}, bf16[144,1024]{1,0:T(8,128)(2,1)S(1)}, u32[]{:S(2)}, u32[]{:S(2)}) collective-permute-start(bf16[144,1024]{1,0:T(8,128)(2,1)} %pack.1), channel_id=1, source_target_pairs={{0,6},{1,7},{2,4},{3,5},{4,2},{5,3},{6,0},{7,1},{8,14},{9,15},{10,... | collective-permute-start | bytes 884744 | tf_op jit(solution)/shard_map/ppermute | solution.py:807
  29.7 7.7 %collective-permute-done.2 = bf16[144,1024]{1,0:T(8,128)(2,1)S(1)} collective-permute-done((bf16[144,1024]{1,0:T(8,128)(2,1)}, bf16[144,1024]{1,0:T(8,128)(2,1)S(1)}, u32[]{:S(2)}, u32[]{:S(2)}) %collective-permute-start.2) | collective-permute-done | bytes 294944 | tf_op jit(solution)/shard_map/ppermute | solution.py:807
  37.4 15.5 %collective-permute-done.1 = bf16[144,1024]{1,0:T(8,128)(2,1)} collective-permute-done((bf16[144,1024]{1,0:T(8,128)(2,1)}, bf16[144,1024]{1,0:T(8,128)(2,1)}, u32[]{:S(2)}, u32[]{:S(2)}) %collective-permute-start.1) | collective-permute-done | bytes 294944 | tf_op jit(solution)/shard_map/ppermute | solution.py:807
  53.7 3.3 %feed_forward_pack.1 = bf16[2176,128]{1,0:T(8,128)(2,1)} custom-call(s32[2]{0:T(128)} %pad_add_fusion.places.scalars, bf16[128,2816]{1,0:T(8,128)(2,1)} %gate_far, bf16[128,2816]{1,0:T(8,128)(2,1)} %up_far.1, bf16[352,1024]{1,0:T(8,128)(2,1)} %down_far.1), custom_call_target="tpu_custom_call" | custom-call | flops 100000000 | bytes 2719744 | tf_op jit(solution)/shard_map/feed_forward_pack/pallas_call | solution.py:782
  61.5 10.3 %mixer_forward.1 = (bf16[512,1024]{1,0:T(8,128)(2,1)S(1)}, f32[512,512]{1,0:T(8,128)S(1)}, f32[512,256]{1,0:T(8,128)S(1)}, f32[512,16]{1,0:T(8,128)S(1)}, f32[51...) custom-call(f32[2]{0:T(128)S(1)} %pad_maximum_fusion.11.scalars, ...), custom_call_target="tpu_custom_call" | custom-call | flops 8000000000 | bytes 9257984 | tf_op jit(solution)/shard_map/mixer_forward/pallas_call | solution.py:782
  73.4 2.5 %collective-permute-start.10 = (bf16[8,128,256]{2,1,0:T(8,128)(2,1)S(1)}, bf16[8,128,256]{2,1,0:T(8,128)(2,1)S(1)}, u32[]{:S(2)}, u32[]{:S(2)}) collective-permute-start(bf16[8,128,256]{2,1,0:T(8,128)(2,1)S(1)} %pad_maximum_fusion.6.refs_0_), channel_id=1, source_target_pairs={{0,24},{8,16},{16,8},{24,0},{1,25},{9,17},{17,9},{25,1},{2,26},{10... | collective-permute-start | bytes 1572872 | tf_op jit(solution)/shard_map/ppermute | solution.py:802
  78.5 3.6 %collective-permute-done.13.refs_10_ = bf16[512,256]{1,0:T(8,128)(2,1)S(1)} collective-permute-done((bf16[512,256]{1,0:T(8,128)(2,1)S(1)}, bf16[512,256]{1,0:T(8,128)(2,1)S(1)}, u32[]{:S(2)}, u32[]{:S(2)}) %collective-permute-start.13) | collective-permute-done | bytes 262176 | tf_op jit(solution)/shard_map/ppermute | solution.py:802
  83.7 25.7 %collective-permute-done.12.refs_9_ = bf16[512,256]{1,0:T(8,128)(2,1)S(1)} collective-permute-done((bf16[512,256]{1,0:T(8,128)(2,1)S(1)}, bf16[512,256]{1,0:T(8,128)(2,1)S(1)}, u32[]{:S(2)}, u32[]{:S(2)}) %collective-permute-start.12) | collective-permute-done | bytes 262176 | tf_op jit(solution)/shard_map/ppermute | solution.py:802
  111.0 16.3 %feed_forward.1 = (bf16[512,1024]{1,0:T(8,128)(2,1)}, f32[128,1024]{1,0:T(8,128)}, bf16[512,1024]{1,0:T(8,128)(2,1)}, f32[1,1024]{1,0:T(1,128)}, bf16[512,1024]{...) custom-call(s32[2]{0:T(128)} %pad_add_fusion.places.scalars, ...), custom_call_target="tpu_custom_call" | custom-call | flops 16000000000 | bytes 19931136 | tf_op jit(solution)/shard_map/feed_forward/pallas_call | solution.py:782
  132.1 5.7 %collective-permute-done.14 = bf16[128,1024]{1,0:T(8,128)(2,1)S(1)} collective-permute-done((bf16[128,1024]{1,0:T(8,128)(2,1)S(1)}, bf16[128,1024]{1,0:T(8,128)(2,1)S(1)}, u32[]{:S(2)}, u32[]{:S(2)}) %collective-permute-start.14) | collective-permute-done | bytes 262176 | tf_op jit(solution)/shard_map/ppermute | solution.py:833
  137.8 4.7 %collective-permute-done.16 = bf16[128,1024]{1,0:T(8,128)(2,1)S(1)} collective-permute-done((bf16[128,1024]{1,0:T(8,128)(2,1)S(1)}, bf16[128,1024]{1,0:T(8,128)(2,1)S(1)}, u32[]{:S(2)}, u32[]{:S(2)}) %collective-permute-start.16) | collective-permute-done | bytes 262176 | tf_op jit(solution)/shard_map/ppermute | solution.py:833
  148.8 6.3 %collective-permute-done.19.refs_3_ = bf16[128,1024]{1,0:T(8,128)(2,1)S(1)} collective-permute-done((bf16[128,1024]{1,0:T(8,128)(2,1)S(1)}, bf16[128,1024]{1,0:T(8,128)(2,1)S(1)}, u32[]{:S(2)}, u32[]{:S(2)}) %collective-permute-start.19) | collective-permute-done | bytes 262176 | tf_op jit(solution)/shard_map/ppermute | solution.py:802
  155.1 2.7 %collective-permute-done.18.refs_2_ = bf16[128,1024]{1,0:T(8,128)(2,1)S(1)} collective-permute-done((bf16[128,1024]{1,0:T(8,128)(2,1)S(1)}, bf16[128,1024]{1,0:T(8,128)(2,1)S(1)}, u32[]{:S(2)}, u32[]{:S(2)}) %collective-permute-start.18) | collective-permute-done | bytes 262176 | tf_op jit(solution)/shard_map/ppermute | solution.py:802
  158.1 14.7 %mixer_backward.1 = (bf16[8,144,1024]{2,1,0:T(8,128)(2,1)}, bf16[512,1024]{1,0:T(8,128)(2,1)S(1)}) custom-call(f32[2]{0:T(128)S(1)} %pad_maximum_fusion.11.scalars, s32[2]{0:T(128)S(1)} %copy-done.5, bf16[128,1024]{1,0:T(8,128)(2,1)S(1)} %get-tuple-element.128.refs_0_, bf16[128,1024]{1,0:T(8,128)(2,1)S(1)} %collective-permute-done.17.refs_1_, ...), custom_call_target="tpu_custom_call" | custom-call | flops 10000000000 | bytes 14234624 | tf_op jit(solution)/shard_map/mixer_backward/pallas_call | solution.py:782
  175.1 3.1 %reduce-scatter.3.cloned.1.call-done = bf16[1,2176,128]{2,1,0:T(8,128)(2,1)} async-done(((bf16[8,2176,128]{2,1,0:T(8,128)(2,1)}), bf16[1,2176,128]{2,1,0:T(8,128)(2,1)}) %reduce-scatter.3.cloned.1.call-update) | async-done | bytes 557072 | tf_op jit(solution)/shard_map/reduce_scatter | solution.py:1063
  185.1 2.7 %collective-permute-done.25.refs_6_ = bf16[1088,128]{1,0:T(8,128)(2,1)S(1)} collective-permute-done((bf16[1088,128]{1,0:T(8,128)(2,1)S(1)}, bf16[1088,128]{1,0:T(8,128)(2,1)S(1)}, u32[]{:S(2)}, u32[]{:S(2)}) %collective-permute-start.25) | collective-permute-done | bytes 278560 | tf_op jit(solution)/shard_map/ppermute | solution.py:807
  187.8 2.4 collective-permute-start.26
  192.6 10.2 %collective-permute-done.23.refs_1_ = bf16[1088,128]{1,0:T(8,128)(2,1)S(1)} collective-permute-done((bf16[1088,128]{1,0:T(8,128)(2,1)S(1)}, bf16[1088,128]{1,0:T(8,128)(2,1)S(1)}, u32[]{:S(2)}, u32[]{:S(2)}) %collective-permute-start.23) | collective-permute-done | bytes 278560 | tf_op jit(solution)/shard_map/ppermute | solution.py:807
  203.5 11.2 %collective-permute-done.26 = bf16[2176,128]{1,0:T(8,128)(2,1)S(1)} collective-permute-done((bf16[2176,128]{1,0:T(8,128)(2,1)S(1)}, bf16[2176,128]{1,0:T(8,128)(2,1)S(1)}, u32[]{:S(2)}, u32[]{:S(2)}) %collective-permute-start.26) | collective-permute-done | bytes 557088 | tf_op jit(solution)/shard_map/ppermute | solution.py:807
  214.7 13.2 %collective-permute-done.24 = bf16[2176,128]{1,0:T(8,128)(2,1)S(1)} collective-permute-done((bf16[2176,128]{1,0:T(8,128)(2,1)S(1)}, bf16[2176,128]{1,0:T(8,128)(2,1)S(1)}, u32[]{:S(2)}, u32[]{:S(2)}) %collective-permute-start.24) | collective-permute-done | bytes 557088 | tf_op jit(solution)/shard_map/ppermute | solution.py:807
  233.5 3.2 %feed_forward_finish.1 = (f32[128,2816]{1,0:T(8,128)}, f32[128,2816]{1,0:T(8,128)}, f32[352,1024]{1,0:T(8,128)}) custom-call(s32[2]{0:T(128)S(1)} %copy-done.5, bf16[1088,128]{1,0:T(8,128)(2,1)S(1)} %get-tuple-element.146.refs_0_, bf16[1088,128]{1,0:T(8,128)(2,1)S(1)} %collective-permute-done.23.refs_1_, bf16[1088,128]{1,0:T(8,128)(2,1)S(1)} %get-tuple-element.148.refs_2_, ...), custom_call_target="tpu_custom_call" | custom-call | flops 100000000 | bytes 6553600 | tf_op jit(solution)/shard_map/feed_forward_finish/pallas_call | solution.py:782
  (172 shorter events, 53.2 us)
Async XLA Ops:
  7.2 103.0 %all-gather.3.cloned.1.call-start = ((), (), s32[]{:S(2)}) async-start(), calls=%async_computation.4 | async-start | bytes 5013504 | tf_op jit(solution)/shard_map/all_gather | solution.py:956
  17.8 35.2 %collective-permute-start.6 = (bf16[256,1024]{1,0:T(8,128)(2,1)S(1)}, bf16[256,1024]{1,0:T(8,128)(2,1)S(1)}, u32[]{:S(2)}, u32[]{:S(2)}) collective-permute-start(bf16[256,1024]{1,0:T(8,128)(2,1)S(1)} %pad_maximum_fusion.5), channel_id=1, source_target_pairs={{0,8},{8,0},{16,24},{24,16},{1,9},{9,1},{17,25},{25,17},{2,10},{10... | collective-permute-start | bytes 1572872 | tf_op jit(solution)/shard_map/ppermute | solution.py:807
  20.6 33.1 %collective-permute-start.4 = (bf16[256,1024]{1,0:T(8,128)(2,1)S(1)}, bf16[256,1024]{1,0:T(8,128)(2,1)S(1)}, u32[]{:S(2)}, u32[]{:S(2)}) collective-permute-start(bf16[256,1024]{1,0:T(8,128)(2,1)S(1)} %pad_maximum_fusion.4), channel_id=1, source_target_pairs={{0,16},{8,24},{16,0},{24,8},{1,17},{9,25},{17,1},{25,9},{2,18},{10... | collective-permute-start | bytes 1572872 | tf_op jit(solution)/shard_map/ppermute | solution.py:807
  25.3 12.1 %collective-permute-start.2 = (bf16[144,1024]{1,0:T(8,128)(2,1)}, bf16[144,1024]{1,0:T(8,128)(2,1)S(1)}, u32[]{:S(2)}, u32[]{:S(2)}) collective-permute-start(bf16[144,1024]{1,0:T(8,128)(2,1)} %pack.1), channel_id=1, source_target_pairs={{0,6},{1,7},{2,4},{3,5},{4,2},{5,3},{6,0},{7,1},{8,14},{9,15},{10,... | collective-permute-start | bytes 884744 | tf_op jit(solution)/shard_map/ppermute | solution.py:807
  29.0 24.0 %collective-permute-start.1 = (bf16[144,1024]{1,0:T(8,128)(2,1)}, bf16[144,1024]{1,0:T(8,128)(2,1)}, u32[]{:S(2)}, u32[]{:S(2)}) collective-permute-start(bf16[144,1024]{1,0:T(8,128)(2,1)} %pack.1), channel_id=1, source_target_pairs={{0,4},{1,5},{2,6},{3,7},{4,0},{5,1},{6,2},{7,3},{8,12},{9,13},{10,... | collective-permute-start | bytes 884744 | tf_op jit(solution)/shard_map/ppermute | solution.py:807
  29.0 24.0 %collective-permute-start = (bf16[144,1024]{1,0:T(8,128)(2,1)}, bf16[144,1024]{1,0:T(8,128)(2,1)S(1)}, u32[]{:S(2)}, u32[]{:S(2)}) collective-permute-start(bf16[144,1024]{1,0:T(8,128)(2,1)} %pack.1), channel_id=1, source_target_pairs={{0,2},{1,3},{2,0},{3,1},{4,6},{5,7},{6,4},{7,5},{8,10},{9,11},{10,... | collective-permute-start | bytes 884744 | tf_op jit(solution)/shard_map/ppermute | solution.py:807
  57.1 121.1 %reduce-scatter.3.cloned.1.call-start = ((), (), s32[]{:S(2)}) async-start(), calls=%async_computation.2 | async-start | bytes 5013504 | tf_op jit(solution)/shard_map/reduce_scatter | solution.py:1063
  73.4 36.0 %collective-permute-start.10 = (bf16[8,128,256]{2,1,0:T(8,128)(2,1)S(1)}, bf16[8,128,256]{2,1,0:T(8,128)(2,1)S(1)}, u32[]{:S(2)}, u32[]{:S(2)}) collective-permute-start(bf16[8,128,256]{2,1,0:T(8,128)(2,1)S(1)} %pad_maximum_fusion.6.refs_0_), channel_id=1, source_target_pairs={{0,24},{8,16},{16,8},{24,0},{1,25},{9,17},{17,9},{25,1},{2,26},{10... | collective-permute-start | bytes 1572872 | tf_op jit(solution)/shard_map/ppermute | solution.py:802
  76.0 33.5 %collective-permute-start.9 = (bf16[8,128,256]{2,1,0:T(8,128)(2,1)S(1)}, bf16[8,128,256]{2,1,0:T(8,128)(2,1)S(1)}, u32[]{:S(2)}, u32[]{:S(2)}) collective-permute-start(bf16[8,128,256]{2,1,0:T(8,128)(2,1)S(1)} %pad_maximum_fusion.6.refs_0_), channel_id=1, source_target_pairs={{0,16},{8,24},{16,0},{24,8},{1,17},{9,25},{17,1},{25,9},{2,18},{10... | collective-permute-start | bytes 1572872 | tf_op jit(solution)/shard_map/ppermute | solution.py:802
  76.4 33.8 %collective-permute-start.8 = (bf16[8,128,256]{2,1,0:T(8,128)(2,1)S(1)}, bf16[8,128,256]{2,1,0:T(8,128)(2,1)}, u32[]{:S(2)}, u32[]{:S(2)}) collective-permute-start(bf16[8,128,256]{2,1,0:T(8,128)(2,1)S(1)} %pad_maximum_fusion.6.refs_0_), channel_id=1, source_target_pairs={{0,8},{8,0},{16,24},{24,16},{1,9},{9,1},{17,25},{25,17},{2,10},{10... | collective-permute-start | bytes 1572872 | tf_op jit(solution)/shard_map/ppermute | solution.py:802
  77.0 32.4 %collective-permute-start.12 = (bf16[512,256]{1,0:T(8,128)(2,1)S(1)}, bf16[512,256]{1,0:T(8,128)(2,1)S(1)}, u32[]{:S(2)}, u32[]{:S(2)}) collective-permute-start(bf16[512,256]{1,0:T(8,128)(2,1)S(1)} %get-tuple-element.76.refs_7_), channel_id=1, source_target_pairs={{0,16},{8,24},{16,0},{24,8},{1,17},{9,25},{17,1},{25,9},{2,18},{10... | collective-permute-start | bytes 786440 | tf_op jit(solution)/shard_map/ppermute | solution.py:802
  82.1 27.4 %collective-permute-start.11 = (bf16[512,256]{1,0:T(8,128)(2,1)S(1)}, bf16[512,256]{1,0:T(8,128)(2,1)S(1)}, u32[]{:S(2)}, u32[]{:S(2)}) collective-permute-start(bf16[512,256]{1,0:T(8,128)(2,1)S(1)} %get-tuple-element.76.refs_7_), channel_id=1, source_target_pairs={{0,8},{8,0},{16,24},{24,16},{1,9},{9,1},{17,25},{25,17},{2,10},{10... | collective-permute-start | bytes 786440 | tf_op jit(solution)/shard_map/ppermute | solution.py:802
  127.4 100.7 %reduce-scatter.5.cloned.1.call-start = ((), (), s32[]{:S(2)}) async-start(), calls=%async_computation.3 | async-start | bytes 2654208 | tf_op jit(solution)/shard_map/reduce_scatter | solution.py:1109
  129.2 13.3 %collective-permute-start.16 = (bf16[128,1024]{1,0:T(8,128)(2,1)S(1)}, bf16[128,1024]{1,0:T(8,128)(2,1)S(1)}, u32[]{:S(2)}, u32[]{:S(2)}) collective-permute-start(bf16[128,1024]{1,0:T(8,128)(2,1)S(1)} %get-tuple-element.141), channel_id=1, source_target_pairs={{0,24},{8,16},{16,8},{24,0},{1,25},{9,17},{17,9},{25,1},{2,26},{10... | collective-permute-start | bytes 786440 | tf_op jit(solution)/shard_map/ppermute | solution.py:833
  130.6 13.2 %collective-permute-start.15 = (bf16[128,1024]{1,0:T(8,128)(2,1)S(1)}, bf16[128,1024]{1,0:T(8,128)(2,1)S(1)}, u32[]{:S(2)}, u32[]{:S(2)}) collective-permute-start(bf16[128,1024]{1,0:T(8,128)(2,1)S(1)} %get-tuple-element.142), channel_id=1, source_target_pairs={{0,16},{8,24},{16,0},{24,8},{1,17},{9,25},{17,1},{25,9},{2,18},{10... | collective-permute-start | bytes 786440 | tf_op jit(solution)/shard_map/ppermute | solution.py:833
  146.8 11.0 %collective-permute-start.18 = (bf16[128,1024]{1,0:T(8,128)(2,1)S(1)}, bf16[128,1024]{1,0:T(8,128)(2,1)S(1)}, u32[]{:S(2)}, u32[]{:S(2)}) collective-permute-start(bf16[128,1024]{1,0:T(8,128)(2,1)S(1)} %get-tuple-element.128.refs_0_), channel_id=1, source_target_pairs={{0,16},{8,24},{16,0},{24,8},{1,17},{9,25},{17,1},{25,9},{2,18},{10... | collective-permute-start | bytes 786440 | tf_op jit(solution)/shard_map/ppermute | solution.py:802
  147.2 10.9 %collective-permute-start.17 = (bf16[128,1024]{1,0:T(8,128)(2,1)S(1)}, bf16[128,1024]{1,0:T(8,128)(2,1)S(1)}, u32[]{:S(2)}, u32[]{:S(2)}) collective-permute-start(bf16[128,1024]{1,0:T(8,128)(2,1)S(1)} %get-tuple-element.128.refs_0_), channel_id=1, source_target_pairs={{0,8},{8,0},{16,24},{24,16},{1,9},{9,1},{17,25},{25,17},{2,10},{10... | collective-permute-start | bytes 786440 | tf_op jit(solution)/shard_map/ppermute | solution.py:802
  181.7 49.3 %collective-permute-start.20 = (bf16[256,1024]{1,0:T(8,128)(2,1)}, bf16[256,1024]{1,0:T(8,128)(2,1)}, u32[]{:S(2)}, u32[]{:S(2)}) collective-permute-start(bf16[256,1024]{1,0:T(8,128)(2,1)} %pad_maximum_fusion.8), channel_id=1, source_target_pairs={{0,8},{8,0},{16,24},{24,16},{1,9},{9,1},{17,25},{25,17},{2,10},{10... | collective-permute-start | bytes 1572872 | tf_op jit(solution)/shard_map/ppermute | solution.py:833
  184.0 47.6 %collective-permute-start.21 = (bf16[256,1024]{1,0:T(8,128)(2,1)}, bf16[256,1024]{1,0:T(8,128)(2,1)}, u32[]{:S(2)}, u32[]{:S(2)}) collective-permute-start(bf16[256,1024]{1,0:T(8,128)(2,1)} %pad_maximum_fusion.9), channel_id=1, source_target_pairs={{0,16},{8,24},{16,0},{24,8},{1,17},{9,25},{17,1},{25,9},{2,18},{10... | collective-permute-start | bytes 1572872 | tf_op jit(solution)/shard_map/ppermute | solution.py:833
  184.6 18.2 %collective-permute-start.23 = (bf16[1088,128]{1,0:T(8,128)(2,1)S(1)}, bf16[1088,128]{1,0:T(8,128)(2,1)S(1)}, u32[]{:S(2)}, u32[]{:S(2)}) collective-permute-start(bf16[1088,128]{1,0:T(8,128)(2,1)S(1)} %get-tuple-element.146.refs_0_), channel_id=1, source_target_pairs={{0,8},{8,0},{16,24},{24,16},{1,9},{9,1},{17,25},{25,17},{2,10},{10... | collective-permute-start | bytes 835592 | tf_op jit(solution)/shard_map/ppermute | solution.py:807
  187.8 26.9 %collective-permute-start.26 = (bf16[2176,128]{1,0:T(8,128)(2,1)S(1)}, bf16[2176,128]{1,0:T(8,128)(2,1)S(1)}, u32[]{:S(2)}, u32[]{:S(2)}) collective-permute-start(bf16[2176,128]{1,0:T(8,128)(2,1)S(1)} %pad_maximum_fusion.3), channel_id=1, source_target_pairs={{0,8},{8,0},{16,24},{24,16},{1,9},{9,1},{17,25},{25,17},{2,10},{10... | collective-permute-start | bytes 1671176 | tf_op jit(solution)/shard_map/ppermute | solution.py:807
  191.1 40.5 %collective-permute-start.22 = (bf16[256,1024]{1,0:T(8,128)(2,1)}, bf16[256,1024]{1,0:T(8,128)(2,1)}, u32[]{:S(2)}, u32[]{:S(2)}) collective-permute-start(bf16[256,1024]{1,0:T(8,128)(2,1)} %pad_maximum_fusion.10), channel_id=1, source_target_pairs={{0,24},{8,16},{16,8},{24,0},{1,25},{9,17},{17,9},{25,1},{2,26},{10... | collective-permute-start | bytes 1572872 | tf_op jit(solution)/shard_map/ppermute | solution.py:833
  202.8 25.2 %collective-permute-start.24 = (bf16[2176,128]{1,0:T(8,128)(2,1)S(1)}, bf16[2176,128]{1,0:T(8,128)(2,1)S(1)}, u32[]{:S(2)}, u32[]{:S(2)}) collective-permute-start(bf16[2176,128]{1,0:T(8,128)(2,1)S(1)} %pad_maximum_fusion.2), channel_id=1, source_target_pairs={{0,16},{8,24},{16,0},{24,8},{1,17},{9,25},{17,1},{25,9},{2,18},{10... | collective-permute-start | bytes 1671176 | tf_op jit(solution)/shard_map/ppermute | solution.py:807
  228.6 10.5 %collective-permute-start.28 = (bf16[144,1024]{1,0:T(8,128)(2,1)}, bf16[144,1024]{1,0:T(8,128)(2,1)S(1)}, u32[]{:S(2)}, u32[]{:S(2)}) collective-permute-start(bf16[144,1024]{1,0:T(8,128)(2,1)} %bitcast.27), channel_id=1, source_target_pairs={{0,16},{8,24},{16,0},{24,8},{1,17},{9,25},{17,1},{25,9},{2,18},{10... | collective-permute-start | bytes 884744 | tf_op jit(solution)/shard_map/ppermute | solution.py:802
  (52 other events, 470.6 us)
Sparse Core Ops, SparseCore 0:
  57.2 47.7 all-gather.2
  127.5 50.6 reduce-scatter.2
  180.5 34.5 reduce-scatter.4

commit v2 on v1

--- a/solution.py
+++ b/solution.py
@@ -286,30 +286,40 @@
     scalars,
     *refs,
 ):
-    far_out, far = refs[:team], refs[team : team + 3]
-    mixed_slots, gain = refs[team + 3 : 2 * team + 3], refs[2 * team + 3]
+    outs_count = team
+    far = refs[: outs_count + 3]
+    refs = refs[outs_count + 3 :]
+    mixed_slots, gain = refs[:team], refs[team]
+    far_outs, gain_grad_out = refs[team + 1 : team + 7], refs[team + 7]
     (
-        mixed_out,
-        hidden_out,
-        second_grad_out,
-        gain_grad_out,
-        result_out,
+        mixed,
         out_full,
-        grads_out,
+        result,
+        second_grad_low,
+        grads,
         hidden,
         up_weights,
         down_weights,
         *near,
         sems,
-    ) = refs[2 * team + 4 :]
+        out_sems,
+    ) = refs[team + 8 :]
+    mixed_out, hidden_out, second_grad_out, result_out, out_rows_out, grads_out = far_outs
     fetch = [
         pltpu.make_async_copy(source, target, sems.at[index])
-        for index, (source, target) in enumerate(zip((*far_out, *far), near))
+        for index, (source, target) in enumerate(zip(far, near))
     ]
     for copy in fetch:
         copy.start()
-    out_slots = near[:team]
-    tokens, packs, cotangents = near[team:]
+    sent = []
+
+    def send(source, target):
+        copy = pltpu.make_async_copy(source, target, out_sems.at[len(sent)])
+        copy.start()
+        sent.append(copy)
+
+    out_slots = near[:outs_count]
+    tokens, packs, cotangents = near[outs_count:]
     part = scalars[0]
     size = tokens.shape[0] // team
     values = mixed_slots[0].shape[1]
@@ -318,43 +328,78 @@
         place = pl.multiple_of(member(part, steps) * values, values)
         for slot in range(team):
             there = slot ^ steps
-            mixed_out[slot * size : (slot + 1) * size, pl.ds(place, values)] = mixed_slots[
-                steps
-            ][there * size : (there + 1) * size]
-    blocks = out_slots[0].shape[0]
-    chunk = out_slots[0].shape[1]
-    for copy in fetch[: team + 1]:
+            mixed[slot * size : (slot + 1) * size, pl.ds(place, values)] = mixed_slots[steps][
+                there * size : (there + 1) * size
+            ]
+    send(mixed, mixed_out)
+    chips, chunk = out_slots[0].shape[0] // 2, out_slots[0].shape[1]
+    for copy in fetch[: outs_count + 1]:
         copy.wait()
-    for steps in range(team):
-        place = pl.multiple_of(member(part, steps) * outs, outs)
-        for slot in range(blocks):
-            chips = blocks // 2
+    for index in range(outs_count):
+        place = pl.multiple_of(member(part, index) * outs, outs)
+        for slot in range(2 * chips):
             shard = slot_shard(scalars, slot % chips, slot < chips)
             line = pl.ds(pl.multiple_of(shard * chunk, chunk), chunk)
-            out_full[line, pl.ds(place, outs)] = out_slots[steps][slot]
-    wide = tokens[...].astype(WIDE) + local_dot(mixed_out[...], out_full[...])
-    hidden_out[...] = wide[:size]
+            out_full[line, pl.ds(place, outs)] = out_slots[index][slot]
+    row = pl.multiple_of(part * values, values)
+    send(out_full.at[pl.ds(row, values)], out_rows_out)
+    hidden[...] = tokens[...].astype(WIDE) + local_dot(mixed[...], out_full[...])
+    send(hidden.at[:size], hidden_out)
+    wide = hidden[...]
     normed = wide * lax.rsqrt(jnp.mean(wide * wide, -1, keepdims=True) + EPS)
     second = (normed * gain[...]).astype(LOW)
-    hidden[...] = normed
-    fetch[team + 1].wait()
+    fetch[outs_count + 1].wait()
     feed_forward_unpack(packs.shape[0], packs, up_weights, down_weights)
-    fetch[team + 2].wait()
+    fetch[outs_count + 2].wait()
     part_width = down_weights.shape[0]
     both = local_dot(second, up_weights[...])
     gate, up = both[:, :part_width], both[:, part_width:]
     gate_sig = sigmoid(gate)
     gate_act = gate * gate_sig
     active = (gate_act * up).astype(LOW)
-    result_out[...] = local_dot(active, down_weights[...]).astype(LOW)
+    result[...] = local_dot(active, down_weights[...]).astype(LOW)
+    send(result, result_out)
     active_grad = right_dot(cotangents[...], down_weights[...])
     gate_back = (active_grad * up * gate_sig * (1.0 + gate * (1.0 - gate_sig))).astype(LOW)
     up_back = (active_grad * gate_act).astype(LOW)
     back = jnp.concatenate([gate_back, up_back], 1)
     second_grad = right_dot(back, up_weights[...])
-    second_grad_out[...] = second_grad.astype(LOW)
-    gain_grad_out[...] = jnp.sum(second_grad * hidden[...], 0, keepdims=True)
-    feed_forward_pack_grads(grads_out.shape[0], second, back, active, cotangents[...], grads_out)
+    second_grad_low[...] = second_grad.astype(LOW)
+    send(second_grad_low, second_grad_out)
+    wide = hidden[...]
+    normed = wide * lax.rsqrt(jnp.mean(wide * wide, -1, keepdims=True) + EPS)
+    gain_grad_out[...] = jnp.sum(second_grad * normed, 0, keepdims=True)
+    shards = grads.shape[0]
+    chunk = out_full.shape[0] // shards
+    each = part_width // shards
+    ups = back.shape[1] // LANES
+    down_grad = left_dot(active, cotangents[...])
+    for shard in range(shards):
+        for index in range(down_grad.shape[1] // (2 * LANES)):
+            start = ups * chunk + 2 * index * each
+            grads[shard, start : start + 2 * each] = on_end(
+                down_grad[shard * each : (shard + 1) * each], index
+            ).astype(LOW)
+    half = shards // 2
+    for first_shard in (0, half):
+        line = slice(first_shard * chunk, (first_shard + half) * chunk)
+        up_grad = left_dot(second[:, line], back)
+        for shard in range(half):
+            for index in range(ups):
+                grads[first_shard + shard, index * chunk : (index + 1) * chunk] = up_grad[
+                    shard * chunk : (shard + 1) * chunk, index * LANES : (index + 1) * LANES
+                ].astype(LOW)
+        place = pl.ds(first_shard, half)
+        send(grads.at[place], grads_out.at[place])
+    for copy in sent:
+        copy.wait()
+
+
+def on_end(rows, index):
+    start = 2 * index * LANES
+    return jnp.concatenate(
+        [rows[:, start : start + LANES], rows[:, start + LANES : start + 2 * LANES]], 0
+    )
 
 
 def feed_forward_pack_kernel(team, shards, places, gate_far, up_far, down_far, pack, gate, up, down, sems):
@@ -366,9 +411,7 @@
         copy.start()
     chunk = gate.shape[0]
     each = down.shape[0] // team
-    padded = -(-each // ROWS16) * ROWS16
     ups = 2 * shards * each // LANES
-    pad = jnp.zeros((padded - each, LANES), WIDE)
     for copy in fetch:
         copy.wait()
 
@@ -386,16 +429,14 @@
                     :, index * LANES : (index + 1) * LANES
                 ].astype(LOW)
             rows = down[...].astype(WIDE)[choice * each : (choice + 1) * each]
-            for index in range(rows.shape[1] // LANES):
-                start = ups * chunk + index * padded
-                block = rows[:, index * LANES : (index + 1) * LANES]
-                pack[start : start + padded] = jnp.concatenate([block, pad], 0).astype(LOW)
+            for index in range(rows.shape[1] // (2 * LANES)):
+                start = ups * chunk + 2 * index * each
+                pack[start : start + 2 * each] = on_end(rows, index).astype(LOW)
 
 
 def feed_forward_unpack(shards, packs, up_out, down_out):
     chunk = up_out.shape[0] // shards
     each = down_out.shape[0] // shards
-    padded = -(-each // ROWS16) * ROWS16
     ups = up_out.shape[1] // LANES
     for shard in range(shards):
         for index in range(ups):
@@ -403,46 +444,24 @@
                 packs[shard, index * chunk : (index + 1) * chunk]
             )
     for pair in range(shards // 2):
-        for index in range(down_out.shape[1] // LANES):
-            start = ups * chunk + index * padded
-            block = jnp.concatenate(
-                [
-                    packs[shard, start : start + padded].astype(WIDE)[:each]
-                    for shard in (2 * pair, 2 * pair + 1)
-                ],
-                0,
+        for index in range(down_out.shape[1] // (2 * LANES)):
+            start = ups * chunk + 2 * index * each
+            even, odd = (
+                packs[shard, start : start + 2 * each].astype(WIDE)
+                for shard in (2 * pair, 2 * pair + 1)
             )
-            down_out[
-                2 * pair * each : 2 * (pair + 1) * each, index * LANES : (index + 1) * LANES
-            ] = block.astype(LOW)
-
-
-def feed_forward_pack_grads(shards, second, back, active, cotangents, pack):
-    up_grad = left_dot(second, back)
-    down_grad = left_dot(active, cotangents)
-    chunk = up_grad.shape[0] // shards
-    each = down_grad.shape[0] // shards
-    padded = -(-each // ROWS16) * ROWS16
-    pad = jnp.zeros((padded - each, LANES), WIDE)
-    ups = up_grad.shape[1] // LANES
-    for shard in range(shards):
-        for index in range(ups):
-            pack[shard, index * chunk : (index + 1) * chunk] = up_grad[
-                shard * chunk : (shard + 1) * chunk, index * LANES : (index + 1) * LANES
-            ].astype(LOW)
-        for index in range(down_grad.shape[1] // LANES):
-            start = ups * chunk + index * padded
-            block = down_grad[
-                shard * each : (shard + 1) * each, index * LANES : (index + 1) * LANES
-            ]
-            pack[shard, start : start + padded] = jnp.concatenate([block, pad], 0).astype(LOW)
+            for side in range(2):
+                lane = (2 * index + side) * LANES
+                line = slice(side * each, (side + 1) * each)
+                down_out[2 * pair * each : 2 * (pair + 1) * each, lane : lane + LANES] = (
+                    jnp.concatenate([even[line], odd[line]], 0).astype(LOW)
+                )
 
 
 def feed_forward_finish_kernel(team, shards, places, *refs):
     *slots, gate_out, up_out, down_out, ordered = refs
     chunk = gate_out.shape[0]
     each = down_out.shape[0] // team
-    padded = -(-each // ROWS16) * ROWS16
     half = shards * each
     ups = 2 * half // LANES
     size = slots[0].shape[0]
@@ -465,11 +484,14 @@
             1,
         )
     for h in range(team):
-        for index in range(down_out.shape[1] // LANES):
-            start = ups * chunk + index * padded
-            down_out[h * each : (h + 1) * each, index * LANES : (index + 1) * LANES] = ordered[
-                h, start : start + padded
-            ].astype(WIDE)[:each]
+        for index in range(down_out.shape[1] // (2 * LANES)):
+            start = ups * chunk + 2 * index * each
+            both = ordered[h, start : start + 2 * each].astype(WIDE)
+            for side in range(2):
+                lane = (2 * index + side) * LANES
+                down_out[h * each : (h + 1) * each, lane : lane + LANES] = both[
+                    side * each : (side + 1) * each
+                ]
 
 
 def mixer_backward_kernel(
@@ -482,7 +504,7 @@
 ):
     branch_slots = refs[:seqs]
     (
-        out_full,
+        out_rows,
         gate_raw,
         heads,
         head_gain,
@@ -505,12 +527,11 @@
         heads_grad,
     ) = refs[seqs:]
     values = heads.shape[1]
-    outs = out_full.shape[1] // seqs
+    outs = out_rows.shape[1] // seqs
     for slot in range(seqs):
         rows_each = branch_slots[slot].shape[0]
         branch_grad[slot * rows_each : (slot + 1) * rows_each] = branch_slots[slot][...]
-    row = pl.multiple_of(places[0] * values, values)
-    mixed_grad = right_dot(branch_grad[...], out_full[pl.ds(row, values)])
+    mixed_grad = right_dot(branch_grad[...], out_rows[...])
     out = heads[...]
     gate = gate_raw[...]
     gain = head_gain[...]
@@ -776,7 +797,7 @@
     return jax.ShapeDtypeStruct(shape, dtype)
 
 
-def run_kernel(kernel, name, scalars, operands, outs, flops, scratch=(), far=0):
+def run_kernel(kernel, name, scalars, operands, outs, flops, scratch=(), far=0, far_outs=0):
     spec = pl.BlockSpec(memory_space=pltpu.VMEM)
     moved = sum(math.prod(v.shape) * v.dtype.itemsize for v in (*operands, *outs))
     return pl.pallas_call(
@@ -785,7 +806,8 @@
         in_specs=[pl.BlockSpec(memory_space=pltpu.SMEM)] * len(scalars)
         + [pl.BlockSpec(memory_space=pl.ANY)] * far
         + [spec] * (len(operands) - far),
-        out_specs=[spec] * len(outs),
+        out_specs=[pl.BlockSpec(memory_space=pl.ANY)] * far_outs
+        + [spec] * (len(outs) - far_outs),
         scratch_shapes=list(scratch),
         compiler_params=pltpu.CompilerParams(vmem_limit_bytes=(60 if far else 48) * 1024 * 1024),
         cost_estimate=pl.CostEstimate(flops=flops, bytes_accessed=moved, transcendentals=0),
@@ -813,15 +835,17 @@
     ]
 
 
+def doubled(block, devices, near, far):
+    size = block.shape[0]
+    pair = swap(block, "rep", devices, near)
+    quad = swap(both_ends(block, pair), "rep", devices, far)
+    held = {0: block, near: pair, far: quad[:size], near | far: quad[size:]}
+    return [held[e] for e in range(4)]
+
+
 def team_halves(block, devices):
     half = block.shape[0] // 2
-    found = []
-    for part, (near, far) in ((block[:half], (1, 2)), (block[half:], (2, 1))):
-        pair = swap(part, "rep", devices, near)
-        quad = swap(both_ends(part, pair), "rep", devices, far)
-        held = {0: part, near: pair, far: quad[:half], near | far: quad[half:]}
-        found.append([held[e] for e in range(4)])
-    return found[0] + found[1]
+    return doubled(block[:half], devices, 1, 2) + doubled(block[half:], devices, 2, 1)
 
 
 def both_ends(block, moved):
@@ -901,8 +925,7 @@
     key_each, value_each = query_conv.shape[1], value_conv.shape[1]
     head_each = head_gain.shape[0]
 
-    padded = -(-hidden_each // ROWS16) * ROWS16
-    ffn_rows = 2 * hidden_part * chunk // LANES + padded * (width // LANES)
+    ffn_rows = 2 * hidden_part * chunk // LANES + hidden_each * (width // LANES)
 
     mixer_pack = run_kernel(
         functools.partial(pack_kernel, team),
@@ -931,18 +954,23 @@
         5,
     )[0]
     pack_slots = line_gather(mixer_pack, shards)
-    token_pair = swap(inputs, "rep", devices, 1)
+    member_index = lax.axis_index("rep")
+    gathered = lax.all_gather(inputs, "rep", axis=0)
+    tokens = jnp.concatenate(
+        [
+            lax.dynamic_index_in_dim(gathered, member_index ^ e, 0, keepdims=False)
+            for e in range(team)
+        ],
+        0,
+    )
     cotangent_pair = swap(cotangent, "rep", devices, 2)
-    token_pair = both_ends(inputs, token_pair)
+    pack_slots = after(pack_slots, cotangent_pair)
     cotangent_pair = both_ends(cotangent, cotangent_pair)
-    token_quad = swap(token_pair, "rep", devices, 2)
-    cotangent_quad = swap(cotangent_pair, "rep", devices, 1)
-    pack_slots = after(pack_slots, (token_quad, cotangent_quad))
     ffn_pack = run_kernel(
         functools.partial(feed_forward_pack_kernel, team, shards),
         "feed_forward_pack",
         (places,),
-        (after(ffn_gate, pack_slots), ffn_up, ffn_down),
+        (after(ffn_gate, mixer_pack), ffn_up, ffn_down),
         (array((ffn_rows, LANES), LOW),),
         10**8,
         (
@@ -953,10 +981,11 @@
         ),
         3,
     )[0]
-    ffn_packs = lax.all_gather(ffn_pack, "shard", axis=0)
+    ffn_packs = lax.all_gather(after(ffn_pack, pack_slots), "shard", axis=0)
     pack_mine = jnp.stack(pack_slots)
     pack_theirs = swap(pack_mine, "shard", shards, 1)
-    tokens = both_ends(token_pair, token_quad)
+    cotangent_quad = swap(after(cotangent_pair, pack_slots), "rep", devices, 1)
+    tokens = after(tokens, cotangent_quad)
     cotangents = jnp.concatenate(
         [
             cotangent,
@@ -1012,22 +1041,22 @@
         8 * 10**9,
         (pltpu.VMEM((ROWS16, width), WIDE),),
     )
-    mixed_slots = team_gather(mixed_part, devices, team)
     proj_all = both_ends(
         pack_mine[:, :chunk, conv_width + values :],
         pack_theirs[:, :chunk, conv_width + values :],
     )
-    proj_all = after(proj_all, mixed_part)
     proj_slots = team_gather(proj_all, devices, team)
+    mixed_part = after(mixed_part, proj_slots)
+    mixed_slots = team_gather(mixed_part, devices, team)
 
     (
         mixed,
         hidden_own,
         second_part,
+        result_part,
+        out_rows,
+        ffn_grads,
         ffn_gain_part,
-        result_part,
-        out_full,
-        ffn_grads,
     ) = run_kernel(
         functools.partial(feed_forward_kernel, team),
         "feed_forward",
@@ -1037,13 +1066,18 @@
             array((count, width), LOW),
             array((tokens_each, width), WIDE),
             array((count, width), LOW),
+            array((count, width), LOW),
+            array((values, width), LOW),
+            array((shards, ffn_rows, LANES), LOW),
             array((1, width), WIDE),
-            array((count, width), LOW),
-            array((width, width), LOW),
-            array((shards, ffn_rows, LANES), LOW),
         ),
         16 * 10**9,
         (
+            pltpu.VMEM((count, width), LOW),
+            pltpu.VMEM((width, width), LOW),
+            pltpu.VMEM((count, width), LOW),
+            pltpu.VMEM((count, width), LOW),
+            pltpu.VMEM((shards, ffn_rows, LANES), LOW),
             pltpu.VMEM((count, width), WIDE),
             pltpu.VMEM((width, 2 * hidden_part), LOW),
             pltpu.VMEM((hidden_part, width), LOW),
@@ -1052,8 +1086,10 @@
             pltpu.VMEM(ffn_packs.shape, LOW),
             pltpu.VMEM(cotangents.shape, LOW),
             pltpu.SemaphoreType.DMA((team + 3,)),
+            pltpu.SemaphoreType.DMA((7,)),
         ),
         team + 3,
+        6,
     )
 
     def slots_of(v):
@@ -1072,13 +1108,16 @@
     branch_slots = team_gather(hidden_grad.astype(LOW), devices, team)
 
 
+    result_part = after(result_part, branch_slots)
+    result_slots = team_send(slots_of(result_part), devices, team)
+
     head_grads, first_part = run_kernel(
         functools.partial(mixer_backward_kernel, team, keys, shards),
         "mixer_backward",
         (scalars, places),
         (
             *branch_slots,
-            out_full,
+            out_rows,
             gate_raw,
             heads,
             head_row,
@@ -1106,17 +1145,14 @@
             pltpu.VMEM((count, values), WIDE),
         ),
     )
+    head_grads = after(head_grads, result_slots)
     head_shard = lax.psum_scatter(head_grads, "shard", scatter_dimension=0)
-    last_slots = [
-        jnp.concatenate(pair, 0) for pair in zip(slots_of(first_part), slots_of(result_part))
-    ]
-    last_slots = team_send(last_slots, devices, team)
+    first_slots = team_send(slots_of(first_part), devices, team)
     if devices == team == 4:
         ffn_totals = team_halves(ffn_shard, devices)
     else:
         ffn_totals = replica_slots(ffn_shard, part, devices, team)
-    last = wide_sum(after(last_slots, ffn_totals))
-    first_grad = last[:tokens_each]
+    first_grad = wide_sum(after(first_slots, ffn_totals))
     seq_in = inputs.astype(WIDE)
     seq_scale = norm_scale(seq_in)
     weighted = first_grad * mix_row
@@ -1124,7 +1160,7 @@
         weighted
         - seq_in * (seq_scale * seq_scale * jnp.mean(seq_in * weighted, -1, keepdims=True))
     )
-    result = hidden_own + last[tokens_each:]
+    result = hidden_own + wide_sum(result_slots)
 
     head_totals = replica_slots(after(head_shard, ffn_totals), part, devices, team)
     gate_grads, up_grads, down_grads = run_kernel(

time: 250 us -> 222 us (0.89)
  waiting for transfers between devices: 120 us -> 99.8 us
  other arithmetic: 12.6 us -> 7.3 us
    ppermute x12 -> x10, waiting for transfers between devices: 65.6 us -> 44.7 us  [swap(): return lax.ppermute(block, name, [(j, j ^ mask) for j in range(size)])]
    ppermute x6 -> x9, starting transfers between devices: 7.08 us -> 10.6 us  [team_send(): lax.ppermute(slots[steps], 'rep', team_pairs(devices, steps))]
    unnamed x88 -> x66, local copies, waits for them, and re-layouts: 4.81 us -> 1.98 us
    reduce_scatter x1, waiting for transfers between devices: 0.02 us -> 2.83 us  [body(): head_shard = lax.psum_scatter(head_grads, 'shard', scatter_dimension=0)]
    ppermute x12 -> x10, starting transfers between devices: 17.5 us -> 14.8 us  [swap(): return lax.ppermute(block, name, [(j, j ^ mask) for j in range(size)])]
    ppermute x12, waiting for transfers between devices: 39.9 us -> 37.3 us  [team_gather(): lax.ppermute(block, 'rep', team_pairs(devices, steps))]
    ppermute x6 -> x9, waiting for transfers between devices: 11.7 us -> 12.8 us  [team_send(): lax.ppermute(slots[steps], 'rep', team_pairs(devices, steps))]
  transfers between devices with their start and end apart: 33 -> 35, of which waited for: 17 -> 22; matrix products, arithmetic and copies ran while one was open for 7% -> 6% of each run, Pallas kernels for 12% -> 15%
where the time goes in v2:
time: 222 us; the launch traced here: 221 us
  waiting for transfers between devices  99.8 us (45%)
  Pallas kernels  51.5 us (23%)
  starting transfers between devices  39.6 us (18%)
  between operations  15 us (7%)
  local copies, waits for them, and re-layouts  7.72 us (3%)
  other arithmetic  7.3 us (3%)
    pallas_call x7, Pallas kernels, run_kernel(): pl.pallas_call(kernel, out_shape=tuple(outs), in_specs=[pl.BlockSpec(memo...  51.5 us
    ppermute x10, waiting for transfers between devices, swap(): return lax.ppermute(block, name, [(j, j ^ mask) for j in range(size)])  44.7 us
    ppermute x12, waiting for transfers between devices, team_gather(): lax.ppermute(block, 'rep', team_pairs(devices, steps))  37.3 us
    ppermute x10, starting transfers between devices, swap(): return lax.ppermute(block, name, [(j, j ^ mask) for j in range(size)])  14.8 us
    ppermute x12, starting transfers between devices, team_gather(): lax.ppermute(block, 'rep', team_pairs(devices, steps))  14 us
    ppermute x9, waiting for transfers between devices, team_send(): lax.ppermute(slots[steps], 'rep', team_pairs(devices, steps))  12.8 us
    ppermute x9, starting transfers between devices, team_send(): lax.ppermute(slots[steps], 'rep', team_pairs(devices, steps))  10.6 us
  transfers between devices with their start and end apart: 35, of which 22 were waited for; matrix products, arithmetic and copies ran while one was open for 6% of the time, Pallas kernels for 15%

profile of v2, /device:TPU:0, one launch (start us, length us, event | category | flops | bytes accessed | tf_op | source)
XLA Modules:
  0.0 220.8 jit_solution(12271423114106497490)
XLA Ops:
  11.1 5.1 %collective-permute-start.2 = (bf16[144,1024]{1,0:T(8,128)(2,1)}, bf16[144,1024]{1,0:T(8,128)(2,1)S(1)}, u32[]{:S(2)}, u32[]{:S(2)}) collective-permute-start(bf16[144,1024]{1,0:T(8,128)(2,1)} %pack.1), channel_id=1, source_target_pairs={{0,6},{1,7},{2,4},{3,5},{4,2},{5,3},{6,0},{7,1},{8,14},{9,15},{10,... | collective-permute-start | bytes 884744 | tf_op jit(solution)/shard_map/ppermute | solution.py:829
  18.5 3.4 %feed_forward_pack.1 = bf16[2112,128]{1,0:T(8,128)(2,1)} custom-call(s32[2]{0:T(128)} %pad_add_fusion.places.scalars, bf16[128,2816]{1,0:T(8,128)(2,1)} %gate_far, bf16[128,2816]{1,0:T(8,128)(2,1)} %up_far.1, bf16[352,1024]{1,0:T(8,128)(2,1)} %down_far.1), custom_call_target="tpu_custom_call" | custom-call | flops 100000000 | bytes 2703360 | tf_op jit(solution)/shard_map/feed_forward_pack/pallas_call | solution.py:803
  21.9 5.2 %collective-permute-done.3 = bf16[128,1024]{1,0:T(8,128)(2,1)S(1)} collective-permute-done((bf16[128,1024]{1,0:T(8,128)(2,1)S(1)}, bf16[128,1024]{1,0:T(8,128)(2,1)S(1)}, u32[]{:S(2)}, u32[]{:S(2)}) %collective-permute-start.3) | collective-permute-done | bytes 262176 | tf_op jit(solution)/shard_map/ppermute | solution.py:829
  27.2 14.4 %collective-permute-done.1 = bf16[144,1024]{1,0:T(8,128)(2,1)S(1)} collective-permute-done((bf16[144,1024]{1,0:T(8,128)(2,1)}, bf16[144,1024]{1,0:T(8,128)(2,1)S(1)}, u32[]{:S(2)}, u32[]{:S(2)}) %collective-permute-start.1) | collective-permute-done | bytes 294944 | tf_op jit(solution)/shard_map/ppermute | solution.py:829
  52.3 4.4 %collective-permute-done.8 = bf16[256,1024]{1,0:T(8,128)(2,1)S(1)} collective-permute-done((bf16[256,1024]{1,0:T(8,128)(2,1)S(1)}, bf16[256,1024]{1,0:T(8,128)(2,1)S(1)}, u32[]{:S(2)}, u32[]{:S(2)}) %collective-permute-start.8) | collective-permute-done | bytes 524320 | tf_op jit(solution)/shard_map/ppermute | solution.py:829
  56.8 9.7 %mixer_forward.1 = (bf16[512,1024]{1,0:T(8,128)(2,1)S(1)}, f32[512,512]{1,0:T(8,128)S(1)}, f32[512,256]{1,0:T(8,128)S(1)}, f32[512,16]{1,0:T(8,128)S(1)}, f32[51...) custom-call(f32[2]{0:T(128)S(1)} %pad_maximum_fusion.7.scalars, ...), custom_call_target="tpu_custom_call" | custom-call | flops 8000000000 | bytes 9257984 | tf_op jit(solution)/shard_map/mixer_forward/pallas_call | solution.py:803
  66.5 2.6 %collective-permute-done.7.refs_3_ = bf16[8,128,256]{2,1,0:T(8,128)(2,1)} collective-permute-done((bf16[8,128,256]{2,1,0:T(8,128)(2,1)S(1)}, bf16[8,128,256]{2,1,0:T(8,128)(2,1)}, u32[]{:S(2)}, u32[]{:S(2)}) %collective-permute-start.7) | collective-permute-done | bytes 524320 | tf_op jit(solution)/shard_map/ppermute | solution.py:824
  69.1 4.8 %collective-permute-done.6.refs_2_ = bf16[8,128,256]{2,1,0:T(8,128)(2,1)} collective-permute-done((bf16[8,128,256]{2,1,0:T(8,128)(2,1)S(1)}, bf16[8,128,256]{2,1,0:T(8,128)(2,1)}, u32[]{:S(2)}, u32[]{:S(2)}) %collective-permute-start.6) | collective-permute-done | bytes 524320 | tf_op jit(solution)/shard_map/ppermute | solution.py:824
  73.9 5.1 %collective-permute-done.5.refs_1_ = bf16[8,128,256]{2,1,0:T(8,128)(2,1)} collective-permute-done((bf16[8,128,256]{2,1,0:T(8,128)(2,1)S(1)}, bf16[8,128,256]{2,1,0:T(8,128)(2,1)}, u32[]{:S(2)}, u32[]{:S(2)}) %collective-permute-start.5) | collective-permute-done | bytes 524320 | tf_op jit(solution)/shard_map/ppermute | solution.py:824
  83.6 5.5 %collective-permute-done.11.refs_10_ = bf16[512,256]{1,0:T(8,128)(2,1)S(1)} collective-permute-done((bf16[512,256]{1,0:T(8,128)(2,1)S(1)}, bf16[512,256]{1,0:T(8,128)(2,1)S(1)}, u32[]{:S(2)}, u32[]{:S(2)}) %collective-permute-start.11) | collective-permute-done | bytes 262176 | tf_op jit(solution)/shard_map/ppermute | solution.py:824
  89.1 4.3 %collective-permute-done.10.refs_9_ = bf16[512,256]{1,0:T(8,128)(2,1)S(1)} collective-permute-done((bf16[512,256]{1,0:T(8,128)(2,1)S(1)}, bf16[512,256]{1,0:T(8,128)(2,1)S(1)}, u32[]{:S(2)}, u32[]{:S(2)}) %collective-permute-start.10) | collective-permute-done | bytes 262176 | tf_op jit(solution)/shard_map/ppermute | solution.py:824
  94.2 16.6 %feed_forward.1 = (bf16[512,1024]{1,0:T(8,128)(2,1)}, f32[128,1024]{1,0:T(8,128)}, bf16[512,1024]{1,0:T(8,128)(2,1)}, bf16[512,1024]{1,0:T(8,128)(2,1)}, bf16[25...) custom-call(s32[2]{0:T(128)} %pad_add_fusion.places.scalars, ...), custom_call_target="tpu_custom_call" | custom-call | flops 16000000000 | bytes 18096128 | tf_op jit(solution)/shard_map/feed_forward/pallas_call | solution.py:803
  115.7 5.7 %collective-permute-done.12 = bf16[128,1024]{1,0:T(8,128)(2,1)S(1)} collective-permute-done((bf16[128,1024]{1,0:T(8,128)(2,1)S(1)}, bf16[128,1024]{1,0:T(8,128)(2,1)S(1)}, u32[]{:S(2)}, u32[]{:S(2)}) %collective-permute-start.12) | collective-permute-done | bytes 262176 | tf_op jit(solution)/shard_map/ppermute | solution.py:857
  121.4 5.7 %collective-permute-done.14 = bf16[128,1024]{1,0:T(8,128)(2,1)S(1)} collective-permute-done((bf16[128,1024]{1,0:T(8,128)(2,1)S(1)}, bf16[128,1024]{1,0:T(8,128)(2,1)S(1)}, u32[]{:S(2)}, u32[]{:S(2)}) %collective-permute-start.14) | collective-permute-done | bytes 262176 | tf_op jit(solution)/shard_map/ppermute | solution.py:857
  133.4 6.4 %collective-permute-done.17.refs_3_ = bf16[128,1024]{1,0:T(8,128)(2,1)S(1)} collective-permute-done((bf16[128,1024]{1,0:T(8,128)(2,1)S(1)}, bf16[128,1024]{1,0:T(8,128)(2,1)S(1)}, u32[]{:S(2)}, u32[]{:S(2)}) %collective-permute-start.17) | collective-permute-done | bytes 262176 | tf_op jit(solution)/shard_map/ppermute | solution.py:824
  139.7 2.7 %collective-permute-done.16.refs_2_ = bf16[128,1024]{1,0:T(8,128)(2,1)S(1)} collective-permute-done((bf16[128,1024]{1,0:T(8,128)(2,1)S(1)}, bf16[128,1024]{1,0:T(8,128)(2,1)S(1)}, u32[]{:S(2)}, u32[]{:S(2)}) %collective-permute-start.16) | collective-permute-done | bytes 262176 | tf_op jit(solution)/shard_map/ppermute | solution.py:824
  146.1 14.1 %mixer_backward.1 = (bf16[8,144,1024]{2,1,0:T(8,128)(2,1)}, bf16[512,1024]{1,0:T(8,128)(2,1)S(1)}) custom-call(f32[2]{0:T(128)S(1)} %pad_maximum_fusion.7.scalars, s32[2]{0:T(128)S(1)} %copy-done.5, bf16[128,1024]{1,0:T(8,128)(2,1)S(1)} %get-tuple-element.138.refs_0_, bf16[128,1024]{1,0:T(8,128)(2,1)S(1)} %collective-permute-done.15.refs_1_, ...), custom_call_target="tpu_custom_call" | custom-call | flops 10000000000 | bytes 12661760 | tf_op jit(solution)/shard_map/mixer_backward/pallas_call | solution.py:803
  170.1 7.5 %collective-permute-done.26.refs_6_ = bf16[1056,128]{1,0:T(8,128)(2,1)S(1)} collective-permute-done((bf16[1056,128]{1,0:T(8,128)(2,1)S(1)}, bf16[1056,128]{1,0:T(8,128)(2,1)S(1)}, u32[]{:S(2)}, u32[]{:S(2)}) %collective-permute-start.26) | collective-permute-done | bytes 270368 | tf_op jit(solution)/shard_map/ppermute | solution.py:829
  178.9 7.1 %collective-permute-done.24.refs_1_ = bf16[1056,128]{1,0:T(8,128)(2,1)S(1)} collective-permute-done((bf16[1056,128]{1,0:T(8,128)(2,1)S(1)}, bf16[1056,128]{1,0:T(8,128)(2,1)S(1)}, u32[]{:S(2)}, u32[]{:S(2)}) %collective-permute-start.24) | collective-permute-done | bytes 270368 | tf_op jit(solution)/shard_map/ppermute | solution.py:829
  189.5 4.6 %collective-permute-done.27 = bf16[2112,128]{1,0:T(8,128)(2,1)S(1)} collective-permute-done((bf16[2112,128]{1,0:T(8,128)(2,1)S(1)}, bf16[2112,128]{1,0:T(8,128)(2,1)S(1)}, u32[]{:S(2)}, u32[]{:S(2)}) %collective-permute-start.27) | collective-permute-done | bytes 540704 | tf_op jit(solution)/shard_map/ppermute | solution.py:829
  195.6 2.8 %reduce-scatter.5.cloned.1.call-done = bf16[1,144,1024]{2,1,0:T(8,128)(2,1)} async-done(((bf16[8,144,1024]{2,1,0:T(8,128)(2,1)}), bf16[1,144,1024]{2,1,0:T(8,128)(2,1)}) %reduce-scatter.5.cloned.1.call-update) | async-done | bytes 294928 | tf_op jit(solution)/shard_map/reduce_scatter | solution.py:1149
  202.2 3.2 %feed_forward_finish.1 = (f32[128,2816]{1,0:T(8,128)}, f32[128,2816]{1,0:T(8,128)}, f32[352,1024]{1,0:T(8,128)}) custom-call(s32[2]{0:T(128)S(1)} %copy-done.5, bf16[1056,128]{1,0:T(8,128)(2,1)S(1)} %get-tuple-element.157.refs_0_, bf16[1056,128]{1,0:T(8,128)(2,1)S(1)} %collective-permute-done.24.refs_1_, bf16[1056,128]{1,0:T(8,128)(2,1)S(1)} %get-tuple-element.159.refs_2_, ...), custom_call_target="tpu_custom_call" | custom-call | flops 100000000 | bytes 6488064 | tf_op jit(solution)/shard_map/feed_forward_finish/pallas_call | solution.py:803
  206.5 2.7 %collective-permute-done.30.refs_3_ = bf16[144,1024]{1,0:T(8,128)(2,1)S(1)} collective-permute-done((bf16[144,1024]{1,0:T(8,128)(2,1)}, bf16[144,1024]{1,0:T(8,128)(2,1)S(1)}, u32[]{:S(2)}, u32[]{:S(2)}) %collective-permute-start.30) | collective-permute-done | bytes 294944 | tf_op jit(solution)/shard_map/ppermute | solution.py:824
  209.2 3.1 %collective-permute-done.29.refs_2_ = bf16[144,1024]{1,0:T(8,128)(2,1)S(1)} collective-permute-done((bf16[144,1024]{1,0:T(8,128)(2,1)}, bf16[144,1024]{1,0:T(8,128)(2,1)S(1)}, u32[]{:S(2)}, u32[]{:S(2)}) %collective-permute-start.29) | collective-permute-done | bytes 294944 | tf_op jit(solution)/shard_map/ppermute | solution.py:824
  (151 shorter events, 59.1 us)
Async XLA Ops:
  7.2 43.6 %all-gather.5.cloned.1.call-start = ((), (), s32[]{:S(2)}) async-start(), calls=%async_computation.4 | async-start | bytes 1310720 | tf_op jit(solution)/shard_map/all_gather | solution.py:958
  7.9 85.6 %all-gather.7.cloned.1.call-start = ((), (), s32[]{:S(2)}) async-start(), calls=%async_computation.5 | async-start | bytes 4866048 | tf_op jit(solution)/shard_map/all_gather | solution.py:984
  11.1 16.1 %collective-permute-start.2 = (bf16[144,1024]{1,0:T(8,128)(2,1)}, bf16[144,1024]{1,0:T(8,128)(2,1)S(1)}, u32[]{:S(2)}, u32[]{:S(2)}) collective-permute-start(bf16[144,1024]{1,0:T(8,128)(2,1)} %pack.1), channel_id=1, source_target_pairs={{0,6},{1,7},{2,4},{3,5},{4,2},{5,3},{6,0},{7,1},{8,14},{9,15},{10,... | collective-permute-start | bytes 884744 | tf_op jit(solution)/shard_map/ppermute | solution.py:829
  16.2 25.3 %collective-permute-start.1 = (bf16[144,1024]{1,0:T(8,128)(2,1)}, bf16[144,1024]{1,0:T(8,128)(2,1)S(1)}, u32[]{:S(2)}, u32[]{:S(2)}) collective-permute-start(bf16[144,1024]{1,0:T(8,128)(2,1)} %pack.1), channel_id=1, source_target_pairs={{0,4},{1,5},{2,6},{3,7},{4,0},{5,1},{6,2},{7,3},{8,12},{9,13},{10,... | collective-permute-start | bytes 884744 | tf_op jit(solution)/shard_map/ppermute | solution.py:829
  16.2 25.3 %collective-permute-start = (bf16[144,1024]{1,0:T(8,128)(2,1)}, bf16[144,1024]{1,0:T(8,128)(2,1)S(1)}, u32[]{:S(2)}, u32[]{:S(2)}) collective-permute-start(bf16[144,1024]{1,0:T(8,128)(2,1)} %pack.1), channel_id=1, source_target_pairs={{0,2},{1,3},{2,0},{3,1},{4,6},{5,7},{6,4},{7,5},{8,10},{9,11},{10,... | collective-permute-start | bytes 884744 | tf_op jit(solution)/shard_map/ppermute | solution.py:829
  41.6 120.1 %reduce-scatter.3.cloned.1.call-start = ((), (), s32[]{:S(2)}) async-start(), calls=%async_computation.2 | async-start | bytes 4866048 | tf_op jit(solution)/shard_map/reduce_scatter | solution.py:1099
  42.0 14.8 %collective-permute-start.8 = (bf16[256,1024]{1,0:T(8,128)(2,1)S(1)}, bf16[256,1024]{1,0:T(8,128)(2,1)S(1)}, u32[]{:S(2)}, u32[]{:S(2)}) collective-permute-start(bf16[256,1024]{1,0:T(8,128)(2,1)S(1)} %pad_maximum_fusion.6), channel_id=1, source_target_pairs={{0,8},{8,0},{16,24},{24,16},{1,9},{9,1},{17,25},{25,17},{2,10},{10... | collective-permute-start | bytes 1572872 | tf_op jit(solution)/shard_map/ppermute | solution.py:829
  47.2 21.9 %collective-permute-start.7 = (bf16[8,128,256]{2,1,0:T(8,128)(2,1)S(1)}, bf16[8,128,256]{2,1,0:T(8,128)(2,1)}, u32[]{:S(2)}, u32[]{:S(2)}) collective-permute-start(bf16[8,128,256]{2,1,0:T(8,128)(2,1)S(1)} %pad_maximum_fusion.5.refs_0_), channel_id=1, source_target_pairs={{0,24},{8,16},{16,8},{24,0},{1,25},{9,17},{17,9},{25,1},{2,26},{10... | collective-permute-start | bytes 1572872 | tf_op jit(solution)/shard_map/ppermute | solution.py:824
  48.8 25.1 %collective-permute-start.6 = (bf16[8,128,256]{2,1,0:T(8,128)(2,1)S(1)}, bf16[8,128,256]{2,1,0:T(8,128)(2,1)}, u32[]{:S(2)}, u32[]{:S(2)}) collective-permute-start(bf16[8,128,256]{2,1,0:T(8,128)(2,1)S(1)} %pad_maximum_fusion.5.refs_0_), channel_id=1, source_target_pairs={{0,16},{8,24},{16,0},{24,8},{1,17},{9,25},{17,1},{25,9},{2,18},{10... | collective-permute-start | bytes 1572872 | tf_op jit(solution)/shard_map/ppermute | solution.py:824
  49.3 29.7 %collective-permute-start.5 = (bf16[8,128,256]{2,1,0:T(8,128)(2,1)S(1)}, bf16[8,128,256]{2,1,0:T(8,128)(2,1)}, u32[]{:S(2)}, u32[]{:S(2)}) collective-permute-start(bf16[8,128,256]{2,1,0:T(8,128)(2,1)S(1)} %pad_maximum_fusion.5.refs_0_), channel_id=1, source_target_pairs={{0,8},{8,0},{16,24},{24,16},{1,9},{9,1},{17,25},{25,17},{2,10},{10... | collective-permute-start | bytes 1572872 | tf_op jit(solution)/shard_map/ppermute | solution.py:824
  81.4 12.0 %collective-permute-start.10 = (bf16[512,256]{1,0:T(8,128)(2,1)S(1)}, bf16[512,256]{1,0:T(8,128)(2,1)S(1)}, u32[]{:S(2)}, u32[]{:S(2)}) collective-permute-start(bf16[512,256]{1,0:T(8,128)(2,1)S(1)} %get-tuple-element.86.refs_7_), channel_id=1, source_target_pairs={{0,16},{8,24},{16,0},{24,8},{1,17},{9,25},{17,1},{25,9},{2,18},{10... | collective-permute-start | bytes 786440 | tf_op jit(solution)/shard_map/ppermute | solution.py:824
  81.9 11.6 %collective-permute-start.9 = (bf16[512,256]{1,0:T(8,128)(2,1)S(1)}, bf16[512,256]{1,0:T(8,128)(2,1)S(1)}, u32[]{:S(2)}, u32[]{:S(2)}) collective-permute-start(bf16[512,256]{1,0:T(8,128)(2,1)S(1)} %get-tuple-element.86.refs_7_), channel_id=1, source_target_pairs={{0,8},{8,0},{16,24},{24,16},{1,9},{9,1},{17,25},{25,17},{2,10},{10... | collective-permute-start | bytes 786440 | tf_op jit(solution)/shard_map/ppermute | solution.py:824
  110.9 87.5 %reduce-scatter.5.cloned.1.call-start = ((), (), s32[]{:S(2)}) async-start(), calls=%async_computation.3 | async-start | bytes 2654208 | tf_op jit(solution)/shard_map/reduce_scatter | solution.py:1149
  113.7 13.4 %collective-permute-start.14 = (bf16[128,1024]{1,0:T(8,128)(2,1)S(1)}, bf16[128,1024]{1,0:T(8,128)(2,1)S(1)}, u32[]{:S(2)}, u32[]{:S(2)}) collective-permute-start(bf16[128,1024]{1,0:T(8,128)(2,1)S(1)} %get-tuple-element.148), channel_id=1, source_target_pairs={{0,24},{8,16},{16,8},{24,0},{1,25},{9,17},{17,9},{25,1},{2,26},{10... | collective-permute-start | bytes 786440 | tf_op jit(solution)/shard_map/ppermute | solution.py:857
  115.2 13.3 %collective-permute-start.13 = (bf16[128,1024]{1,0:T(8,128)(2,1)S(1)}, bf16[128,1024]{1,0:T(8,128)(2,1)S(1)}, u32[]{:S(2)}, u32[]{:S(2)}) collective-permute-start(bf16[128,1024]{1,0:T(8,128)(2,1)S(1)} %get-tuple-element.149), channel_id=1, source_target_pairs={{0,16},{8,24},{16,0},{24,8},{1,17},{9,25},{17,1},{25,9},{2,18},{10... | collective-permute-start | bytes 786440 | tf_op jit(solution)/shard_map/ppermute | solution.py:857
  142.5 17.7 %collective-permute-start.18 = (bf16[128,1024]{1,0:T(8,128)(2,1)S(1)}, bf16[128,1024]{1,0:T(8,128)(2,1)S(1)}, u32[]{:S(2)}, u32[]{:S(2)}) collective-permute-start(bf16[128,1024]{1,0:T(8,128)(2,1)S(1)} %get-tuple-element.144), channel_id=1, source_target_pairs={{0,8},{8,0},{16,24},{24,16},{1,9},{9,1},{17,25},{25,17},{2,10},{10... | collective-permute-start | bytes 786440 | tf_op jit(solution)/shard_map/ppermute | solution.py:857
  143.1 17.1 %collective-permute-start.20 = (bf16[128,1024]{1,0:T(8,128)(2,1)S(1)}, bf16[128,1024]{1,0:T(8,128)(2,1)S(1)}, u32[]{:S(2)}, u32[]{:S(2)}) collective-permute-start(bf16[128,1024]{1,0:T(8,128)(2,1)S(1)} %get-tuple-element.145), channel_id=1, source_target_pairs={{0,24},{8,16},{16,8},{24,0},{1,25},{9,17},{17,9},{25,1},{2,26},{10... | collective-permute-start | bytes 786440 | tf_op jit(solution)/shard_map/ppermute | solution.py:857
  144.7 15.6 %collective-permute-start.19 = (bf16[128,1024]{1,0:T(8,128)(2,1)S(1)}, bf16[128,1024]{1,0:T(8,128)(2,1)S(1)}, u32[]{:S(2)}, u32[]{:S(2)}) collective-permute-start(bf16[128,1024]{1,0:T(8,128)(2,1)S(1)} %get-tuple-element.146), channel_id=1, source_target_pairs={{0,16},{8,24},{16,0},{24,8},{1,17},{9,25},{17,1},{25,9},{2,18},{10... | collective-permute-start | bytes 786440 | tf_op jit(solution)/shard_map/ppermute | solution.py:857
  162.8 14.9 %collective-permute-start.26 = (bf16[1056,128]{1,0:T(8,128)(2,1)S(1)}, bf16[1056,128]{1,0:T(8,128)(2,1)S(1)}, u32[]{:S(2)}, u32[]{:S(2)}) collective-permute-start(bf16[1056,128]{1,0:T(8,128)(2,1)S(1)} %get-tuple-element.156.refs_4_), channel_id=1, source_target_pairs={{0,16},{8,24},{16,0},{24,8},{1,17},{9,25},{17,1},{25,9},{2,18},{10... | collective-permute-start | bytes 811016 | tf_op jit(solution)/shard_map/ppermute | solution.py:829
  165.2 36.2 %collective-permute-start.23 = (bf16[128,1024]{1,0:T(8,128)(2,1)}, bf16[128,1024]{1,0:T(8,128)(2,1)S(1)}, u32[]{:S(2)}, u32[]{:S(2)}) collective-permute-start(bf16[128,1024]{1,0:T(8,128)(2,1)} %get-tuple-element.140), channel_id=1, source_target_pairs={{0,24},{8,16},{16,8},{24,0},{1,25},{9,17},{17,9},{25,1},{2,26},{10... | collective-permute-start | bytes 786440 | tf_op jit(solution)/shard_map/ppermute | solution.py:857
  166.6 35.2 %collective-permute-start.22 = (bf16[128,1024]{1,0:T(8,128)(2,1)}, bf16[128,1024]{1,0:T(8,128)(2,1)S(1)}, u32[]{:S(2)}, u32[]{:S(2)}) collective-permute-start(bf16[128,1024]{1,0:T(8,128)(2,1)} %get-tuple-element.141), channel_id=1, source_target_pairs={{0,16},{8,24},{16,0},{24,8},{1,17},{9,25},{17,1},{25,9},{2,18},{10... | collective-permute-start | bytes 786440 | tf_op jit(solution)/shard_map/ppermute | solution.py:857
  168.1 33.8 %collective-permute-start.21 = (bf16[128,1024]{1,0:T(8,128)(2,1)}, bf16[128,1024]{1,0:T(8,128)(2,1)S(1)}, u32[]{:S(2)}, u32[]{:S(2)}) collective-permute-start(bf16[128,1024]{1,0:T(8,128)(2,1)} %get-tuple-element.142), channel_id=1, source_target_pairs={{0,8},{8,0},{16,24},{24,16},{1,9},{9,1},{17,25},{25,17},{2,10},{10... | collective-permute-start | bytes 786440 | tf_op jit(solution)/shard_map/ppermute | solution.py:857
  168.7 17.4 %collective-permute-start.24 = (bf16[1056,128]{1,0:T(8,128)(2,1)S(1)}, bf16[1056,128]{1,0:T(8,128)(2,1)S(1)}, u32[]{:S(2)}, u32[]{:S(2)}) collective-permute-start(bf16[1056,128]{1,0:T(8,128)(2,1)S(1)} %get-tuple-element.157.refs_0_), channel_id=1, source_target_pairs={{0,8},{8,0},{16,24},{24,16},{1,9},{9,1},{17,25},{25,17},{2,10},{10... | collective-permute-start | bytes 811016 | tf_op jit(solution)/shard_map/ppermute | solution.py:829
  177.7 16.4 %collective-permute-start.27 = (bf16[2112,128]{1,0:T(8,128)(2,1)S(1)}, bf16[2112,128]{1,0:T(8,128)(2,1)S(1)}, u32[]{:S(2)}, u32[]{:S(2)}) collective-permute-start(bf16[2112,128]{1,0:T(8,128)(2,1)S(1)} %pad_maximum_fusion.4), channel_id=1, source_target_pairs={{0,8},{8,0},{16,24},{24,16},{1,9},{9,1},{17,25},{25,17},{2,10},{10... | collective-permute-start | bytes 1622024 | tf_op jit(solution)/shard_map/ppermute | solution.py:829
  (44 other events, 540.3 us)
Sparse Core Ops, SparseCore 0:
  9.9 31.0 all-gather.4
  43.1 48.4 all-gather.6
  111.0 50.6 reduce-scatter.2
  164.0 34.3 reduce-scatter.4

commit v3 on v2

--- a/solution.py
+++ b/solution.py
@@ -309,6 +309,7 @@
         pltpu.make_async_copy(source, target, sems.at[index])
         for index, (source, target) in enumerate(zip(far, near))
     ]
+    early = outs_count + 1
     for copy in fetch:
         copy.start()
     sent = []
@@ -333,7 +334,7 @@
             ]
     send(mixed, mixed_out)
     chips, chunk = out_slots[0].shape[0] // 2, out_slots[0].shape[1]
-    for copy in fetch[: outs_count + 1]:
+    for copy in fetch[:early]:
         copy.wait()
     for index in range(outs_count):
         place = pl.multiple_of(member(part, index) * outs, outs)
@@ -348,9 +349,9 @@
     wide = hidden[...]
     normed = wide * lax.rsqrt(jnp.mean(wide * wide, -1, keepdims=True) + EPS)
     second = (normed * gain[...]).astype(LOW)
-    fetch[outs_count + 1].wait()
+    fetch[early].wait()
     feed_forward_unpack(packs.shape[0], packs, up_weights, down_weights)
-    fetch[outs_count + 2].wait()
+    fetch[early + 1].wait()
     part_width = down_weights.shape[0]
     both = local_dot(second, up_weights[...])
     gate, up = both[:, :part_width], both[:, part_width:]
@@ -359,20 +360,10 @@
     active = (gate_act * up).astype(LOW)
     result[...] = local_dot(active, down_weights[...]).astype(LOW)
     send(result, result_out)
-    active_grad = right_dot(cotangents[...], down_weights[...])
-    gate_back = (active_grad * up * gate_sig * (1.0 + gate * (1.0 - gate_sig))).astype(LOW)
-    up_back = (active_grad * gate_act).astype(LOW)
-    back = jnp.concatenate([gate_back, up_back], 1)
-    second_grad = right_dot(back, up_weights[...])
-    second_grad_low[...] = second_grad.astype(LOW)
-    send(second_grad_low, second_grad_out)
-    wide = hidden[...]
-    normed = wide * lax.rsqrt(jnp.mean(wide * wide, -1, keepdims=True) + EPS)
-    gain_grad_out[...] = jnp.sum(second_grad * normed, 0, keepdims=True)
     shards = grads.shape[0]
     chunk = out_full.shape[0] // shards
     each = part_width // shards
-    ups = back.shape[1] // LANES
+    ups = 2 * part_width // LANES
     down_grad = left_dot(active, cotangents[...])
     for shard in range(shards):
         for index in range(down_grad.shape[1] // (2 * LANES)):
@@ -380,6 +371,12 @@
             grads[shard, start : start + 2 * each] = on_end(
                 down_grad[shard * each : (shard + 1) * each], index
             ).astype(LOW)
+    lower = pl.ds(ups * chunk, grads.shape[1] - ups * chunk)
+    send(grads.at[:, lower], grads_out.at[:, lower])
+    active_grad = right_dot(cotangents[...], down_weights[...])
+    gate_back = (active_grad * up * gate_sig * (1.0 + gate * (1.0 - gate_sig))).astype(LOW)
+    up_back = (active_grad * gate_act).astype(LOW)
+    back = jnp.concatenate([gate_back, up_back], 1)
     half = shards // 2
     for first_shard in (0, half):
         line = slice(first_shard * chunk, (first_shard + half) * chunk)
@@ -389,8 +386,14 @@
                 grads[first_shard + shard, index * chunk : (index + 1) * chunk] = up_grad[
                     shard * chunk : (shard + 1) * chunk, index * LANES : (index + 1) * LANES
                 ].astype(LOW)
-        place = pl.ds(first_shard, half)
-        send(grads.at[place], grads_out.at[place])
+        spot = pl.ds(first_shard, half), pl.ds(0, ups * chunk)
+        send(grads.at[spot], grads_out.at[spot])
+    second_grad = right_dot(back, up_weights[...])
+    second_grad_low[...] = second_grad.astype(LOW)
+    send(second_grad_low, second_grad_out)
+    wide = hidden[...]
+    normed = wide * lax.rsqrt(jnp.mean(wide * wide, -1, keepdims=True) + EPS)
+    gain_grad_out[...] = jnp.sum(second_grad * normed, 0, keepdims=True)
     for copy in sent:
         copy.wait()
 
@@ -1086,7 +1089,7 @@
             pltpu.VMEM(ffn_packs.shape, LOW),
             pltpu.VMEM(cotangents.shape, LOW),
             pltpu.SemaphoreType.DMA((team + 3,)),
-            pltpu.SemaphoreType.DMA((7,)),
+            pltpu.SemaphoreType.DMA((8,)),
         ),
         team + 3,
         6,

time: 222 us -> 221 us (level)
  transfers between devices with their start and end apart: 35 -> 35, of which waited for: 22 -> 23; matrix products, arithmetic and copies ran while one was open for 6% -> 6% of each run, Pallas kernels for 15% -> 15%
where the time goes in v3:
time: 221 us; the launch traced here: 220 us
  waiting for transfers between devices  99.8 us (45%)
  Pallas kernels  50.6 us (23%)
  starting transfers between devices  39.6 us (18%)
  between operations  15 us (7%)
  local copies, waits for them, and re-layouts  7.72 us (3%)
  other arithmetic  7.3 us (3%)
    pallas_call x7, Pallas kernels, run_kernel(): pl.pallas_call(kernel, out_shape=tuple(outs), in_specs=[pl.BlockSpec(memo...  50.6 us
    ppermute x10, waiting for transfers between devices, swap(): return lax.ppermute(block, name, [(j, j ^ mask) for j in range(size)])  44.7 us
    ppermute x12, waiting for transfers between devices, team_gather(): lax.ppermute(block, 'rep', team_pairs(devices, steps))  37.2 us
    ppermute x10, starting transfers between devices, swap(): return lax.ppermute(block, name, [(j, j ^ mask) for j in range(size)])  14.8 us
    ppermute x12, starting transfers between devices, team_gather(): lax.ppermute(block, 'rep', team_pairs(devices, steps))  14 us
    ppermute x9, waiting for transfers between devices, team_send(): lax.ppermute(slots[steps], 'rep', team_pairs(devices, steps))  12.8 us
    ppermute x9, starting transfers between devices, team_send(): lax.ppermute(slots[steps], 'rep', team_pairs(devices, steps))  10.6 us
  transfers between devices with their start and end apart: 35, of which 23 were waited for; matrix products, arithmetic and copies ran while one was open for 6% of the time, Pallas kernels for 15%

profile of v3, /device:TPU:0, one launch (start us, length us, event | category | flops | bytes accessed | tf_op | source)
XLA Modules:
  0.0 220.0 jit_solution(5944627792500983991)
XLA Ops:
  11.1 5.1 %collective-permute-start.2 = (bf16[144,1024]{1,0:T(8,128)(2,1)}, bf16[144,1024]{1,0:T(8,128)(2,1)S(1)}, u32[]{:S(2)}, u32[]{:S(2)}) collective-permute-start(bf16[144,1024]{1,0:T(8,128)(2,1)} %pack.1), channel_id=1, source_target_pairs={{0,6},{1,7},{2,4},{3,5},{4,2},{5,3},{6,0},{7,1},{8,14},{9,15},{10,... | collective-permute-start | bytes 884744 | tf_op jit(solution)/shard_map/ppermute | solution.py:832
  18.5 3.4 %feed_forward_pack.1 = bf16[2112,128]{1,0:T(8,128)(2,1)} custom-call(s32[2]{0:T(128)} %pad_add_fusion.places.scalars, bf16[128,2816]{1,0:T(8,128)(2,1)} %gate_far, bf16[128,2816]{1,0:T(8,128)(2,1)} %up_far.1, bf16[352,1024]{1,0:T(8,128)(2,1)} %down_far.1), custom_call_target="tpu_custom_call" | custom-call | flops 100000000 | bytes 2703360 | tf_op jit(solution)/shard_map/feed_forward_pack/pallas_call | solution.py:806
  21.9 5.2 %collective-permute-done.3 = bf16[128,1024]{1,0:T(8,128)(2,1)S(1)} collective-permute-done((bf16[128,1024]{1,0:T(8,128)(2,1)S(1)}, bf16[128,1024]{1,0:T(8,128)(2,1)S(1)}, u32[]{:S(2)}, u32[]{:S(2)}) %collective-permute-start.3) | collective-permute-done | bytes 262176 | tf_op jit(solution)/shard_map/ppermute | solution.py:832
  27.2 14.4 %collective-permute-done.1 = bf16[144,1024]{1,0:T(8,128)(2,1)S(1)} collective-permute-done((bf16[144,1024]{1,0:T(8,128)(2,1)}, bf16[144,1024]{1,0:T(8,128)(2,1)S(1)}, u32[]{:S(2)}, u32[]{:S(2)}) %collective-permute-start.1) | collective-permute-done | bytes 294944 | tf_op jit(solution)/shard_map/ppermute | solution.py:832
  52.3 4.4 %collective-permute-done.8 = bf16[256,1024]{1,0:T(8,128)(2,1)S(1)} collective-permute-done((bf16[256,1024]{1,0:T(8,128)(2,1)S(1)}, bf16[256,1024]{1,0:T(8,128)(2,1)S(1)}, u32[]{:S(2)}, u32[]{:S(2)}) %collective-permute-start.8) | collective-permute-done | bytes 524320 | tf_op jit(solution)/shard_map/ppermute | solution.py:832
  56.8 9.7 %mixer_forward.1 = (bf16[512,1024]{1,0:T(8,128)(2,1)S(1)}, f32[512,512]{1,0:T(8,128)S(1)}, f32[512,256]{1,0:T(8,128)S(1)}, f32[512,16]{1,0:T(8,128)S(1)}, f32[51...) custom-call(f32[2]{0:T(128)S(1)} %pad_maximum_fusion.7.scalars, ...), custom_call_target="tpu_custom_call" | custom-call | flops 8000000000 | bytes 9257984 | tf_op jit(solution)/shard_map/mixer_forward/pallas_call | solution.py:806
  66.5 2.6 %collective-permute-done.7.refs_3_ = bf16[8,128,256]{2,1,0:T(8,128)(2,1)} collective-permute-done((bf16[8,128,256]{2,1,0:T(8,128)(2,1)S(1)}, bf16[8,128,256]{2,1,0:T(8,128)(2,1)}, u32[]{:S(2)}, u32[]{:S(2)}) %collective-permute-start.7) | collective-permute-done | bytes 524320 | tf_op jit(solution)/shard_map/ppermute | solution.py:827
  69.1 4.8 %collective-permute-done.6.refs_2_ = bf16[8,128,256]{2,1,0:T(8,128)(2,1)} collective-permute-done((bf16[8,128,256]{2,1,0:T(8,128)(2,1)S(1)}, bf16[8,128,256]{2,1,0:T(8,128)(2,1)}, u32[]{:S(2)}, u32[]{:S(2)}) %collective-permute-start.6) | collective-permute-done | bytes 524320 | tf_op jit(solution)/shard_map/ppermute | solution.py:827
  73.9 5.1 %collective-permute-done.5.refs_1_ = bf16[8,128,256]{2,1,0:T(8,128)(2,1)} collective-permute-done((bf16[8,128,256]{2,1,0:T(8,128)(2,1)S(1)}, bf16[8,128,256]{2,1,0:T(8,128)(2,1)}, u32[]{:S(2)}, u32[]{:S(2)}) %collective-permute-start.5) | collective-permute-done | bytes 524320 | tf_op jit(solution)/shard_map/ppermute | solution.py:827
  83.6 5.5 %collective-permute-done.11.refs_10_ = bf16[512,256]{1,0:T(8,128)(2,1)S(1)} collective-permute-done((bf16[512,256]{1,0:T(8,128)(2,1)S(1)}, bf16[512,256]{1,0:T(8,128)(2,1)S(1)}, u32[]{:S(2)}, u32[]{:S(2)}) %collective-permute-start.11) | collective-permute-done | bytes 262176 | tf_op jit(solution)/shard_map/ppermute | solution.py:827
  89.1 4.3 %collective-permute-done.10.refs_9_ = bf16[512,256]{1,0:T(8,128)(2,1)S(1)} collective-permute-done((bf16[512,256]{1,0:T(8,128)(2,1)S(1)}, bf16[512,256]{1,0:T(8,128)(2,1)S(1)}, u32[]{:S(2)}, u32[]{:S(2)}) %collective-permute-start.10) | collective-permute-done | bytes 262176 | tf_op jit(solution)/shard_map/ppermute | solution.py:827
  94.2 15.7 %feed_forward.1 = (bf16[512,1024]{1,0:T(8,128)(2,1)}, f32[128,1024]{1,0:T(8,128)}, bf16[512,1024]{1,0:T(8,128)(2,1)}, bf16[512,1024]{1,0:T(8,128)(2,1)}, bf16[25...) custom-call(s32[2]{0:T(128)} %pad_add_fusion.places.scalars, ...), custom_call_target="tpu_custom_call" | custom-call | flops 16000000000 | bytes 18096128 | tf_op jit(solution)/shard_map/feed_forward/pallas_call | solution.py:806
  114.8 5.7 %collective-permute-done.12 = bf16[128,1024]{1,0:T(8,128)(2,1)S(1)} collective-permute-done((bf16[128,1024]{1,0:T(8,128)(2,1)S(1)}, bf16[128,1024]{1,0:T(8,128)(2,1)S(1)}, u32[]{:S(2)}, u32[]{:S(2)}) %collective-permute-start.12) | collective-permute-done | bytes 262176 | tf_op jit(solution)/shard_map/ppermute | solution.py:860
  120.5 5.7 %collective-permute-done.14 = bf16[128,1024]{1,0:T(8,128)(2,1)S(1)} collective-permute-done((bf16[128,1024]{1,0:T(8,128)(2,1)S(1)}, bf16[128,1024]{1,0:T(8,128)(2,1)S(1)}, u32[]{:S(2)}, u32[]{:S(2)}) %collective-permute-start.14) | collective-permute-done | bytes 262176 | tf_op jit(solution)/shard_map/ppermute | solution.py:860
  132.5 6.4 %collective-permute-done.17.refs_3_ = bf16[128,1024]{1,0:T(8,128)(2,1)S(1)} collective-permute-done((bf16[128,1024]{1,0:T(8,128)(2,1)S(1)}, bf16[128,1024]{1,0:T(8,128)(2,1)S(1)}, u32[]{:S(2)}, u32[]{:S(2)}) %collective-permute-start.17) | collective-permute-done | bytes 262176 | tf_op jit(solution)/shard_map/ppermute | solution.py:827
  138.9 2.7 %collective-permute-done.16.refs_2_ = bf16[128,1024]{1,0:T(8,128)(2,1)S(1)} collective-permute-done((bf16[128,1024]{1,0:T(8,128)(2,1)S(1)}, bf16[128,1024]{1,0:T(8,128)(2,1)S(1)}, u32[]{:S(2)}, u32[]{:S(2)}) %collective-permute-start.16) | collective-permute-done | bytes 262176 | tf_op jit(solution)/shard_map/ppermute | solution.py:827
  145.3 14.1 %mixer_backward.1 = (bf16[8,144,1024]{2,1,0:T(8,128)(2,1)}, bf16[512,1024]{1,0:T(8,128)(2,1)S(1)}) custom-call(f32[2]{0:T(128)S(1)} %pad_maximum_fusion.7.scalars, s32[2]{0:T(128)S(1)} %copy-done.5, bf16[128,1024]{1,0:T(8,128)(2,1)S(1)} %get-tuple-element.138.refs_0_, bf16[128,1024]{1,0:T(8,128)(2,1)S(1)} %collective-permute-done.15.refs_1_, ...), custom_call_target="tpu_custom_call" | custom-call | flops 10000000000 | bytes 12661760 | tf_op jit(solution)/shard_map/mixer_backward/pallas_call | solution.py:806
  169.3 7.5 %collective-permute-done.26.refs_6_ = bf16[1056,128]{1,0:T(8,128)(2,1)S(1)} collective-permute-done((bf16[1056,128]{1,0:T(8,128)(2,1)S(1)}, bf16[1056,128]{1,0:T(8,128)(2,1)S(1)}, u32[]{:S(2)}, u32[]{:S(2)}) %collective-permute-start.26) | collective-permute-done | bytes 270368 | tf_op jit(solution)/shard_map/ppermute | solution.py:832
  178.0 7.1 %collective-permute-done.24.refs_1_ = bf16[1056,128]{1,0:T(8,128)(2,1)S(1)} collective-permute-done((bf16[1056,128]{1,0:T(8,128)(2,1)S(1)}, bf16[1056,128]{1,0:T(8,128)(2,1)S(1)}, u32[]{:S(2)}, u32[]{:S(2)}) %collective-permute-start.24) | collective-permute-done | bytes 270368 | tf_op jit(solution)/shard_map/ppermute | solution.py:832
  188.6 4.6 %collective-permute-done.27 = bf16[2112,128]{1,0:T(8,128)(2,1)S(1)} collective-permute-done((bf16[2112,128]{1,0:T(8,128)(2,1)S(1)}, bf16[2112,128]{1,0:T(8,128)(2,1)S(1)}, u32[]{:S(2)}, u32[]{:S(2)}) %collective-permute-start.27) | collective-permute-done | bytes 540704 | tf_op jit(solution)/shard_map/ppermute | solution.py:832
  194.7 3.0 %reduce-scatter.5.cloned.1.call-done = bf16[1,144,1024]{2,1,0:T(8,128)(2,1)} async-done(((bf16[8,144,1024]{2,1,0:T(8,128)(2,1)}), bf16[1,144,1024]{2,1,0:T(8,128)(2,1)}) %reduce-scatter.5.cloned.1.call-update) | async-done | bytes 294928 | tf_op jit(solution)/shard_map/reduce_scatter | solution.py:1152
  201.5 3.2 %feed_forward_finish.1 = (f32[128,2816]{1,0:T(8,128)}, f32[128,2816]{1,0:T(8,128)}, f32[352,1024]{1,0:T(8,128)}) custom-call(s32[2]{0:T(128)S(1)} %copy-done.5, bf16[1056,128]{1,0:T(8,128)(2,1)S(1)} %get-tuple-element.157.refs_0_, bf16[1056,128]{1,0:T(8,128)(2,1)S(1)} %collective-permute-done.24.refs_1_, bf16[1056,128]{1,0:T(8,128)(2,1)S(1)} %get-tuple-element.159.refs_2_, ...), custom_call_target="tpu_custom_call" | custom-call | flops 100000000 | bytes 6488064 | tf_op jit(solution)/shard_map/feed_forward_finish/pallas_call | solution.py:806
  205.8 2.5 %collective-permute-done.30.refs_3_ = bf16[144,1024]{1,0:T(8,128)(2,1)S(1)} collective-permute-done((bf16[144,1024]{1,0:T(8,128)(2,1)}, bf16[144,1024]{1,0:T(8,128)(2,1)S(1)}, u32[]{:S(2)}, u32[]{:S(2)}) %collective-permute-start.30) | collective-permute-done | bytes 294944 | tf_op jit(solution)/shard_map/ppermute | solution.py:827
  208.4 3.1 %collective-permute-done.29.refs_2_ = bf16[144,1024]{1,0:T(8,128)(2,1)S(1)} collective-permute-done((bf16[144,1024]{1,0:T(8,128)(2,1)}, bf16[144,1024]{1,0:T(8,128)(2,1)S(1)}, u32[]{:S(2)}, u32[]{:S(2)}) %collective-permute-start.29) | collective-permute-done | bytes 294944 | tf_op jit(solution)/shard_map/ppermute | solution.py:827
  (151 shorter events, 59.1 us)
Async XLA Ops:
  7.2 43.6 %all-gather.5.cloned.1.call-start = ((), (), s32[]{:S(2)}) async-start(), calls=%async_computation.4 | async-start | bytes 1310720 | tf_op jit(solution)/shard_map/all_gather | solution.py:961
  7.9 85.6 %all-gather.7.cloned.1.call-start = ((), (), s32[]{:S(2)}) async-start(), calls=%async_computation.5 | async-start | bytes 4866048 | tf_op jit(solution)/shard_map/all_gather | solution.py:987
  11.1 16.1 %collective-permute-start.2 = (bf16[144,1024]{1,0:T(8,128)(2,1)}, bf16[144,1024]{1,0:T(8,128)(2,1)S(1)}, u32[]{:S(2)}, u32[]{:S(2)}) collective-permute-start(bf16[144,1024]{1,0:T(8,128)(2,1)} %pack.1), channel_id=1, source_target_pairs={{0,6},{1,7},{2,4},{3,5},{4,2},{5,3},{6,0},{7,1},{8,14},{9,15},{10,... | collective-permute-start | bytes 884744 | tf_op jit(solution)/shard_map/ppermute | solution.py:832
  16.2 25.3 %collective-permute-start.1 = (bf16[144,1024]{1,0:T(8,128)(2,1)}, bf16[144,1024]{1,0:T(8,128)(2,1)S(1)}, u32[]{:S(2)}, u32[]{:S(2)}) collective-permute-start(bf16[144,1024]{1,0:T(8,128)(2,1)} %pack.1), channel_id=1, source_target_pairs={{0,4},{1,5},{2,6},{3,7},{4,0},{5,1},{6,2},{7,3},{8,12},{9,13},{10,... | collective-permute-start | bytes 884744 | tf_op jit(solution)/shard_map/ppermute | solution.py:832
  16.2 25.3 %collective-permute-start = (bf16[144,1024]{1,0:T(8,128)(2,1)}, bf16[144,1024]{1,0:T(8,128)(2,1)S(1)}, u32[]{:S(2)}, u32[]{:S(2)}) collective-permute-start(bf16[144,1024]{1,0:T(8,128)(2,1)} %pack.1), channel_id=1, source_target_pairs={{0,2},{1,3},{2,0},{3,1},{4,6},{5,7},{6,4},{7,5},{8,10},{9,11},{10,... | collective-permute-start | bytes 884744 | tf_op jit(solution)/shard_map/ppermute | solution.py:832
  41.6 119.2 %reduce-scatter.3.cloned.1.call-start = ((), (), s32[]{:S(2)}) async-start(), calls=%async_computation.2 | async-start | bytes 4866048 | tf_op jit(solution)/shard_map/reduce_scatter | solution.py:1102
  42.0 14.8 %collective-permute-start.8 = (bf16[256,1024]{1,0:T(8,128)(2,1)S(1)}, bf16[256,1024]{1,0:T(8,128)(2,1)S(1)}, u32[]{:S(2)}, u32[]{:S(2)}) collective-permute-start(bf16[256,1024]{1,0:T(8,128)(2,1)S(1)} %pad_maximum_fusion.6), channel_id=1, source_target_pairs={{0,8},{8,0},{16,24},{24,16},{1,9},{9,1},{17,25},{25,17},{2,10},{10... | collective-permute-start | bytes 1572872 | tf_op jit(solution)/shard_map/ppermute | solution.py:832
  47.2 21.9 %collective-permute-start.7 = (bf16[8,128,256]{2,1,0:T(8,128)(2,1)S(1)}, bf16[8,128,256]{2,1,0:T(8,128)(2,1)}, u32[]{:S(2)}, u32[]{:S(2)}) collective-permute-start(bf16[8,128,256]{2,1,0:T(8,128)(2,1)S(1)} %pad_maximum_fusion.5.refs_0_), channel_id=1, source_target_pairs={{0,24},{8,16},{16,8},{24,0},{1,25},{9,17},{17,9},{25,1},{2,26},{10... | collective-permute-start | bytes 1572872 | tf_op jit(solution)/shard_map/ppermute | solution.py:827
  48.8 25.1 %collective-permute-start.6 = (bf16[8,128,256]{2,1,0:T(8,128)(2,1)S(1)}, bf16[8,128,256]{2,1,0:T(8,128)(2,1)}, u32[]{:S(2)}, u32[]{:S(2)}) collective-permute-start(bf16[8,128,256]{2,1,0:T(8,128)(2,1)S(1)} %pad_maximum_fusion.5.refs_0_), channel_id=1, source_target_pairs={{0,16},{8,24},{16,0},{24,8},{1,17},{9,25},{17,1},{25,9},{2,18},{10... | collective-permute-start | bytes 1572872 | tf_op jit(solution)/shard_map/ppermute | solution.py:827
  49.3 29.7 %collective-permute-start.5 = (bf16[8,128,256]{2,1,0:T(8,128)(2,1)S(1)}, bf16[8,128,256]{2,1,0:T(8,128)(2,1)}, u32[]{:S(2)}, u32[]{:S(2)}) collective-permute-start(bf16[8,128,256]{2,1,0:T(8,128)(2,1)S(1)} %pad_maximum_fusion.5.refs_0_), channel_id=1, source_target_pairs={{0,8},{8,0},{16,24},{24,16},{1,9},{9,1},{17,25},{25,17},{2,10},{10... | collective-permute-start | bytes 1572872 | tf_op jit(solution)/shard_map/ppermute | solution.py:827
  81.4 12.0 %collective-permute-start.10 = (bf16[512,256]{1,0:T(8,128)(2,1)S(1)}, bf16[512,256]{1,0:T(8,128)(2,1)S(1)}, u32[]{:S(2)}, u32[]{:S(2)}) collective-permute-start(bf16[512,256]{1,0:T(8,128)(2,1)S(1)} %get-tuple-element.86.refs_7_), channel_id=1, source_target_pairs={{0,16},{8,24},{16,0},{24,8},{1,17},{9,25},{17,1},{25,9},{2,18},{10... | collective-permute-start | bytes 786440 | tf_op jit(solution)/shard_map/ppermute | solution.py:827
  81.9 11.6 %collective-permute-start.9 = (bf16[512,256]{1,0:T(8,128)(2,1)S(1)}, bf16[512,256]{1,0:T(8,128)(2,1)S(1)}, u32[]{:S(2)}, u32[]{:S(2)}) collective-permute-start(bf16[512,256]{1,0:T(8,128)(2,1)S(1)} %get-tuple-element.86.refs_7_), channel_id=1, source_target_pairs={{0,8},{8,0},{16,24},{24,16},{1,9},{9,1},{17,25},{25,17},{2,10},{10... | collective-permute-start | bytes 786440 | tf_op jit(solution)/shard_map/ppermute | solution.py:827
  110.0 87.6 %reduce-scatter.5.cloned.1.call-start = ((), (), s32[]{:S(2)}) async-start(), calls=%async_computation.3 | async-start | bytes 2654208 | tf_op jit(solution)/shard_map/reduce_scatter | solution.py:1152
  112.8 13.4 %collective-permute-start.14 = (bf16[128,1024]{1,0:T(8,128)(2,1)S(1)}, bf16[128,1024]{1,0:T(8,128)(2,1)S(1)}, u32[]{:S(2)}, u32[]{:S(2)}) collective-permute-start(bf16[128,1024]{1,0:T(8,128)(2,1)S(1)} %get-tuple-element.148), channel_id=1, source_target_pairs={{0,24},{8,16},{16,8},{24,0},{1,25},{9,17},{17,9},{25,1},{2,26},{10... | collective-permute-start | bytes 786440 | tf_op jit(solution)/shard_map/ppermute | solution.py:860
  114.3 13.3 %collective-permute-start.13 = (bf16[128,1024]{1,0:T(8,128)(2,1)S(1)}, bf16[128,1024]{1,0:T(8,128)(2,1)S(1)}, u32[]{:S(2)}, u32[]{:S(2)}) collective-permute-start(bf16[128,1024]{1,0:T(8,128)(2,1)S(1)} %get-tuple-element.149), channel_id=1, source_target_pairs={{0,16},{8,24},{16,0},{24,8},{1,17},{9,25},{17,1},{25,9},{2,18},{10... | collective-permute-start | bytes 786440 | tf_op jit(solution)/shard_map/ppermute | solution.py:860
  141.7 17.7 %collective-permute-start.18 = (bf16[128,1024]{1,0:T(8,128)(2,1)S(1)}, bf16[128,1024]{1,0:T(8,128)(2,1)S(1)}, u32[]{:S(2)}, u32[]{:S(2)}) collective-permute-start(bf16[128,1024]{1,0:T(8,128)(2,1)S(1)} %get-tuple-element.144), channel_id=1, source_target_pairs={{0,8},{8,0},{16,24},{24,16},{1,9},{9,1},{17,25},{25,17},{2,10},{10... | collective-permute-start | bytes 786440 | tf_op jit(solution)/shard_map/ppermute | solution.py:860
  142.3 17.1 %collective-permute-start.20 = (bf16[128,1024]{1,0:T(8,128)(2,1)S(1)}, bf16[128,1024]{1,0:T(8,128)(2,1)S(1)}, u32[]{:S(2)}, u32[]{:S(2)}) collective-permute-start(bf16[128,1024]{1,0:T(8,128)(2,1)S(1)} %get-tuple-element.145), channel_id=1, source_target_pairs={{0,24},{8,16},{16,8},{24,0},{1,25},{9,17},{17,9},{25,1},{2,26},{10... | collective-permute-start | bytes 786440 | tf_op jit(solution)/shard_map/ppermute | solution.py:860
  143.8 15.6 %collective-permute-start.19 = (bf16[128,1024]{1,0:T(8,128)(2,1)S(1)}, bf16[128,1024]{1,0:T(8,128)(2,1)S(1)}, u32[]{:S(2)}, u32[]{:S(2)}) collective-permute-start(bf16[128,1024]{1,0:T(8,128)(2,1)S(1)} %get-tuple-element.146), channel_id=1, source_target_pairs={{0,16},{8,24},{16,0},{24,8},{1,17},{9,25},{17,1},{25,9},{2,18},{10... | collective-permute-start | bytes 786440 | tf_op jit(solution)/shard_map/ppermute | solution.py:860
  161.9 14.9 %collective-permute-start.26 = (bf16[1056,128]{1,0:T(8,128)(2,1)S(1)}, bf16[1056,128]{1,0:T(8,128)(2,1)S(1)}, u32[]{:S(2)}, u32[]{:S(2)}) collective-permute-start(bf16[1056,128]{1,0:T(8,128)(2,1)S(1)} %get-tuple-element.156.refs_4_), channel_id=1, source_target_pairs={{0,16},{8,24},{16,0},{24,8},{1,17},{9,25},{17,1},{25,9},{2,18},{10... | collective-permute-start | bytes 811016 | tf_op jit(solution)/shard_map/ppermute | solution.py:832
  164.3 36.3 %collective-permute-start.23 = (bf16[128,1024]{1,0:T(8,128)(2,1)}, bf16[128,1024]{1,0:T(8,128)(2,1)S(1)}, u32[]{:S(2)}, u32[]{:S(2)}) collective-permute-start(bf16[128,1024]{1,0:T(8,128)(2,1)} %get-tuple-element.140), channel_id=1, source_target_pairs={{0,24},{8,16},{16,8},{24,0},{1,25},{9,17},{17,9},{25,1},{2,26},{10... | collective-permute-start | bytes 786440 | tf_op jit(solution)/shard_map/ppermute | solution.py:860
  165.8 35.4 %collective-permute-start.22 = (bf16[128,1024]{1,0:T(8,128)(2,1)}, bf16[128,1024]{1,0:T(8,128)(2,1)S(1)}, u32[]{:S(2)}, u32[]{:S(2)}) collective-permute-start(bf16[128,1024]{1,0:T(8,128)(2,1)} %get-tuple-element.141), channel_id=1, source_target_pairs={{0,16},{8,24},{16,0},{24,8},{1,17},{9,25},{17,1},{25,9},{2,18},{10... | collective-permute-start | bytes 786440 | tf_op jit(solution)/shard_map/ppermute | solution.py:860
  167.3 33.9 %collective-permute-start.21 = (bf16[128,1024]{1,0:T(8,128)(2,1)}, bf16[128,1024]{1,0:T(8,128)(2,1)S(1)}, u32[]{:S(2)}, u32[]{:S(2)}) collective-permute-start(bf16[128,1024]{1,0:T(8,128)(2,1)} %get-tuple-element.142), channel_id=1, source_target_pairs={{0,8},{8,0},{16,24},{24,16},{1,9},{9,1},{17,25},{25,17},{2,10},{10... | collective-permute-start | bytes 786440 | tf_op jit(solution)/shard_map/ppermute | solution.py:860
  167.8 17.4 %collective-permute-start.24 = (bf16[1056,128]{1,0:T(8,128)(2,1)S(1)}, bf16[1056,128]{1,0:T(8,128)(2,1)S(1)}, u32[]{:S(2)}, u32[]{:S(2)}) collective-permute-start(bf16[1056,128]{1,0:T(8,128)(2,1)S(1)} %get-tuple-element.157.refs_0_), channel_id=1, source_target_pairs={{0,8},{8,0},{16,24},{24,16},{1,9},{9,1},{17,25},{25,17},{2,10},{10... | collective-permute-start | bytes 811016 | tf_op jit(solution)/shard_map/ppermute | solution.py:832
  176.8 16.4 %collective-permute-start.27 = (bf16[2112,128]{1,0:T(8,128)(2,1)S(1)}, bf16[2112,128]{1,0:T(8,128)(2,1)S(1)}, u32[]{:S(2)}, u32[]{:S(2)}) collective-permute-start(bf16[2112,128]{1,0:T(8,128)(2,1)S(1)} %pad_maximum_fusion.4), channel_id=1, source_target_pairs={{0,8},{8,0},{16,24},{24,16},{1,9},{9,1},{17,25},{25,17},{2,10},{10... | collective-permute-start | bytes 1622024 | tf_op jit(solution)/shard_map/ppermute | solution.py:832
  (44 other events, 540.1 us)
Sparse Core Ops, SparseCore 0:
  9.9 31.0 all-gather.4
  43.1 48.4 all-gather.6
  110.1 50.6 reduce-scatter.2
  163.1 34.5 reduce-scatter.4
